TPU v7x, 32 devices: a whole 2x2x4 slice. The times are simulated.
32 devices in a mesh: group: 2 (over y), tile: 16 (over z, x, core).
Axes of the slice: x: 2, y: 2, z: 4, core: 2. Of those that a mesh axis runs over, the one named last changes fastest.
Arguments:
- density: float32 [2, 2048, 1024], P(None, ('group', 'tile')), parts along dimension 1, may hold values from -6 to 6
- observed: float32 [6, 2048, 1024], P(None, ('group', 'tile')), parts along dimension 1, may hold values from -3 to 3
- active: int32 [2048, 1024], P(('group', 'tile')), parts along dimension 0, may hold values 0 or 1
- layer_depth: float32 [2], replicated, may hold values from 0.5 to 4
Outputs:
- predicted: float32 [6, 2048, 1024], P(None, ('group', 'tile')), parts along dimension 1
- gradient: float32 [2, 2048, 1024], P(None, ('group', 'tile')), parts along dimension 1
There are 2 independent parts, one for each index of `group`. A program takes and returns all parts, laid end to end along the dimension named above; an argument that names none is the same for every part. Nothing has to cross between parts.
All inputs are finite; a program needn't handle non-finite values. No bound on the sum of `active` on one device may be relied on, other than what follows from the above.
Results may differ from a plain program's by a relative error of at most 0.0001.
Values sent between devices are 32-bit elements; how exact they have to be, the bound alone decides.
No kernel may reach another device: no remote copies, remote signals or barrier semaphores. Data moves between devices by JAX's collectives and lax.ppermute only.
A program may use at most 128 MiB of HBM per device.

v0:
```python
import functools
import math

import jax
import jax.numpy as jnp
import numpy as np
from jax import lax
from jax.experimental import pallas as pl
from jax.experimental.pallas import tpu as pltpu
from jax.sharding import PartitionSpec as P

LANES = 128
HIGH = lax.Precision.HIGH


def half_waves(side):
    groups = side // LANES
    step = 2 * groups
    even = np.arange(LANES // 2) * step
    rows = [np.concatenate([even, even + groups])]
    for g in range(1, groups):
        rows.append(np.arange(LANES) * step + g)
    index = np.stack(rows)
    return np.where(index < side, index, index - 2 * side)


def angle_parts(left, right, period):
    phase = (left[:, None].astype(np.int64) * right[None, :].astype(np.int64)) % period
    angle = phase * (2.0 * math.pi / period)
    return np.cos(angle), np.sin(angle)


def ring_order(chips):
    width = max(1, int(round(chips ** (1.0 / 3.0))))
    if chips % width:
        width = 1
    height = chips // width
    order = [z * width for z in range(height)]
    for z in reversed(range(height)):
        row = list(range(1, width))
        if (height - 1 - z) % 2:
            row.reverse()
        order += [z * width + x for x in row]
    return np.array(order)


def dot(a, b):
    return jnp.dot(a, b, precision=HIGH)


def halves(a):
    high = a.astype(jnp.bfloat16)
    return high, (a - high.astype(jnp.float32)).astype(jnp.bfloat16)


def np_halves(a):
    a = a.astype(np.float32)
    high = a.astype(jnp.bfloat16)
    return high, (a - high.astype(np.float32)).astype(jnp.bfloat16)


def table_of(a, axis):
    return jnp.asarray(np.concatenate(np_halves(a), axis=axis))


def product(left, right, dims=((1,), (0,))):
    def one(a, b):
        return lax.dot_general(a, b, (dims, ((), ())), preferred_element_type=jnp.float32)

    return one(left[0], right[0]) + (one(left[0], right[1]) + one(left[1], right[0]))


def stacked(table, high, low, rows):
    both = jnp.dot(table, high, preferred_element_type=jnp.float32)
    rest = jnp.dot(table[:rows], low, preferred_element_type=jnp.float32)
    return both[:rows] + (both[rows:] + rest)


def mixed(values, high, low):
    rows = values.shape[0] // 2
    both = jnp.dot(values, high, preferred_element_type=jnp.float32)
    rest = jnp.dot(values[:rows], low, preferred_element_type=jnp.float32)
    return both[:rows] + (both[rows:] + rest)


def accumulate(terms):
    total = None
    for factor, value in terms:
        if abs(factor) < 1e-9:
            continue
        if abs(abs(factor) - 1.0) < 1e-9:
            if total is None:
                total = value if factor > 0 else -value
            else:
                total = total + value if factor > 0 else total - value
        else:
            scaled = value * np.float32(factor)
            total = scaled if total is None else total + scaled
    return total


def spread(f):
    count = len(f)
    half = count // 2
    plus = [f[a] + f[a + half] for a in range(half)]
    minus = [f[a] - f[a + half] for a in range(half)]
    even = [None] + [f[a] + f[count - a] for a in range(1, half)]
    odd = [None] + [f[a] - f[count - a] for a in range(1, half)]
    out = []
    for g in range(count):
        angle = [math.pi * a * g / count for a in range(count)]
        if g == 0:
            top = accumulate([(1.0, plus[a]) for a in range(0, half, 2)])
            low = accumulate([(1.0, plus[a]) for a in range(1, half, 2)])
            out.append((top + low, top - low))
        elif g % 2:
            p = accumulate([(1.0, f[0])] + [(math.cos(angle[a]), odd[a]) for a in range(1, half)])
            q = accumulate(
                [(math.sin(angle[half]), f[half])]
                + [(math.sin(angle[a]), even[a]) for a in range(1, half)]
            )
            out.append((p, q))
        else:
            base = minus if (g // 2) % 2 else plus
            p = accumulate([(math.cos(angle[a]), base[a]) for a in range(half)])
            q = accumulate([(math.sin(angle[a]), base[a]) for a in range(half)])
            out.append((p, q))
    return out


def gather(pairs):
    count = len(pairs)
    half = count // 2
    out = [None] * count
    there = [g for g in range(count) if pairs[g] is not None]

    def wave(a, g):
        angle = math.pi * a * g / count
        return [(math.cos(angle), pairs[g][0]), (math.sin(angle), pairs[g][1])]

    for a in range(half):
        same = []
        if 0 in there:
            same = [(1.0, pairs[0][0]), ((-1.0) ** a, pairs[0][1])]
        for g in there:
            if g and g % 4 == 0:
                same += wave(a, g)
        flip = []
        for g in there:
            if g % 4 == 2:
                flip += wave(a, g)
        same, flip = accumulate(same), accumulate(flip)
        out[a] = same + flip
        out[a + half] = same - flip
    odds = [g for g in there if g % 2]
    for a in range(1, half):
        cosine = accumulate([(math.cos(math.pi * a * g / count), pairs[g][0]) for g in odds])
        sine = accumulate([(math.sin(math.pi * a * g / count), pairs[g][1]) for g in odds])
        out[a] = out[a] + (cosine + sine)
        out[count - a] = out[count - a] + (sine - cosine)
    out[0] = out[0] + accumulate([(1.0, pairs[g][0]) for g in odds])
    out[half] = out[half] + accumulate([(math.sin(math.pi * g / 2), pairs[g][1]) for g in odds])
    return out


def double(a):
    a = jnp.concatenate([a, a], axis=0)
    return jnp.concatenate([a, a], axis=1)


def turn(a, ky):
    return jnp.concatenate([-ky * a[:, LANES:], ky * a[:, :LANES]], axis=1)


def twofold(ky):
    return jnp.concatenate([ky, ky], axis=1)


STRIP = 16


def decay(modulus, gain, depth, l, g):
    here = slice(g * LANES, (g + 1) * LANES)
    return jnp.exp(-modulus[0, here, :] * depth[l]) * gain[0, here, :]


def on_core(place, run):
    for c in (0, 1):

        @pl.when(place[0] == c)
        def _(c=c):
            run(c)


def split_lanes(core, own, read, write):
    sums = spread([read(slice(a * LANES, (a + 1) * LANES)) for a in range(2 * own)])
    for g in range(own):
        for k in (0, 1):
            write(g, slice(k * LANES, (k + 1) * LANES), *halves(sums[core * own + g][k]))


def join_lanes(core, own, read):
    pairs = [None] * (2 * own)
    for g in range(own):
        pairs[core * own + g] = (read(g, slice(0, LANES)), read(g, slice(LANES, 2 * LANES)))
    return gather(pairs)


def rows_kernel(later, place, fore, rear, far_fore, far_rear, mix_h, mix_l, *rest):
    spec_a, spec_b, val = rest[2:] if later else rest
    rows = fore.shape[0]
    own = mix_h.shape[1]
    span = 2 * rows
    wide = 2 * LANES

    def run(core):
        for l, pair in enumerate(((fore, far_fore), (rear, far_rear))):
            for k, source in enumerate(pair):
                start = l * span + (core if k == 0 else 1 - core) * rows
                for i in range(rows // STRIP):
                    at = slice(i * STRIP, (i + 1) * STRIP)
                    here = slice(start + i * STRIP, start + (i + 1) * STRIP)
                    below = slice(2 * span + here.start, 2 * span + here.stop)

                    def write(g, lane, high, low):
                        val[g, here, lane] = high
                        val[g, below, lane] = low

                    split_lanes(core, own, lambda lane: source[at, lane], write)

    on_core(place, run)
    for g in range(own):
        out = mixed(val[g], mix_h[0, g], mix_l[0, g])
        spec_a[:, g * wide : (g + 1) * wide] = out[:span]
        spec_b[:, g * wide : (g + 1) * wide] = out[span:]


def strips_kernel(place, high_a, low_a, high_b, low_b, mix_h, mix_l, keep, give, val):
    rows = keep.shape[1]
    own = mix_h.shape[1]
    span = 2 * rows
    for g in range(own):
        lanes = slice(g * 2 * LANES, (g + 1) * 2 * LANES)
        values = jnp.concatenate([a[:, lanes] for a in (high_a, high_b, low_a, low_b)])
        val[g] = mixed(values, mix_h[0, g], mix_l[0, g])

    def run(core):
        for l in (0, 1):
            for target, part in ((keep, core), (give, 1 - core)):
                for i in range(rows // 8):
                    start = l * span + part * rows + i * 8
                    blocks = join_lanes(
                        core, own, lambda g, lane: val[g, start : start + 8, lane]
                    )
                    for a, value in enumerate(blocks):
                        target[l, i * 8 : (i + 1) * 8, a * LANES : (a + 1) * LANES] = value

    on_core(place, run)


def forward_kernel(
    place, depth, spec_a, spec_b, gain, modulus, wave, mix, near, back_h, back_l,
    out, val_h, val_l, sum_h, sum_l, steep_h, steep_l, lines,
):
    specs = (spec_a, spec_b)
    layers = len(specs)
    groups = mix.shape[0]
    span = near.shape[1] // 6
    wide = 2 * LANES
    own = groups // 2

    for l in range(layers):

        def strip(i, carry, l=l):
            at = pl.multiple_of(i * STRIP, STRIP)
            f = [specs[l][pl.ds(a * LANES + at, STRIP), :] for a in range(groups)]
            for g, (p, q) in enumerate(spread(f)):
                high, low = halves(p)
                val_h[l, g, pl.ds(at, STRIP), :] = high
                val_l[l, g, pl.ds(at, STRIP), :] = low
                high, low = halves(q)
                val_h[l, g, pl.ds(LANES + at, STRIP), :] = high
                val_l[l, g, pl.ds(LANES + at, STRIP), :] = low
            return carry

        lax.fori_loop(0, LANES // STRIP, strip, 0)

    for g in range(groups):
        total = None
        for l in range(layers):
            cols = stacked(mix[g], val_h[l, g], val_l[l, g], wide)
            cols = cols * double(decay(modulus, gain, depth, l, g))
            total = cols if total is None else total + cols
        here = pl.ds(g * wide, wide)
        sum_h[here, :], sum_l[here, :] = halves(total)
        steep = total * double(modulus[0, g * LANES : (g + 1) * LANES, :])
        steep_h[here, :], steep_l[here, :] = halves(steep)

    plain = stacked(near[0], sum_h[...], sum_l[...], 3 * span)
    slopes = jnp.concatenate([near[0, : 2 * span], near[0, 3 * span : 5 * span]])
    sloped = stacked(slopes, steep_h[...], steep_l[...], 2 * span)
    ky = wave[0, 0, 0:1, :]
    both = twofold(ky)
    values = jnp.concatenate(
        [
            plain[2 * span :],
            turn(plain[span : 2 * span], ky),
            sloped[span:],
            -(both * both) * plain[:span],
            turn(sloped[:span], ky),
        ]
    )
    step = pl.program_id(0)
    lines[step] = mixed(jnp.concatenate(halves(values)), back_h[0, 0], back_l[0, 0])

    @pl.when(step == own - 1)
    def _():
        def run(core):
            def strip(i, carry):
                here = pl.ds(pl.multiple_of(i * 8, 8), 8)
                blocks = join_lanes(core, own, lambda g, lane: lines[g, here, lane])
                for a, value in enumerate(blocks):
                    out[here, a * LANES : (a + 1) * LANES] = value
                return carry

            lax.fori_loop(0, 5 * span // 8, strip, 0)

        on_core(place, run)


def transpose_kernel(place, near, far):
    for g in range(far.shape[0] // (2 * LANES)):
        lane = slice(g * 2 * LANES, (g + 1) * 2 * LANES)
        far[lane, :] = near[0, :, lane].T


def adjoint_kernel(
    place, depth, field, other, seen, far_seen, gain, modulus, wave, mix, far, fold_h, fold_l,
    predicted, high_a, low_a, high_b, low_b, left, val_y, val,
):
    grids = ((high_a, low_a), (high_b, low_b))
    layers = len(grids)
    groups = mix.shape[0]
    rows = predicted.shape[1]
    span = 2 * rows
    wide = 2 * LANES
    own = groups // 2

    @pl.when(pl.program_id(0) == 0)
    def _():
        def total(c, at):
            here = pl.ds(c * span + at, 8)
            return field[here, :] + other[here, :]

        def strip(start, look, write):
            def one(i, carry):
                to = pl.multiple_of(i * 8, 8)
                at = pl.multiple_of(start + i * 8, 8)
                xx, xy, xz, yy, yz = [total(c, at) for c in range(5)]
                zz = -(xx + yy)
                rest_zz = zz - look[5, pl.ds(to, 8), :]
                rest = [
                    rest_zz - (yy - look[3, pl.ds(to, 8), :]),
                    xy - look[1, pl.ds(to, 8), :],
                    rest_zz - (xx - look[0, pl.ds(to, 8), :]),
                    yz - look[4, pl.ds(to, 8), :],
                    xz - look[2, pl.ds(to, 8), :],
                ]
                for c, value in enumerate(rest):
                    left[pl.ds(c * span + at, 8), :] = value
                if write:
                    for c, value in enumerate([xx, xy, xz, yy, yz, zz]):
                        predicted[c, pl.ds(to, 8), :] = value
                return carry

            lax.fori_loop(0, rows // 8, one, 0)

        strip(place[0] * rows, seen, True)
        strip((1 - place[0]) * rows, far_seen, False)

        def run(core):
            def cut(i, carry):
                at = pl.multiple_of(i * STRIP, STRIP)
                here = pl.ds(at, STRIP)
                below = pl.ds(5 * span + at, STRIP)

                def write(g, lane, high, low):
                    val_y[g, here, lane] = high
                    val_y[g, below, lane] = low

                split_lanes(core, own, lambda lane: left[here, lane], write)
                return carry

            lax.fori_loop(0, 5 * span // STRIP, cut, 0)

        on_core(place, run)

    back = mixed(val_y[pl.program_id(0)], fold_h[0, 0], fold_l[0, 0])
    ky = wave[0, 0, 0:1, :]
    both = twofold(ky)
    part = [back[c * span : (c + 1) * span] for c in range(5)]
    low = halves(jnp.concatenate([both * both * part[0], -turn(part[1], ky), -part[2]]))
    high = halves(jnp.concatenate([-turn(part[3], ky), part[4]]))

    for g in range(groups):
        here = slice(g * wide, (g + 1) * wide)
        table = jnp.concatenate([far[here, : 3 * span], far[here, 3 * span :]])
        sums = stacked(table, *low, wide)
        slopes = stacked(table[:, : 2 * span], *high, wide)
        sums = sums + double(modulus[0, g * LANES : (g + 1) * LANES, :]) * slopes
        for l in range(layers):
            scaled = sums * double(decay(modulus, gain, depth, l, g))
            val[l, g] = stacked(mix[g], *halves(scaled), wide)

    for l in range(layers):

        def strip(i, carry, l=l):
            at = pl.multiple_of(i * STRIP, STRIP)
            pairs = [
                (val[l, g, pl.ds(at, STRIP), :], val[l, g, pl.ds(LANES + at, STRIP), :])
                for g in range(groups)
            ]
            for a, value in enumerate(gather(pairs)):
                here = pl.ds(a * LANES + at, STRIP)
                grids[l][0][here, :], grids[l][1][here, :] = halves(value)
            return carry

        lax.fori_loop(0, LANES // STRIP, strip, 0)


def body(density, observed, active, layer_depth):
    layers, rows, side = density.shape
    period = 2 * side
    tiles = lax.axis_size("tile")
    chips = tiles // 2
    place = lax.axis_index("tile")
    chip, core = place // 2, place % 2
    span = 2 * rows
    groups = side // LANES
    own = groups // 2
    wide = 2 * LANES

    order = ring_order(chips)
    spot = np.argsort(order)
    index = np.zeros((tiles, 2 + 2 * (chips + 1)), np.int32)
    for i in range(tiles):
        p = spot[i // 2]
        index[i, :2] = i % 2, i // 2
        for o in range(chips + 1):
            index[i, 2 + 2 * o] = order[(p - o) % chips]
            index[i, 3 + 2 * o] = order[(p + o) % chips]
    index = lax.dynamic_index_in_dim(jnp.asarray(index), place, 0, False)

    def ring(shift):
        return [
            (2 * int(order[p]) + c, 2 * int(order[(p + shift) % chips]) + c)
            for p in range(chips)
            for c in (0, 1)
        ]

    ahead, back = ring(1), ring(-1)
    pair = [(i, i ^ 1) for i in range(tiles)]

    unit = 2.0 * math.pi / period
    waves = half_waves(side)
    cells = np.arange(side)
    cos_t, sin_t = angle_parts(cells, waves.reshape(-1), period)
    cos_t = cos_t.reshape(side, groups, 1, LANES)
    sin_t = sin_t.reshape(side, groups, 1, LANES)
    full_y = np.concatenate([cos_t, -sin_t], axis=2).reshape(side, 2, side).transpose(1, 2, 0)
    value = np.concatenate([cos_t, sin_t], axis=2).reshape(side, period)
    slope = np.concatenate([-sin_t, cos_t], axis=2).reshape(side, period)
    flat_wave = np.repeat((waves * unit)[:, None], 2, axis=1).reshape(1, period)
    near = np.stack([value, flat_wave * slope, -(flat_wave**2) * value])
    near = near.reshape(3, chips, span, period).transpose(1, 0, 2, 3).reshape(chips, 3 * span, period)
    near = table_of(near, 1)

    low_cells = np.arange(LANES)
    mix = np.zeros((groups, 2 * LANES, 2 * LANES))
    for g in range(groups):
        c, s = angle_parts(waves[g], low_cells, period)
        if g:
            mix[g] = np.block([[c, -s], [s, c]])
        else:
            top = (np.arange(LANES) < LANES // 2)[:, None]
            mix[g] = np.block([[c * top, c * ~top], [s * top, s * ~top]])
    mix_f = table_of(mix, 1)
    mix_b = table_of(mix.transpose(0, 2, 1), 1)

    mix_y = mix.transpose(0, 2, 1) * np.repeat([1.0, -1.0], LANES)
    mix_y = mix_y.reshape(2, own, wide, wide)
    mix_yf = [jnp.asarray(a) for a in np_halves(mix_y)]
    mix_yb = [jnp.asarray(a) for a in np_halves(mix_y.transpose(0, 1, 3, 2))]

    flat_x = (waves * unit).reshape(1, -1, 1)
    flat_y = (waves * unit).reshape(2, 1, -1)
    modulus = np.sqrt(flat_x**2 + flat_y**2).astype(np.float32)
    slab = np.where(modulus > 0, -np.expm1(-modulus) / np.maximum(modulus, 0.001), 1.0)
    twice = np.where(waves == 0, 1.0, 2.0)
    gain = slab * (twice.reshape(1, -1, 1) * twice.reshape(2, 1, -1) / (period * period))
    modulus, gain = jnp.asarray(modulus), jnp.asarray(gain, jnp.float32)
    wave = np.broadcast_to((waves * unit).reshape(2, own, 1, LANES), (2, own, 8, LANES))
    wave = jnp.asarray(wave, jnp.float32)

    active_cells = active.astype(jnp.float32)
    masked = density * active_cells[None]
    far_seen = lax.ppermute(observed, "tile", pair)

    def const(shape):
        return pl.BlockSpec(shape, lambda g, *_: (0,) * len(shape))

    def lanes(shape):
        return pl.BlockSpec(shape, lambda g, *_: (0,) * (len(shape) - 1) + (g,))

    def by_core(shape):
        return pl.BlockSpec(shape, lambda g, p: (p[0],) + (0,) * (len(shape) - 1))

    def call(kernel, grid, in_specs, out_specs, out_shape, scratch, aliases={}):
        return pl.pallas_call(
            kernel,
            grid_spec=pltpu.PrefetchScalarGridSpec(
                num_scalar_prefetch=1,
                grid=(grid,),
                in_specs=in_specs,
                out_specs=out_specs,
                scratch_shapes=scratch,
            ),
            out_shape=out_shape,
            input_output_aliases=aliases,
            compiler_params=pltpu.CompilerParams(
                dimension_semantics=("arbitrary",), vmem_limit_bytes=56 * 1024 * 1024
            ),
        )

    def chip_block(shape, layer, offset):
        return pl.BlockSpec(shape, lambda g, p: (p[2 + 2 * offset + layer], 0))

    far = call(
        transpose_kernel,
        1,
        [pl.BlockSpec((1, 6 * span, period), lambda g, p: (p[1], 0, 0))],
        const((period, 6 * span)),
        jax.ShapeDtypeStruct((period, 6 * span), jnp.bfloat16),
        [],
    )(index, near)

    if chips <= 8:
        done = []
        fore, rear = masked[0], masked[1]
        for step in range(chips):
            if step:
                if step >= 2:
                    fore, rear, done[step - 2] = lax.optimization_barrier(
                        (fore, rear, done[step - 2])
                    )
                if step == 3:
                    fore, rear, far_seen, far = lax.optimization_barrier(
                        (fore, rear, far_seen, far)
                    )
                fore = lax.ppermute(fore, "tile", ahead)
                rear = lax.ppermute(rear, "tile", back)
            far_fore = lax.ppermute(fore, "tile", pair)
            far_rear = lax.ppermute(rear, "tile", pair)
            args = [index, fore, rear, far_fore, far_rear, *mix_yf]
            in_specs = [const((rows, side))] * 4 + [by_core((1,) + mix_y.shape[1:])] * 2
            if step:
                args += done[-1]
                in_specs += [pl.BlockSpec(memory_space=pl.ANY)] * 2
            spec = call(
                functools.partial(rows_kernel, step > 0),
                1,
                in_specs,
                [chip_block((span, side), l, step) for l in (0, 1)],
                [jax.ShapeDtypeStruct((side, side), jnp.float32)] * 2,
                [pltpu.VMEM((own, 4 * span, wide), jnp.bfloat16)],
                {7: 0, 8: 1} if step else {},
            )(*args)
            done.append(spec)
    else:
        whole = lax.all_gather(masked, "tile", axis=1, tiled=True)
        table_y = lax.dynamic_index_in_dim(jnp.asarray(full_y, jnp.float32), core, 0, False)
        spec = lax.dot_general(whole, table_y, (((2,), (1,)), ((), ())), precision=HIGH)
        spec = [spec[0], spec[1]]

    shared = [
        pl.BlockSpec((1, side, LANES), lambda g, p: (p[0], 0, g)),
        pl.BlockSpec((1, side, LANES), lambda g, p: (p[0], 0, g)),
        pl.BlockSpec((1, 1, 8, LANES), lambda g, p: (p[0], g, 0, 0)),
        const(mix_f.shape),
    ]
    group_spec = pl.BlockSpec((1, 1, wide, wide), lambda g, p: (p[0], g, 0, 0))
    smem = pl.BlockSpec(memory_space=pltpu.SMEM)
    partial = call(
        forward_kernel,
        own,
        [smem]
        + [lanes((side, wide))] * 2
        + shared
        + [pl.BlockSpec((1, 6 * span, period), lambda g, p: (p[1], 0, 0))]
        + [group_spec] * 2,
        const((5 * span, side)),
        jax.ShapeDtypeStruct((5 * span, side), jnp.float32),
        [pltpu.VMEM((layers, groups, wide, wide), jnp.bfloat16)] * 2
        + [pltpu.VMEM((period, wide), jnp.bfloat16)] * 4
        + [pltpu.VMEM((own, 5 * span, wide), jnp.float32)],
    )(index, layer_depth, *spec, gain, modulus, wave, mix_f, near, *mix_yb)

    other = lax.ppermute(partial, "tile", pair)
    predicted, *grids = call(
        adjoint_kernel,
        own,
        [smem]
        + [const((5 * span, side))] * 2
        + [const((6, rows, side))] * 2
        + shared
        + [const((period, 6 * span))]
        + [group_spec] * 2,
        [const((6, rows, side))] + [lanes((side, wide))] * 4,
        [jax.ShapeDtypeStruct((6, rows, side), jnp.float32)]
        + [jax.ShapeDtypeStruct((side, side), jnp.bfloat16)] * 4,
        [
            pltpu.VMEM((5 * span, side), jnp.float32),
            pltpu.VMEM((own, 10 * span, wide), jnp.bfloat16),
            pltpu.VMEM((layers, groups, wide, wide), jnp.float32),
        ],
    )(
        index, layer_depth, partial, other, observed, far_seen, gain, modulus, wave,
        mix_b, far, *mix_yf,
    )

    if chips <= 8:

        def share(offset, grids):
            keep, give = call(
                strips_kernel,
                1,
                [chip_block((span, side), l, offset) for l in (0, 0, 1, 1)]
                + [by_core((1,) + mix_y.shape[1:])] * 2,
                [const((layers, rows, side))] * 2,
                [jax.ShapeDtypeStruct((layers, rows, side), jnp.float32)] * 2,
                [pltpu.VMEM((own, 2 * span, wide), jnp.float32)],
            )(index, *grids, *mix_yb)
            return keep, lax.ppermute(give, "tile", pair)

        keep, give = share(1, grids)
        now = [keep[l] + give[l] for l in (0, 1)]
        ready = share(2, grids)
        for step in range(1, chips):
            keep, give = ready
            if step < chips - 1:
                now, grids = lax.optimization_barrier((now, grids))
                ready = share(step + 2, grids)
            fore = lax.ppermute(now[0], "tile", ahead)
            rear = lax.ppermute(now[1], "tile", back)
            now = [fore + (keep[0] + give[0]), rear + (keep[1] + give[1])]
        gradient = jnp.stack(now)
    else:
        table_y = lax.dynamic_index_in_dim(jnp.asarray(full_y, jnp.float32), core, 0, False)
        strip = jnp.stack([h.astype(jnp.float32) + l for h, l in (grids[:2], grids[2:])])
        strip = lax.dot_general(strip, table_y, (((2,), (0,)), ((), ())), precision=HIGH)
        gradient = lax.psum_scatter(strip, "tile", scatter_dimension=1, tiled=True)
    return (predicted, gradient * active_cells[None])


def solution(mesh):
    return jax.shard_map(
        body,
        mesh=mesh,
        in_specs=(
            P(None, ("group", "tile"), None),
            P(None, ("group", "tile"), None),
            P(("group", "tile"), None),
            P(),
        ),
        out_specs=(P(None, ("group", "tile"), None), P(None, ("group", "tile"), None)),
        check_vma=False,
    )
```

profile of v0, /device:TPU:0, one launch (start us, length us, event | category | flops | bytes accessed | tf_op | source)
XLA Modules:
  0.0 232.7 jit_solution(14367136418228413398)
XLA Ops:
  3.9 2.6 %collective-permute-start = (f32[64,1024]{1,0:T(8,128)S(1)}, f32[64,1024]{1,0:T(8,128)S(1)}, u32[]{:S(2)}, u32[]{:S(2)}) collective-permute-start(f32[64,1024]{1,0:T(8,128)S(1)} %get-tuple-element.197.fore), channel_id=1, source_target_pairs={{0,4},{1,5},{4,8},{5,9},{8,12},{9,13},{12,14},{13,15},{14,10},{15,... | collective-permute-start | bytes 786440 | tf_op jit(solution)/shard_map/ppermute | solution.py:560
  6.5 1.3 dynamic-slice_bitcast_fusion.place
  9.2 4.1 %shard_map.158 = (f32[1024,1024]{1,0:T(8,128)}, f32[1024,1024]{1,0:T(8,128)}) custom-call(s32[20]{0:T(128)} %dynamic-slice_bitcast_fusion.place, f32[64,1024]{1,0:T(8,128)} %copy-done.3, f32[64,1024]{1,0:T(8,128)} %copy-done.2, f32[64,1024]{1,0:T(8,128)} %copy-done.39, f32[64,1024]{1,0:T(8,128)} %copy-done.40, ...), custom_call_target="tpu_custom_call" | custom-call | tf_op jit(solution)/shard_map/pallas_call | solution.py:569
  13.3 1.6 collective-permute-done.1.rear
  15.4 1.6 collective-permute-start.4
  17.4 5.1 %shard_map.160.far = bf16[2048,768]{1,0:T(8,128)(2,1)} custom-call(s32[20]{0:T(128)} %dynamic-slice_bitcast_fusion.place, bf16[8,768,2048]{2,1,0:T(8,128)(2,1)} %constant.33.clone.near), custom_call_target="tpu_custom_call" | custom-call | tf_op jit(solution)/shard_map/pallas_call | solution.py:538
  23.9 4.1 %shard_map.159 = (f32[1024,1024]{1,0:T(8,128)}, f32[1024,1024]{1,0:T(8,128)}) custom-call(s32[20]{0:T(128)} %dynamic-slice_bitcast_fusion.place, f32[64,1024]{1,0:T(8,128)} %copy-done.11, f32[64,1024]{1,0:T(8,128)} %copy-done.12, f32[64,1024]{1,0:T(8,128)} %copy-done.30, f32[64,1024]{1,0:T(8,128)} %copy-done.35, ...), custom_call_target="tpu_custom_call", output_to_operand_aliasing={{0}: (7, {}), {1}: (8, {})} | custom-call | tf_op jit(solution)/shard_map/pallas_call | solution.py:569
  29.1 1.6 collective-permute-start.9
  32.1 4.1 %shard_map.161 = (f32[1024,1024]{1,0:T(8,128)}, f32[1024,1024]{1,0:T(8,128)}) custom-call(s32[20]{0:T(128)} %dynamic-slice_bitcast_fusion.place, f32[64,1024]{1,0:T(8,128)} %copy-done.14, f32[64,1024]{1,0:T(8,128)} %copy-done.17, f32[64,1024]{1,0:T(8,128)} %copy-done.29, f32[64,1024]{1,0:T(8,128)} %copy-done.31, ...), custom_call_target="tpu_custom_call", output_to_operand_aliasing={{0}: (7, {}), {1}: (8, {})} | custom-call | tf_op jit(solution)/shard_map/pallas_call | solution.py:569
  37.6 1.6 collective-permute-start.13
  41.0 4.1 %shard_map.162 = (f32[1024,1024]{1,0:T(8,128)}, f32[1024,1024]{1,0:T(8,128)}) custom-call(s32[20]{0:T(128)} %dynamic-slice_bitcast_fusion.place, f32[64,1024]{1,0:T(8,128)} %copy-done.22, f32[64,1024]{1,0:T(8,128)} %copy-done.16, f32[64,1024]{1,0:T(8,128)} %copy-done.32, f32[64,1024]{1,0:T(8,128)} %copy-done.36, ...), custom_call_target="tpu_custom_call", output_to_operand_aliasing={{0}: (7, {}), {1}: (8, {})} | custom-call | tf_op jit(solution)/shard_map/pallas_call | solution.py:569
  45.8 1.3 collective-permute-done.14.rear
  47.6 1.6 collective-permute-start.17
  51.1 4.1 %shard_map.163 = (f32[1024,1024]{1,0:T(8,128)}, f32[1024,1024]{1,0:T(8,128)}) custom-call(s32[20]{0:T(128)} %dynamic-slice_bitcast_fusion.place, f32[64,1024]{1,0:T(8,128)} %copy-done.18, f32[64,1024]{1,0:T(8,128)} %copy-done.19, f32[64,1024]{1,0:T(8,128)} %copy-done.33, f32[64,1024]{1,0:T(8,128)} %copy-done.37, ...), custom_call_target="tpu_custom_call", output_to_operand_aliasing={{0}: (7, {}), {1}: (8, {})} | custom-call | tf_op jit(solution)/shard_map/pallas_call | solution.py:569
  55.8 1.3 collective-permute-done.18.rear
  57.6 1.6 collective-permute-start.21
  61.1 4.1 %shard_map.164 = (f32[1024,1024]{1,0:T(8,128)}, f32[1024,1024]{1,0:T(8,128)}) custom-call(s32[20]{0:T(128)} %dynamic-slice_bitcast_fusion.place, f32[64,1024]{1,0:T(8,128)} %copy-done.20, f32[64,1024]{1,0:T(8,128)} %copy-done.21, f32[64,1024]{1,0:T(8,128)} %copy-done.34, f32[64,1024]{1,0:T(8,128)} %copy-done.38, ...), custom_call_target="tpu_custom_call", output_to_operand_aliasing={{0}: (7, {}), {1}: (8, {})} | custom-call | tf_op jit(solution)/shard_map/pallas_call | solution.py:569
  65.8 1.3 collective-permute-done.22.rear
  67.2 1.5 collective-permute-start.25
  69.7 4.5 %collective-permute-done.25.fore = f32[64,1024]{1,0:T(8,128)S(1)} collective-permute-done((f32[64,1024]{1,0:T(8,128)S(1)}, f32[64,1024]{1,0:T(8,128)S(1)}, u32[]{:S(2)}, u32[]{:S(2)}) %collective-permute-start.25) | collective-permute-done | bytes 262176 | tf_op jit(solution)/shard_map/ppermute | solution.py:560
  74.2 1.3 collective-permute-done.26.rear
  76.9 4.2 %shard_map.165 = (f32[1024,1024]{1,0:T(8,128)}, f32[1024,1024]{1,0:T(8,128)}) custom-call(s32[20]{0:T(128)} %dynamic-slice_bitcast_fusion.place, f32[64,1024]{1,0:T(8,128)} %copy-done.13, f32[64,1024]{1,0:T(8,128)} %copy-done.15, f32[64,1024]{1,0:T(8,128)} %copy-done.26, f32[64,1024]{1,0:T(8,128)} %copy-done.27, ...), custom_call_target="tpu_custom_call", output_to_operand_aliasing={{0}: (7, {}), {1}: (8, {})} | custom-call | tf_op jit(solution)/shard_map/pallas_call | solution.py:569
  82.0 4.1 %shard_map.166 = (f32[1024,1024]{1,0:T(8,128)}, f32[1024,1024]{1,0:T(8,128)}) custom-call(s32[20]{0:T(128)} %dynamic-slice_bitcast_fusion.place, f32[64,1024]{1,0:T(8,128)} %copy-done.23, f32[64,1024]{1,0:T(8,128)} %copy-done.24, f32[64,1024]{1,0:T(8,128)} %copy-done.25, f32[64,1024]{1,0:T(8,128)} %copy-done.28, ...), custom_call_target="tpu_custom_call", output_to_operand_aliasing={{0}: (7, {}), {1}: (8, {})} | custom-call | tf_op jit(solution)/shard_map/pallas_call | solution.py:569
  86.0 31.8 %shard_map.167.field = f32[640,1024]{1,0:T(8,128)} custom-call(s32[20]{0:T(128)} %dynamic-slice_bitcast_fusion.place, f32[2]{0:T(128)} %depth.3, f32[1024,1024]{1,0:T(8,128)} %get-tuple-element.119.spec_a, f32[1024,1024]{1,0:T(8,128)} %get-tuple-element.120.spec_b, f32[2,1024,512]{2,1,0:T(8,128)} %constant.41.clone.gain, ...), custom_call_target="tpu_custom_call" | custom-call | tf_op jit(solution)/shard_map/pallas_call | solution.py:593
  118.2 4.7 %collective-permute-done.31.other = f32[640,1024]{1,0:T(8,128)S(1)} collective-permute-done((f32[640,1024]{1,0:T(8,128)}, f32[640,1024]{1,0:T(8,128)S(1)}, u32[]{:S(2)}, u32[]{:S(2)}) %collective-permute-start.31) | collective-permute-done | bytes 2621472 | tf_op jit(solution)/shard_map/ppermute | solution.py:608
  123.0 1.5 copy-done
  124.5 42.3 %shard_map.168 = (f32[6,64,1024]{2,1,0:T(8,128)}, bf16[1024,1024]{1,0:T(8,128)(2,1)}, bf16[1024,1024]{1,0:T(8,128)(2,1)}, bf16[1024,1024]{1,0:T(8,128)(2,1)}, bf16[1024,1024]{1,0:T(8,128)(2,1)}) custom-call(s32[20]{0:T(128)} %dynamic-slice_bitcast_fusion.place, f32[2]{0:T(128)} %depth.3, f32[640,1024]{1,0:T(8,128)} %shard_map.167.field, ...), custom_call_target="tpu_custom_call" | custom-call | tf_op jit(solution)/shard_map/pallas_call | solution.py:609
  166.8 3.9 %shard_map.169 = (f32[2,64,1024]{2,1,0:T(8,128)}, f32[2,64,1024]{2,1,0:T(8,128)}) custom-call(s32[20]{0:T(128)} %dynamic-slice_bitcast_fusion.place, bf16[1024,1024]{1,0:T(8,128)(2,1)} %get-tuple-element.173.high_a, bf16[1024,1024]{1,0:T(8,128)(2,1)} %get-tuple-element.174.low_a, bf16[1024,1024]{1,0:T(8,128)(2,1)} %get-tuple-element.175.high_b, ...), custom_call_target="tpu_custom_call" | custom-call | tf_op jit(solution)/shard_map/pallas_call | solution.py:634
  171.1 4.2 %shard_map.170 = (f32[2,64,1024]{2,1,0:T(8,128)}, f32[2,64,1024]{2,1,0:T(8,128)}) custom-call(s32[20]{0:T(128)} %dynamic-slice_bitcast_fusion.place, bf16[1024,1024]{1,0:T(8,128)(2,1)} %get-tuple-element.173.high_a, bf16[1024,1024]{1,0:T(8,128)(2,1)} %get-tuple-element.174.low_a, bf16[1024,1024]{1,0:T(8,128)(2,1)} %get-tuple-element.175.high_b, ...), custom_call_target="tpu_custom_call" | custom-call | tf_op jit(solution)/shard_map/pallas_call | solution.py:634
  176.3 1.4 collective-permute-start.35
  177.7 3.9 %shard_map.171 = (f32[2,64,1024]{2,1,0:T(8,128)}, f32[2,64,1024]{2,1,0:T(8,128)}) custom-call(s32[20]{0:T(128)} %dynamic-slice_bitcast_fusion.place, bf16[1024,1024]{1,0:T(8,128)(2,1)} %get-tuple-element.173.high_a, bf16[1024,1024]{1,0:T(8,128)(2,1)} %get-tuple-element.174.low_a, bf16[1024,1024]{1,0:T(8,128)(2,1)} %get-tuple-element.175.high_b, ...), custom_call_target="tpu_custom_call" | custom-call | tf_op jit(solution)/shard_map/pallas_call | solution.py:634
  181.6 2.5 %collective-permute-done.33 = f32[64,1024]{1,0:T(8,128)S(1)} collective-permute-done((f32[64,1024]{1,0:T(8,128)S(1)}, f32[64,1024]{1,0:T(8,128)S(1)}, u32[]{:S(2)}, u32[]{:S(2)}) %collective-permute-start.33) | collective-permute-done | bytes 262176 | tf_op jit(solution)/shard_map/ppermute | solution.py:653
  185.3 1.4 collective-permute-start.38
  186.8 4.0 %shard_map.172 = (f32[2,64,1024]{2,1,0:T(8,128)}, f32[2,64,1024]{2,1,0:T(8,128)}) custom-call(s32[20]{0:T(128)} %dynamic-slice_bitcast_fusion.place, bf16[1024,1024]{1,0:T(8,128)(2,1)} %get-tuple-element.173.high_a, bf16[1024,1024]{1,0:T(8,128)(2,1)} %get-tuple-element.174.low_a, bf16[1024,1024]{1,0:T(8,128)(2,1)} %get-tuple-element.175.high_b, ...), custom_call_target="tpu_custom_call" | custom-call | tf_op jit(solution)/shard_map/pallas_call | solution.py:634
  190.7 1.4 collective-permute-done.36
  193.1 1.6 collective-permute-start.41
  194.7 3.9 %shard_map.173 = (f32[2,64,1024]{2,1,0:T(8,128)}, f32[2,64,1024]{2,1,0:T(8,128)}) custom-call(s32[20]{0:T(128)} %dynamic-slice_bitcast_fusion.place, bf16[1024,1024]{1,0:T(8,128)(2,1)} %get-tuple-element.173.high_a, bf16[1024,1024]{1,0:T(8,128)(2,1)} %get-tuple-element.174.low_a, bf16[1024,1024]{1,0:T(8,128)(2,1)} %get-tuple-element.175.high_b, ...), custom_call_target="tpu_custom_call" | custom-call | tf_op jit(solution)/shard_map/pallas_call | solution.py:634
  200.6 1.6 collective-permute-start.44
  202.2 4.0 %shard_map.174 = (f32[2,64,1024]{2,1,0:T(8,128)}, f32[2,64,1024]{2,1,0:T(8,128)}) custom-call(s32[20]{0:T(128)} %dynamic-slice_bitcast_fusion.place, bf16[1024,1024]{1,0:T(8,128)(2,1)} %get-tuple-element.173.high_a, bf16[1024,1024]{1,0:T(8,128)(2,1)} %get-tuple-element.174.low_a, bf16[1024,1024]{1,0:T(8,128)(2,1)} %get-tuple-element.175.high_b, ...), custom_call_target="tpu_custom_call" | custom-call | tf_op jit(solution)/shard_map/pallas_call | solution.py:634
  206.1 1.4 collective-permute-done.42
  208.4 1.5 collective-permute-start.47
  209.9 3.9 %shard_map.175 = (f32[2,64,1024]{2,1,0:T(8,128)}, f32[2,64,1024]{2,1,0:T(8,128)}) custom-call(s32[20]{0:T(128)} %dynamic-slice_bitcast_fusion.place, bf16[1024,1024]{1,0:T(8,128)(2,1)} %get-tuple-element.173.high_a, bf16[1024,1024]{1,0:T(8,128)(2,1)} %get-tuple-element.174.low_a, bf16[1024,1024]{1,0:T(8,128)(2,1)} %get-tuple-element.175.high_b, ...), custom_call_target="tpu_custom_call" | custom-call | tf_op jit(solution)/shard_map/pallas_call | solution.py:634
  213.8 1.2 collective-permute-done.45
  216.1 1.3 collective-permute-start.52
  217.4 3.9 %shard_map.176 = (f32[2,64,1024]{2,1,0:T(8,128)}, f32[2,64,1024]{2,1,0:T(8,128)}) custom-call(s32[20]{0:T(128)} %dynamic-slice_bitcast_fusion.place, bf16[1024,1024]{1,0:T(8,128)(2,1)} %get-tuple-element.173.high_a, bf16[1024,1024]{1,0:T(8,128)(2,1)} %get-tuple-element.174.low_a, bf16[1024,1024]{1,0:T(8,128)(2,1)} %get-tuple-element.175.high_b, ...), custom_call_target="tpu_custom_call" | custom-call | tf_op jit(solution)/shard_map/pallas_call | solution.py:634
  221.3 1.4 collective-permute-done.48
  223.1 1.2 collective-permute-start.50
  225.1 5.1 %collective-permute-done.50 = f32[64,1024]{1,0:T(8,128)S(1)} collective-permute-done((f32[64,1024]{1,0:T(8,128)S(1)}, f32[64,1024]{1,0:T(8,128)S(1)}, u32[]{:S(2)}, u32[]{:S(2)}) %collective-permute-start.50) | collective-permute-done | bytes 262176 | tf_op jit(solution)/shard_map/ppermute | solution.py:653
  (174 shorter events, 33.9 us)
Async XLA Ops:
  0.6 28.0 %collective-permute-start.8 = (f32[6,64,1024]{2,1,0:T(8,128)}, f32[6,64,1024]{2,1,0:T(8,128)S(1)}, u32[]{:S(2)}, u32[]{:S(2)}) collective-permute-start(f32[6,64,1024]{2,1,0:T(8,128)} %seen.1), channel_id=1, source_target_pairs={{0,1},{1,0},{2,3},{3,2},{4,5},{5,4},{6,7},{7,6},{8,9},{9,8},{10,11... | collective-permute-start | bytes 4718600 | tf_op jit(solution)/shard_map/ppermute | solution.py:507
  3.3 4.5 %collective-permute-start.2 = (f32[64,1024]{1,0:T(8,128)S(1)}, f32[64,1024]{1,0:T(8,128)S(1)}, u32[]{:S(2)}, u32[]{:S(2)}) collective-permute-start(f32[64,1024]{1,0:T(8,128)S(1)} %get-tuple-element.197.fore), channel_id=1, source_target_pairs={{0,1},{1,0},{2,3},{3,2},{4,5},{5,4},{6,7},{7,6},{8,9},{9,8},{10,11... | collective-permute-start | bytes 786440 | tf_op jit(solution)/shard_map/ppermute | solution.py:562
  3.4 4.4 %collective-permute-start.3 = (f32[64,1024]{1,0:T(8,128)S(1)}, f32[64,1024]{1,0:T(8,128)S(1)}, u32[]{:S(2)}, u32[]{:S(2)}) collective-permute-start(f32[64,1024]{1,0:T(8,128)S(1)} %get-tuple-element.196.rear), channel_id=1, source_target_pairs={{0,1},{1,0},{2,3},{3,2},{4,5},{5,4},{6,7},{7,6},{8,9},{9,8},{10,11... | collective-permute-start | bytes 786440 | tf_op jit(solution)/shard_map/ppermute | solution.py:563
  3.9 9.5 %collective-permute-start = (f32[64,1024]{1,0:T(8,128)S(1)}, f32[64,1024]{1,0:T(8,128)S(1)}, u32[]{:S(2)}, u32[]{:S(2)}) collective-permute-start(f32[64,1024]{1,0:T(8,128)S(1)} %get-tuple-element.197.fore), channel_id=1, source_target_pairs={{0,4},{1,5},{4,8},{5,9},{8,12},{9,13},{12,14},{13,15},{14,10},{15,... | collective-permute-start | bytes 786440 | tf_op jit(solution)/shard_map/ppermute | solution.py:560
  6.5 8.4 %collective-permute-start.1 = (f32[64,1024]{1,0:T(8,128)S(1)}, f32[64,1024]{1,0:T(8,128)S(1)}, u32[]{:S(2)}, u32[]{:S(2)}) collective-permute-start(f32[64,1024]{1,0:T(8,128)S(1)} %get-tuple-element.196.rear), channel_id=1, source_target_pairs={{0,2},{1,3},{4,0},{5,1},{8,4},{9,5},{12,8},{13,9},{14,12},{15,13},... | collective-permute-start | bytes 786440 | tf_op jit(solution)/shard_map/ppermute | solution.py:561
  14.9 7.6 %collective-permute-start.6 = (f32[64,1024]{1,0:T(8,128)S(1)}, f32[64,1024]{1,0:T(8,128)S(1)}, u32[]{:S(2)}, u32[]{:S(2)}) collective-permute-start(f32[64,1024]{1,0:T(8,128)S(1)} %collective-permute-done.fore), channel_id=1, source_target_pairs={{0,1},{1,0},{2,3},{3,2},{4,5},{5,4},{6,7},{7,6},{8,9},{9,8},{10,11... | collective-permute-start | bytes 786440 | tf_op jit(solution)/shard_map/ppermute | solution.py:562
  14.9 7.7 %collective-permute-start.7 = (f32[64,1024]{1,0:T(8,128)S(1)}, f32[64,1024]{1,0:T(8,128)S(1)}, u32[]{:S(2)}, u32[]{:S(2)}) collective-permute-start(f32[64,1024]{1,0:T(8,128)S(1)} %collective-permute-done.1.rear), channel_id=1, source_target_pairs={{0,1},{1,0},{2,3},{3,2},{4,5},{5,4},{6,7},{7,6},{8,9},{9,8},{10,11... | collective-permute-start | bytes 786440 | tf_op jit(solution)/shard_map/ppermute | solution.py:563
  15.4 12.6 %collective-permute-start.4 = (f32[64,1024]{1,0:T(8,128)S(1)}, f32[64,1024]{1,0:T(8,128)S(1)}, u32[]{:S(2)}, u32[]{:S(2)}) collective-permute-start(f32[64,1024]{1,0:T(8,128)S(1)} %collective-permute-done.fore), channel_id=1, source_target_pairs={{0,4},{1,5},{4,8},{5,9},{8,12},{9,13},{12,14},{13,15},{14,10},{15,... | collective-permute-start | bytes 786440 | tf_op jit(solution)/shard_map/ppermute | solution.py:560
  17.0 11.0 %collective-permute-start.5 = (f32[64,1024]{1,0:T(8,128)S(1)}, f32[64,1024]{1,0:T(8,128)S(1)}, u32[]{:S(2)}, u32[]{:S(2)}) collective-permute-start(f32[64,1024]{1,0:T(8,128)S(1)} %collective-permute-done.1.rear), channel_id=1, source_target_pairs={{0,2},{1,3},{4,0},{5,1},{8,4},{9,5},{12,8},{13,9},{14,12},{15,13},... | collective-permute-start | bytes 786440 | tf_op jit(solution)/shard_map/ppermute | solution.py:561
  28.0 2.6 %collective-permute-start.11 = (f32[64,1024]{1,0:T(8,128)S(1)}, f32[64,1024]{1,0:T(8,128)S(1)}, u32[]{:S(2)}, u32[]{:S(2)}) collective-permute-start(f32[64,1024]{1,0:T(8,128)S(1)} %collective-permute-done.4.fore), channel_id=1, source_target_pairs={{0,1},{1,0},{2,3},{3,2},{4,5},{5,4},{6,7},{7,6},{8,9},{9,8},{10,11... | collective-permute-start | bytes 786440 | tf_op jit(solution)/shard_map/ppermute | solution.py:562
  28.6 8.3 %collective-permute-start.10 = (f32[64,1024]{1,0:T(8,128)S(1)}, f32[64,1024]{1,0:T(8,128)S(1)}, u32[]{:S(2)}, u32[]{:S(2)}) collective-permute-start(f32[64,1024]{1,0:T(8,128)S(1)} %collective-permute-done.5.rear), channel_id=1, source_target_pairs={{0,2},{1,3},{4,0},{5,1},{8,4},{9,5},{12,8},{13,9},{14,12},{15,13},... | collective-permute-start | bytes 786440 | tf_op jit(solution)/shard_map/ppermute | solution.py:561
  29.1 8.0 %collective-permute-start.9 = (f32[64,1024]{1,0:T(8,128)S(1)}, f32[64,1024]{1,0:T(8,128)S(1)}, u32[]{:S(2)}, u32[]{:S(2)}) collective-permute-start(f32[64,1024]{1,0:T(8,128)S(1)} %collective-permute-done.4.fore), channel_id=1, source_target_pairs={{0,4},{1,5},{4,8},{5,9},{8,12},{9,13},{12,14},{13,15},{14,10},{15,... | collective-permute-start | bytes 786440 | tf_op jit(solution)/shard_map/ppermute | solution.py:560
  37.1 2.5 %collective-permute-start.16 = (f32[64,1024]{1,0:T(8,128)S(1)}, f32[64,1024]{1,0:T(8,128)S(1)}, u32[]{:S(2)}, u32[]{:S(2)}) collective-permute-start(f32[64,1024]{1,0:T(8,128)S(1)} %collective-permute-done.10.rear), channel_id=1, source_target_pairs={{0,1},{1,0},{2,3},{3,2},{4,5},{5,4},{6,7},{7,6},{8,9},{9,8},{10,11... | collective-permute-start | bytes 786440 | tf_op jit(solution)/shard_map/ppermute | solution.py:563
  37.6 8.2 %collective-permute-start.13 = (f32[64,1024]{1,0:T(8,128)S(1)}, f32[64,1024]{1,0:T(8,128)S(1)}, u32[]{:S(2)}, u32[]{:S(2)}) collective-permute-start(f32[64,1024]{1,0:T(8,128)S(1)} %collective-permute-done.9.fore), channel_id=1, source_target_pairs={{0,4},{1,5},{4,8},{5,9},{8,12},{9,13},{12,14},{13,15},{14,10},{15,... | collective-permute-start | bytes 786440 | tf_op jit(solution)/shard_map/ppermute | solution.py:560
  39.2 7.9 %collective-permute-start.14 = (f32[64,1024]{1,0:T(8,128)S(1)}, f32[64,1024]{1,0:T(8,128)S(1)}, u32[]{:S(2)}, u32[]{:S(2)}) collective-permute-start(f32[64,1024]{1,0:T(8,128)S(1)} %collective-permute-done.10.rear), channel_id=1, source_target_pairs={{0,2},{1,3},{4,0},{5,1},{8,4},{9,5},{12,8},{13,9},{14,12},{15,13},... | collective-permute-start | bytes 786440 | tf_op jit(solution)/shard_map/ppermute | solution.py:561
  47.6 8.2 %collective-permute-start.17 = (f32[64,1024]{1,0:T(8,128)S(1)}, f32[64,1024]{1,0:T(8,128)S(1)}, u32[]{:S(2)}, u32[]{:S(2)}) collective-permute-start(f32[64,1024]{1,0:T(8,128)S(1)} %collective-permute-done.13.fore), channel_id=1, source_target_pairs={{0,4},{1,5},{4,8},{5,9},{8,12},{9,13},{12,14},{13,15},{14,10},{15,... | collective-permute-start | bytes 786440 | tf_op jit(solution)/shard_map/ppermute | solution.py:560
  49.2 7.9 %collective-permute-start.18 = (f32[64,1024]{1,0:T(8,128)S(1)}, f32[64,1024]{1,0:T(8,128)S(1)}, u32[]{:S(2)}, u32[]{:S(2)}) collective-permute-start(f32[64,1024]{1,0:T(8,128)S(1)} %collective-permute-done.14.rear), channel_id=1, source_target_pairs={{0,2},{1,3},{4,0},{5,1},{8,4},{9,5},{12,8},{13,9},{14,12},{15,13},... | collective-permute-start | bytes 786440 | tf_op jit(solution)/shard_map/ppermute | solution.py:561
  57.6 8.2 %collective-permute-start.21 = (f32[64,1024]{1,0:T(8,128)S(1)}, f32[64,1024]{1,0:T(8,128)S(1)}, u32[]{:S(2)}, u32[]{:S(2)}) collective-permute-start(f32[64,1024]{1,0:T(8,128)S(1)} %collective-permute-done.17.fore), channel_id=1, source_target_pairs={{0,4},{1,5},{4,8},{5,9},{8,12},{9,13},{12,14},{13,15},{14,10},{15,... | collective-permute-start | bytes 786440 | tf_op jit(solution)/shard_map/ppermute | solution.py:560
  59.2 7.9 %collective-permute-start.22 = (f32[64,1024]{1,0:T(8,128)S(1)}, f32[64,1024]{1,0:T(8,128)S(1)}, u32[]{:S(2)}, u32[]{:S(2)}) collective-permute-start(f32[64,1024]{1,0:T(8,128)S(1)} %collective-permute-done.18.rear), channel_id=1, source_target_pairs={{0,2},{1,3},{4,0},{5,1},{8,4},{9,5},{12,8},{13,9},{14,12},{15,13},... | collective-permute-start | bytes 786440 | tf_op jit(solution)/shard_map/ppermute | solution.py:561
  67.2 7.0 %collective-permute-start.25 = (f32[64,1024]{1,0:T(8,128)S(1)}, f32[64,1024]{1,0:T(8,128)S(1)}, u32[]{:S(2)}, u32[]{:S(2)}) collective-permute-start(f32[64,1024]{1,0:T(8,128)S(1)} %collective-permute-done.21.fore), channel_id=1, source_target_pairs={{0,4},{1,5},{4,8},{5,9},{8,12},{9,13},{12,14},{13,15},{14,10},{15,... | collective-permute-start | bytes 786440 | tf_op jit(solution)/shard_map/ppermute | solution.py:560
  68.7 6.8 %collective-permute-start.26 = (f32[64,1024]{1,0:T(8,128)S(1)}, f32[64,1024]{1,0:T(8,128)S(1)}, u32[]{:S(2)}, u32[]{:S(2)}) collective-permute-start(f32[64,1024]{1,0:T(8,128)S(1)} %collective-permute-done.22.rear), channel_id=1, source_target_pairs={{0,2},{1,3},{4,0},{5,1},{8,4},{9,5},{12,8},{13,9},{14,12},{15,13},... | collective-permute-start | bytes 786440 | tf_op jit(solution)/shard_map/ppermute | solution.py:561
  69.2 6.3 %collective-permute-start.29 = (f32[64,1024]{1,0:T(8,128)S(1)}, f32[64,1024]{1,0:T(8,128)S(1)}, u32[]{:S(2)}, u32[]{:S(2)}) collective-permute-start(f32[64,1024]{1,0:T(8,128)S(1)} %collective-permute-done.21.fore), channel_id=1, source_target_pairs={{0,1},{1,0},{2,3},{3,2},{4,5},{5,4},{6,7},{7,6},{8,9},{9,8},{10,11... | collective-permute-start | bytes 786440 | tf_op jit(solution)/shard_map/ppermute | solution.py:562
  69.2 6.3 %collective-permute-start.30 = (f32[64,1024]{1,0:T(8,128)S(1)}, f32[64,1024]{1,0:T(8,128)S(1)}, u32[]{:S(2)}, u32[]{:S(2)}) collective-permute-start(f32[64,1024]{1,0:T(8,128)S(1)} %collective-permute-done.22.rear), channel_id=1, source_target_pairs={{0,1},{1,0},{2,3},{3,2},{4,5},{5,4},{6,7},{7,6},{8,9},{9,8},{10,11... | collective-permute-start | bytes 786440 | tf_op jit(solution)/shard_map/ppermute | solution.py:563
  74.2 7.0 %collective-permute-start.27 = (f32[64,1024]{1,0:T(8,128)S(1)}, f32[64,1024]{1,0:T(8,128)S(1)}, u32[]{:S(2)}, u32[]{:S(2)}) collective-permute-start(f32[64,1024]{1,0:T(8,128)S(1)} %collective-permute-done.25.fore), channel_id=1, source_target_pairs={{0,1},{1,0},{2,3},{3,2},{4,5},{5,4},{6,7},{7,6},{8,9},{9,8},{10,11... | collective-permute-start | bytes 786440 | tf_op jit(solution)/shard_map/ppermute | solution.py:562
  75.5 5.7 %collective-permute-start.28 = (f32[64,1024]{1,0:T(8,128)S(1)}, f32[64,1024]{1,0:T(8,128)S(1)}, u32[]{:S(2)}, u32[]{:S(2)}) collective-permute-start(f32[64,1024]{1,0:T(8,128)S(1)} %collective-permute-done.26.rear), channel_id=1, source_target_pairs={{0,1},{1,0},{2,3},{3,2},{4,5},{5,4},{6,7},{7,6},{8,9},{9,8},{10,11... | collective-permute-start | bytes 786440 | tf_op jit(solution)/shard_map/ppermute | solution.py:563
  117.8 5.2 %collective-permute-start.31 = (f32[640,1024]{1,0:T(8,128)}, f32[640,1024]{1,0:T(8,128)S(1)}, u32[]{:S(2)}, u32[]{:S(2)}) collective-permute-start(f32[640,1024]{1,0:T(8,128)} %shard_map.167.field), channel_id=1, source_target_pairs={{0,1},{1,0},{2,3},{3,2},{4,5},{5,4},{6,7},{7,6},{8,9},{9,8},{10,11... | collective-permute-start | bytes 7864328 | tf_op jit(solution)/shard_map/ppermute | solution.py:608
  170.7 4.8 %collective-permute-start.32 = (f32[2,64,1024]{2,1,0:T(8,128)}, f32[2,64,1024]{2,1,0:T(8,128)S(1)}, u32[]{:S(2)}, u32[]{:S(2)}) collective-permute-start(f32[2,64,1024]{2,1,0:T(8,128)} %get-tuple-element.129), channel_id=1, source_target_pairs={{0,1},{1,0},{2,3},{3,2},{4,5},{5,4},{6,7},{7,6},{8,9},{9,8},{10,11... | collective-permute-start | bytes 1572872 | tf_op jit(solution)/shard_map/ppermute | solution.py:643
  175.3 6.4 %collective-permute-start.34 = (f32[2,64,1024]{2,1,0:T(8,128)}, f32[2,64,1024]{2,1,0:T(8,128)S(1)}, u32[]{:S(2)}, u32[]{:S(2)}) collective-permute-start(f32[2,64,1024]{2,1,0:T(8,128)} %get-tuple-element.132), channel_id=1, source_target_pairs={{0,1},{1,0},{2,3},{3,2},{4,5},{5,4},{6,7},{7,6},{8,9},{9,8},{10,11... | collective-permute-start | bytes 1572872 | tf_op jit(solution)/shard_map/ppermute | solution.py:643
  175.6 8.5 %collective-permute-start.33 = (f32[64,1024]{1,0:T(8,128)S(1)}, f32[64,1024]{1,0:T(8,128)S(1)}, u32[]{:S(2)}, u32[]{:S(2)}) collective-permute-start(f32[64,1024]{1,0:T(8,128)S(1)} %get-tuple-element.130), channel_id=1, source_target_pairs={{0,4},{1,5},{4,8},{5,9},{8,12},{9,13},{12,14},{13,15},{14,10},{15,... | collective-permute-start | bytes 786440 | tf_op jit(solution)/shard_map/ppermute | solution.py:653
  176.3 8.3 %collective-permute-start.35 = (f32[64,1024]{1,0:T(8,128)S(1)}, f32[64,1024]{1,0:T(8,128)S(1)}, u32[]{:S(2)}, u32[]{:S(2)}) collective-permute-start(f32[64,1024]{1,0:T(8,128)S(1)} %get-tuple-element.133), channel_id=1, source_target_pairs={{0,2},{1,3},{4,0},{5,1},{8,4},{9,5},{12,8},{13,9},{14,12},{15,13},... | collective-permute-start | bytes 786440 | tf_op jit(solution)/shard_map/ppermute | solution.py:654
  181.6 9.1 %collective-permute-start.37 = (f32[2,64,1024]{2,1,0:T(8,128)}, f32[2,64,1024]{2,1,0:T(8,128)S(1)}, u32[]{:S(2)}, u32[]{:S(2)}) collective-permute-start(f32[2,64,1024]{2,1,0:T(8,128)} %get-tuple-element.140), channel_id=1, source_target_pairs={{0,1},{1,0},{2,3},{3,2},{4,5},{5,4},{6,7},{7,6},{8,9},{9,8},{10,11... | collective-permute-start | bytes 1572872 | tf_op jit(solution)/shard_map/ppermute | solution.py:643
  184.7 7.5 %collective-permute-start.36 = (f32[64,1024]{1,0:T(8,128)S(1)}, f32[64,1024]{1,0:T(8,128)S(1)}, u32[]{:S(2)}, u32[]{:S(2)}) collective-permute-start(f32[64,1024]{1,0:T(8,128)S(1)} %get-tuple-element.138), channel_id=1, source_target_pairs={{0,4},{1,5},{4,8},{5,9},{8,12},{9,13},{12,14},{13,15},{14,10},{15,... | collective-permute-start | bytes 786440 | tf_op jit(solution)/shard_map/ppermute | solution.py:653
  185.3 7.2 %collective-permute-start.38 = (f32[64,1024]{1,0:T(8,128)S(1)}, f32[64,1024]{1,0:T(8,128)S(1)}, u32[]{:S(2)}, u32[]{:S(2)}) collective-permute-start(f32[64,1024]{1,0:T(8,128)S(1)} %get-tuple-element.141), channel_id=1, source_target_pairs={{0,2},{1,3},{4,0},{5,1},{8,4},{9,5},{12,8},{13,9},{14,12},{15,13},... | collective-permute-start | bytes 786440 | tf_op jit(solution)/shard_map/ppermute | solution.py:654
  190.7 7.9 %collective-permute-start.40 = (f32[2,64,1024]{2,1,0:T(8,128)}, f32[2,64,1024]{2,1,0:T(8,128)S(1)}, u32[]{:S(2)}, u32[]{:S(2)}) collective-permute-start(f32[2,64,1024]{2,1,0:T(8,128)} %get-tuple-element.148), channel_id=1, source_target_pairs={{0,1},{1,0},{2,3},{3,2},{4,5},{5,4},{6,7},{7,6},{8,9},{9,8},{10,11... | collective-permute-start | bytes 1572872 | tf_op jit(solution)/shard_map/ppermute | solution.py:643
  192.6 7.0 %collective-permute-start.39 = (f32[64,1024]{1,0:T(8,128)S(1)}, f32[64,1024]{1,0:T(8,128)S(1)}, u32[]{:S(2)}, u32[]{:S(2)}) collective-permute-start(f32[64,1024]{1,0:T(8,128)S(1)} %get-tuple-element.146), channel_id=1, source_target_pairs={{0,4},{1,5},{4,8},{5,9},{8,12},{9,13},{12,14},{13,15},{14,10},{15,... | collective-permute-start | bytes 786440 | tf_op jit(solution)/shard_map/ppermute | solution.py:653
  193.1 6.8 %collective-permute-start.41 = (f32[64,1024]{1,0:T(8,128)S(1)}, f32[64,1024]{1,0:T(8,128)S(1)}, u32[]{:S(2)}, u32[]{:S(2)}) collective-permute-start(f32[64,1024]{1,0:T(8,128)S(1)} %get-tuple-element.149), channel_id=1, source_target_pairs={{0,2},{1,3},{4,0},{5,1},{8,4},{9,5},{12,8},{13,9},{14,12},{15,13},... | collective-permute-start | bytes 786440 | tf_op jit(solution)/shard_map/ppermute | solution.py:654
  198.6 7.5 %collective-permute-start.43 = (f32[2,64,1024]{2,1,0:T(8,128)}, f32[2,64,1024]{2,1,0:T(8,128)S(1)}, u32[]{:S(2)}, u32[]{:S(2)}) collective-permute-start(f32[2,64,1024]{2,1,0:T(8,128)} %get-tuple-element.156), channel_id=1, source_target_pairs={{0,1},{1,0},{2,3},{3,2},{4,5},{5,4},{6,7},{7,6},{8,9},{9,8},{10,11... | collective-permute-start | bytes 1572872 | tf_op jit(solution)/shard_map/ppermute | solution.py:643
  200.1 7.5 %collective-permute-start.42 = (f32[64,1024]{1,0:T(8,128)S(1)}, f32[64,1024]{1,0:T(8,128)S(1)}, u32[]{:S(2)}, u32[]{:S(2)}) collective-permute-start(f32[64,1024]{1,0:T(8,128)S(1)} %get-tuple-element.154), channel_id=1, source_target_pairs={{0,4},{1,5},{4,8},{5,9},{8,12},{9,13},{12,14},{13,15},{14,10},{15,... | collective-permute-start | bytes 786440 | tf_op jit(solution)/shard_map/ppermute | solution.py:653
  200.6 7.1 %collective-permute-start.44 = (f32[64,1024]{1,0:T(8,128)S(1)}, f32[64,1024]{1,0:T(8,128)S(1)}, u32[]{:S(2)}, u32[]{:S(2)}) collective-permute-start(f32[64,1024]{1,0:T(8,128)S(1)} %get-tuple-element.157), channel_id=1, source_target_pairs={{0,2},{1,3},{4,0},{5,1},{8,4},{9,5},{12,8},{13,9},{14,12},{15,13},... | collective-permute-start | bytes 786440 | tf_op jit(solution)/shard_map/ppermute | solution.py:654
  206.1 7.7 %collective-permute-start.46 = (f32[2,64,1024]{2,1,0:T(8,128)}, f32[2,64,1024]{2,1,0:T(8,128)S(1)}, u32[]{:S(2)}, u32[]{:S(2)}) collective-permute-start(f32[2,64,1024]{2,1,0:T(8,128)} %get-tuple-element.164), channel_id=1, source_target_pairs={{0,1},{1,0},{2,3},{3,2},{4,5},{5,4},{6,7},{7,6},{8,9},{9,8},{10,11... | collective-permute-start | bytes 1572872 | tf_op jit(solution)/shard_map/ppermute | solution.py:643
  207.8 7.2 %collective-permute-start.45 = (f32[64,1024]{1,0:T(8,128)S(1)}, f32[64,1024]{1,0:T(8,128)S(1)}, u32[]{:S(2)}, u32[]{:S(2)}) collective-permute-start(f32[64,1024]{1,0:T(8,128)S(1)} %get-tuple-element.162), channel_id=1, source_target_pairs={{0,4},{1,5},{4,8},{5,9},{8,12},{9,13},{12,14},{13,15},{14,10},{15,... | collective-permute-start | bytes 786440 | tf_op jit(solution)/shard_map/ppermute | solution.py:653
  208.4 6.8 %collective-permute-start.47 = (f32[64,1024]{1,0:T(8,128)S(1)}, f32[64,1024]{1,0:T(8,128)S(1)}, u32[]{:S(2)}, u32[]{:S(2)}) collective-permute-start(f32[64,1024]{1,0:T(8,128)S(1)} %get-tuple-element.165), channel_id=1, source_target_pairs={{0,2},{1,3},{4,0},{5,1},{8,4},{9,5},{12,8},{13,9},{14,12},{15,13},... | collective-permute-start | bytes 786440 | tf_op jit(solution)/shard_map/ppermute | solution.py:654
  213.8 7.5 %collective-permute-start.49 = (f32[2,64,1024]{2,1,0:T(8,128)}, f32[2,64,1024]{2,1,0:T(8,128)S(1)}, u32[]{:S(2)}, u32[]{:S(2)}) collective-permute-start(f32[2,64,1024]{2,1,0:T(8,128)} %get-tuple-element.172), channel_id=1, source_target_pairs={{0,1},{1,0},{2,3},{3,2},{4,5},{5,4},{6,7},{7,6},{8,9},{9,8},{10,11... | collective-permute-start | bytes 1572872 | tf_op jit(solution)/shard_map/ppermute | solution.py:643
  215.3 7.5 %collective-permute-start.48 = (f32[64,1024]{1,0:T(8,128)S(1)}, f32[64,1024]{1,0:T(8,128)S(1)}, u32[]{:S(2)}, u32[]{:S(2)}) collective-permute-start(f32[64,1024]{1,0:T(8,128)S(1)} %get-tuple-element.170), channel_id=1, source_target_pairs={{0,4},{1,5},{4,8},{5,9},{8,12},{9,13},{12,14},{13,15},{14,10},{15,... | collective-permute-start | bytes 786440 | tf_op jit(solution)/shard_map/ppermute | solution.py:653
  216.1 6.9 %collective-permute-start.52 = (f32[64,1024]{1,0:T(8,128)S(1)}, f32[64,1024]{1,0:T(8,128)S(1)}, u32[]{:S(2)}, u32[]{:S(2)}) collective-permute-start(f32[64,1024]{1,0:T(8,128)S(1)} %get-tuple-element.179), channel_id=1, source_target_pairs={{0,2},{1,3},{4,0},{5,1},{8,4},{9,5},{12,8},{13,9},{14,12},{15,13},... | collective-permute-start | bytes 786440 | tf_op jit(solution)/shard_map/ppermute | solution.py:654
  221.3 3.8 %collective-permute-start.51 = (f32[2,64,1024]{2,1,0:T(8,128)}, f32[2,64,1024]{2,1,0:T(8,128)S(1)}, u32[]{:S(2)}, u32[]{:S(2)}) collective-permute-start(f32[2,64,1024]{2,1,0:T(8,128)} %get-tuple-element.178), channel_id=1, source_target_pairs={{0,1},{1,0},{2,3},{3,2},{4,5},{5,4},{6,7},{7,6},{8,9},{9,8},{10,11... | collective-permute-start | bytes 1572872 | tf_op jit(solution)/shard_map/ppermute | solution.py:643
  223.1 7.2 %collective-permute-start.50 = (f32[64,1024]{1,0:T(8,128)S(1)}, f32[64,1024]{1,0:T(8,128)S(1)}, u32[]{:S(2)}, u32[]{:S(2)}) collective-permute-start(f32[64,1024]{1,0:T(8,128)S(1)} %get-tuple-element.182), channel_id=1, source_target_pairs={{0,4},{1,5},{4,8},{5,9},{8,12},{9,13},{12,14},{13,15},{14,10},{15,... | collective-permute-start | bytes 786440 | tf_op jit(solution)/shard_map/ppermute | solution.py:653
  224.3 6.4 %collective-permute-start.53 = (f32[64,1024]{1,0:T(8,128)S(1)}, f32[64,1024]{1,0:T(8,128)S(1)}, u32[]{:S(2)}, u32[]{:S(2)}) collective-permute-start(f32[64,1024]{1,0:T(8,128)S(1)} %get-tuple-element.183), channel_id=1, source_target_pairs={{0,2},{1,3},{4,0},{5,1},{8,4},{9,5},{12,8},{13,9},{14,12},{15,13},... | collective-permute-start | bytes 786440 | tf_op jit(solution)/shard_map/ppermute | solution.py:654
  (47 other events, 167.2 us)
where the time goes:
time: 234 us; the launch traced here: 233 us
  Pallas kernels  144 us (62%)
  waiting for transfers between devices  35.1 us (15%)
  starting transfers between devices  34.7 us (15%)
  local copies, waits for them, and re-layouts  13.3 us (6%)
  other arithmetic  4.68 us (2%)
    pallas_call x1, Pallas kernels, body(): call(adjoint_kernel, own, [smem] + [const((5 * span, side))] * 2 + [const...  42.3 us
    pallas_call x8, Pallas kernels, body(): call(functools.partial(rows_kernel, step > 0), 1, in_specs, [chip_block((...  32.9 us
    pallas_call x1, Pallas kernels, body(): call(forward_kernel, own, [smem] + [lanes((side, wide))] * 2 + shared + [...  31.8 us
    pallas_call x8, Pallas kernels, share(): call(strips_kernel, 1, [chip_block((span, side), l, offset) for l in (0,...  31.7 us
    ppermute x7, waiting for transfers between devices, body(): fore = lax.ppermute(now[0], 'tile', ahead)  14 us
    ppermute x7, starting transfers between devices, body(): fore = lax.ppermute(fore, 'tile', ahead)  12.1 us
    unnamed x82, local copies, waits for them, and re-layouts  12 us
    ppermute x7, starting transfers between devices, body(): rear = lax.ppermute(now[1], 'tile', back)  9.71 us
  transfers between devices with their start and end apart: 54, of which 26 were waited for; matrix products, arithmetic and copies ran while one was open for 2% of the time, Pallas kernels for 27%

commit v1 on v0

--- a/solution.py
+++ b/solution.py
@@ -179,9 +179,13 @@
 STRIP = 16
 
 
+def length(wave_x, ky, g):
+    kx = wave_x[g * LANES : (g + 1) * LANES, :]
+    return jnp.sqrt(kx * kx + ky * ky)
+
+
 def decay(modulus, gain, depth, l, g):
-    here = slice(g * LANES, (g + 1) * LANES)
-    return jnp.exp(-modulus[0, here, :] * depth[l]) * gain[0, here, :]
+    return jnp.exp(-modulus * depth[l]) * gain[0, g * LANES : (g + 1) * LANES, :]
 
 
 def on_core(place, run):
@@ -206,74 +210,107 @@
     return gather(pairs)
 
 
-def rows_kernel(later, place, fore, rear, far_fore, far_rear, mix_h, mix_l, *rest):
-    spec_a, spec_b, val = rest[2:] if later else rest
-    rows = fore.shape[0]
+def rows_kernel(at, place, *refs):
+    blocks, far, olds, spec, give, val = refs
+    core = place[0]
+    rows = (far[0][1] if give is None else give).shape[0] // 2
+    span = 2 * rows
+
+    def spot(offset, layer, whose):
+        chip = place[2 + 2 * offset + layer]
+        return pl.ds(pl.multiple_of(chip * span + whose * rows, rows), rows)
+
+    for offset, source in far:
+        for l in (0, 1):
+            spec[l][spot(offset, l, 1 - core), :] = source[l * rows : (l + 1) * rows, :]
+    if not blocks:
+        return
+    mix_h, mix_l = olds
+    own = mix_h.shape[1]
+    wide = 2 * LANES
+    height = blocks[0].shape[0]
+    for n, source in enumerate(blocks):
+        for i in range(height // STRIP):
+            strip = slice(i * STRIP, (i + 1) * STRIP)
+            here = slice(n * height + strip.start, n * height + strip.stop)
+            below = slice(span + here.start, span + here.stop)
+            f = [source[strip, a * LANES : (a + 1) * LANES] for a in range(2 * own)]
+            for g, pair in enumerate(spread(f)):
+                for k, value in enumerate(pair):
+                    lane = slice(k * LANES, (k + 1) * LANES)
+                    val[g, here, lane], val[g, below, lane] = halves(value)
+    for g in range(own):
+        lane = slice(g * wide, (g + 1) * wide)
+        out = mixed(val[core * own + g], mix_h[core, g], mix_l[core, g])
+        for l in (0, 1):
+            spec[l][spot(at, l, core), lane] = out[l * rows : (l + 1) * rows]
+        peer = 1 - core
+        give[:, lane] = mixed(val[peer * own + g], mix_h[peer, g], mix_l[peer, g])
+
+
+def rows_first(place, a, b, mix_h, mix_l, spec_a, spec_b, give, val):
+    rows_kernel(0, place, (a, b), (), (mix_h, mix_l), (spec_a, spec_b), give, val)
+
+
+def rows_next(at, place, a, b, mix_h, mix_l, far, x, y, spec_a, spec_b, give, val):
+    rows_kernel(at, place, (a, b), ((at - 1, far),), (mix_h, mix_l), (spec_a, spec_b), give, val)
+
+
+def rows_apart(at, place, a, b, mix_h, mix_l, x, y, spec_a, spec_b, give, val):
+    rows_kernel(at, place, (a, b), (), (mix_h, mix_l), (spec_a, spec_b), give, val)
+
+
+def rows_last(at, place, before, far, x, y, spec_a, spec_b):
+    rows_kernel(
+        at, place, (), ((at - 1, before), (at, far)), None, (spec_a, spec_b), None, None
+    )
+
+
+def strips_kernel(at, place, high_a, low_a, high_b, low_b, mix_h, mix_l, *rest):
+    keep, give, val = rest[:2], rest[2], rest[3]
+    rows = keep[0].shape[0]
     own = mix_h.shape[1]
     span = 2 * rows
-    wide = 2 * LANES
-
-    def run(core):
-        for l, pair in enumerate(((fore, far_fore), (rear, far_rear))):
-            for k, source in enumerate(pair):
-                start = l * span + (core if k == 0 else 1 - core) * rows
-                for i in range(rows // STRIP):
-                    at = slice(i * STRIP, (i + 1) * STRIP)
-                    here = slice(start + i * STRIP, start + (i + 1) * STRIP)
-                    below = slice(2 * span + here.start, 2 * span + here.stop)
-
-                    def write(g, lane, high, low):
-                        val[g, here, lane] = high
-                        val[g, below, lane] = low
-
-                    split_lanes(core, own, lambda lane: source[at, lane], write)
-
-    on_core(place, run)
-    for g in range(own):
-        out = mixed(val[g], mix_h[0, g], mix_l[0, g])
-        spec_a[:, g * wide : (g + 1) * wide] = out[:span]
-        spec_b[:, g * wide : (g + 1) * wide] = out[span:]
-
-
-def strips_kernel(place, high_a, low_a, high_b, low_b, mix_h, mix_l, keep, give, val):
-    rows = keep.shape[1]
-    own = mix_h.shape[1]
-    span = 2 * rows
+    spot = [pl.ds(pl.multiple_of(place[at + l] * span, span), span) for l in (0, 1)]
     for g in range(own):
         lanes = slice(g * 2 * LANES, (g + 1) * 2 * LANES)
-        values = jnp.concatenate([a[:, lanes] for a in (high_a, high_b, low_a, low_b)])
-        val[g] = mixed(values, mix_h[0, g], mix_l[0, g])
+        parts = ((high_a, 0), (high_b, 1), (low_a, 0), (low_b, 1))
+        values = jnp.concatenate([a[spot[l], lanes] for a, l in parts])
+        val[g] = mixed(values, mix_h[place[0], g], mix_l[place[0], g])
 
     def run(core):
         for l in (0, 1):
-            for target, part in ((keep, core), (give, 1 - core)):
+            for target, part, base in ((keep[l], core, 0), (give, 1 - core, l * rows)):
                 for i in range(rows // 8):
                     start = l * span + part * rows + i * 8
                     blocks = join_lanes(
                         core, own, lambda g, lane: val[g, start : start + 8, lane]
                     )
+                    here = slice(base + i * 8, base + (i + 1) * 8)
                     for a, value in enumerate(blocks):
-                        target[l, i * 8 : (i + 1) * 8, a * LANES : (a + 1) * LANES] = value
+                        target[here, a * LANES : (a + 1) * LANES] = value
 
     on_core(place, run)
 
 
 def forward_kernel(
-    place, depth, spec_a, spec_b, gain, modulus, wave, mix, near, back_h, back_l,
+    place, depth, spec_a, spec_b, gain, wave_x, wave, mix, near, back_h, back_l,
     out, val_h, val_l, sum_h, sum_l, steep_h, steep_l, lines,
 ):
     specs = (spec_a, spec_b)
     layers = len(specs)
     groups = mix.shape[0]
-    span = near.shape[1] // 6
+    span = near.shape[0] // 6
     wide = 2 * LANES
     own = groups // 2
+    step = pl.program_id(0)
+    column = pl.ds(pl.multiple_of(step * wide, wide), wide)
 
     for l in range(layers):
 
         def strip(i, carry, l=l):
             at = pl.multiple_of(i * STRIP, STRIP)
-            f = [specs[l][pl.ds(a * LANES + at, STRIP), :] for a in range(groups)]
+            f = [specs[l][pl.ds(a * LANES + at, STRIP), column] for a in range(groups)]
             for g, (p, q) in enumerate(spread(f)):
                 high, low = halves(p)
                 val_h[l, g, pl.ds(at, STRIP), :] = high
@@ -285,21 +322,22 @@
 
         lax.fori_loop(0, LANES // STRIP, strip, 0)
 
+    ky = wave[0, 0, 0:1, :]
     for g in range(groups):
         total = None
+        modulus = length(wave_x, ky, g)
         for l in range(layers):
             cols = stacked(mix[g], val_h[l, g], val_l[l, g], wide)
             cols = cols * double(decay(modulus, gain, depth, l, g))
             total = cols if total is None else total + cols
         here = pl.ds(g * wide, wide)
         sum_h[here, :], sum_l[here, :] = halves(total)
-        steep = total * double(modulus[0, g * LANES : (g + 1) * LANES, :])
+        steep = total * double(modulus)
         steep_h[here, :], steep_l[here, :] = halves(steep)
 
-    plain = stacked(near[0], sum_h[...], sum_l[...], 3 * span)
-    slopes = jnp.concatenate([near[0, : 2 * span], near[0, 3 * span : 5 * span]])
+    plain = stacked(near[...], sum_h[...], sum_l[...], 3 * span)
+    slopes = jnp.concatenate([near[: 2 * span], near[3 * span : 5 * span]])
     sloped = stacked(slopes, steep_h[...], steep_l[...], 2 * span)
-    ky = wave[0, 0, 0:1, :]
     both = twofold(ky)
     values = jnp.concatenate(
         [
@@ -310,7 +348,6 @@
             turn(sloped[:span], ky),
         ]
     )
-    step = pl.program_id(0)
     lines[step] = mixed(jnp.concatenate(halves(values)), back_h[0, 0], back_l[0, 0])
 
     @pl.when(step == own - 1)
@@ -328,14 +365,30 @@
         on_core(place, run)
 
 
-def transpose_kernel(place, near, far):
-    for g in range(far.shape[0] // (2 * LANES)):
-        lane = slice(g * 2 * LANES, (g + 1) * 2 * LANES)
-        far[lane, :] = near[0, :, lane].T
+def near_kernel(place, base, rotate, wave, near, far):
+    span = near.shape[0] // 6
+    start = place[1] * span
+    first = pl.multiple_of(lax.rem(start, LANES), STRIP)
+    rows = pl.ds(first, span)
+    block = lax.div(start, LANES)
+    for g in range(far.shape[0]):
+        lane = slice(g * LANES, (g + 1) * LANES)
+        both = slice(2 * g * LANES, 2 * (g + 1) * LANES)
+        cos_b, sin_b = base[0, rows, lane], base[1, rows, lane]
+        cos_a, sin_a = rotate[block, 0:1, lane], rotate[block, 8:9, lane]
+        c = cos_b * cos_a - sin_b * sin_a
+        s = sin_b * cos_a + cos_b * sin_a
+        k = wave[0:1, lane]
+        value = jnp.concatenate([c, s], axis=1)
+        slope = jnp.concatenate([-k * s, k * c], axis=1)
+        bend = -twofold(k * k) * value
+        for n, half in enumerate(halves(jnp.concatenate([value, slope, bend]))):
+            near[n * 3 * span : (n + 1) * 3 * span, both] = half
+            far[g, n * 2 * LANES : (n + 1) * 2 * LANES, :] = half.T
 
 
 def adjoint_kernel(
-    place, depth, field, other, seen, far_seen, gain, modulus, wave, mix, far, fold_h, fold_l,
+    place, depth, field, other, seen, far_seen, gain, wave_x, wave, mix, far, fold_h, fold_l,
     predicted, high_a, low_a, high_b, low_b, left, val_y, val,
 ):
     grids = ((high_a, low_a), (high_b, low_b))
@@ -395,6 +448,7 @@
 
         on_core(place, run)
 
+    column = pl.ds(pl.multiple_of(pl.program_id(0) * wide, wide), wide)
     back = mixed(val_y[pl.program_id(0)], fold_h[0, 0], fold_l[0, 0])
     ky = wave[0, 0, 0:1, :]
     both = twofold(ky)
@@ -403,11 +457,10 @@
     high = halves(jnp.concatenate([-turn(part[3], ky), part[4]]))
 
     for g in range(groups):
-        here = slice(g * wide, (g + 1) * wide)
-        table = jnp.concatenate([far[here, : 3 * span], far[here, 3 * span :]])
-        sums = stacked(table, *low, wide)
-        slopes = stacked(table[:, : 2 * span], *high, wide)
-        sums = sums + double(modulus[0, g * LANES : (g + 1) * LANES, :]) * slopes
+        sums = stacked(far[g], *low, wide)
+        slopes = stacked(far[g, :, : 2 * span], *high, wide)
+        modulus = length(wave_x, ky, g)
+        sums = sums + double(modulus) * slopes
         for l in range(layers):
             scaled = sums * double(decay(modulus, gain, depth, l, g))
             val[l, g] = stacked(mix[g], *halves(scaled), wide)
@@ -422,7 +475,7 @@
             ]
             for a, value in enumerate(gather(pairs)):
                 here = pl.ds(a * LANES + at, STRIP)
-                grids[l][0][here, :], grids[l][1][here, :] = halves(value)
+                grids[l][0][here, column], grids[l][1][here, column] = halves(value)
             return carry
 
         lax.fori_loop(0, LANES // STRIP, strip, 0)
@@ -468,12 +521,12 @@
     cos_t = cos_t.reshape(side, groups, 1, LANES)
     sin_t = sin_t.reshape(side, groups, 1, LANES)
     full_y = np.concatenate([cos_t, -sin_t], axis=2).reshape(side, 2, side).transpose(1, 2, 0)
-    value = np.concatenate([cos_t, sin_t], axis=2).reshape(side, period)
-    slope = np.concatenate([-sin_t, cos_t], axis=2).reshape(side, period)
-    flat_wave = np.repeat((waves * unit)[:, None], 2, axis=1).reshape(1, period)
-    near = np.stack([value, flat_wave * slope, -(flat_wave**2) * value])
-    near = near.reshape(3, chips, span, period).transpose(1, 0, 2, 3).reshape(chips, 3 * span, period)
-    near = table_of(near, 1)
+    base = np.stack(angle_parts(np.arange(LANES), waves.reshape(-1), period))
+    base = jnp.asarray(base, jnp.float32)
+    rotate = np.zeros((groups, 16, side))
+    rotate[:, 0], rotate[:, 8] = angle_parts(np.arange(groups) * LANES, waves.reshape(-1), period)
+    rotate = jnp.asarray(rotate, jnp.float32)
+    line = jnp.asarray(np.broadcast_to((waves * unit).reshape(1, -1), (8, side)), jnp.float32)
 
     low_cells = np.arange(LANES)
     mix = np.zeros((groups, 2 * LANES, 2 * LANES))
@@ -498,12 +551,11 @@
     slab = np.where(modulus > 0, -np.expm1(-modulus) / np.maximum(modulus, 0.001), 1.0)
     twice = np.where(waves == 0, 1.0, 2.0)
     gain = slab * (twice.reshape(1, -1, 1) * twice.reshape(2, 1, -1) / (period * period))
-    modulus, gain = jnp.asarray(modulus), jnp.asarray(gain, jnp.float32)
+    gain = jnp.asarray(gain, jnp.float32)
+    wave_x = jnp.asarray(np.broadcast_to(flat_x[0], (side, LANES)), jnp.float32)
     wave = np.broadcast_to((waves * unit).reshape(2, own, 1, LANES), (2, own, 8, LANES))
     wave = jnp.asarray(wave, jnp.float32)
 
-    active_cells = active.astype(jnp.float32)
-    masked = density * active_cells[None]
     far_seen = lax.ppermute(observed, "tile", pair)
 
     def const(shape):
@@ -512,10 +564,9 @@
     def lanes(shape):
         return pl.BlockSpec(shape, lambda g, *_: (0,) * (len(shape) - 1) + (g,))
 
-    def by_core(shape):
-        return pl.BlockSpec(shape, lambda g, p: (p[0],) + (0,) * (len(shape) - 1))
-
-    def call(kernel, grid, in_specs, out_specs, out_shape, scratch, aliases={}):
+    held = pl.BlockSpec(memory_space=pltpu.VMEM)
+
+    def call(kernel, grid, in_specs, out_specs, out_shape, scratch, aliases={}, mib=20):
         return pl.pallas_call(
             kernel,
             grid_spec=pltpu.PrefetchScalarGridSpec(
@@ -528,54 +579,75 @@
             out_shape=out_shape,
             input_output_aliases=aliases,
             compiler_params=pltpu.CompilerParams(
-                dimension_semantics=("arbitrary",), vmem_limit_bytes=56 * 1024 * 1024
+                dimension_semantics=("arbitrary",), vmem_limit_bytes=mib * 1024 * 1024
             ),
         )
 
-    def chip_block(shape, layer, offset):
-        return pl.BlockSpec(shape, lambda g, p: (p[2 + 2 * offset + layer], 0))
-
-    far = call(
-        transpose_kernel,
+    masked = density * active.astype(jnp.float32)[None]
+    near, far = call(
+        near_kernel,
         1,
-        [pl.BlockSpec((1, 6 * span, period), lambda g, p: (p[1], 0, 0))],
-        const((period, 6 * span)),
-        jax.ShapeDtypeStruct((period, 6 * span), jnp.bfloat16),
+        [held] * 3,
+        [held] * 2,
+        [
+            jax.ShapeDtypeStruct((6 * span, period), jnp.bfloat16),
+            jax.ShapeDtypeStruct((groups, 2 * wide, 3 * span), jnp.bfloat16),
+        ],
         [],
-    )(index, near)
+        mib=4,
+    )(index, base, rotate, line)
 
     if chips <= 8:
-        done = []
-        fore, rear = masked[0], masked[1]
-        for step in range(chips):
+        chains = [masked[0], masked[1]]
+        ways = (ahead, back)
+        shapes = [jax.ShapeDtypeStruct((side, side), jnp.float32)] * 2
+        shapes.append(jax.ShapeDtypeStruct((2 * rows, side), jnp.float32))
+
+        def transformed(step, chains, far, spec):
+            args = [index, *chains, *mix_yf]
+            kernel, aliases = rows_first, {}
             if step:
-                if step >= 2:
-                    fore, rear, done[step - 2] = lax.optimization_barrier(
-                        (fore, rear, done[step - 2])
-                    )
-                if step == 3:
-                    fore, rear, far_seen, far = lax.optimization_barrier(
-                        (fore, rear, far_seen, far)
-                    )
-                fore = lax.ppermute(fore, "tile", ahead)
-                rear = lax.ppermute(rear, "tile", back)
-            far_fore = lax.ppermute(fore, "tile", pair)
-            far_rear = lax.ppermute(rear, "tile", pair)
-            args = [index, fore, rear, far_fore, far_rear, *mix_yf]
-            in_specs = [const((rows, side))] * 4 + [by_core((1,) + mix_y.shape[1:])] * 2
-            if step:
-                args += done[-1]
-                in_specs += [pl.BlockSpec(memory_space=pl.ANY)] * 2
-            spec = call(
-                functools.partial(rows_kernel, step > 0),
+                kernel = rows_apart if far is None else rows_next
+                kernel = functools.partial(kernel, step)
+                args += [*([] if far is None else [far]), *spec]
+                aliases = {len(args) - 2: 0, len(args) - 1: 1}
+            *spec, give = call(
+                kernel,
                 1,
-                in_specs,
-                [chip_block((span, side), l, step) for l in (0, 1)],
-                [jax.ShapeDtypeStruct((side, side), jnp.float32)] * 2,
-                [pltpu.VMEM((own, 4 * span, wide), jnp.bfloat16)],
-                {7: 0, 8: 1} if step else {},
+                [held] * (len(args) - 1),
+                [held] * 3,
+                shapes,
+                [pltpu.VMEM((groups, 2 * span, wide), jnp.bfloat16)],
+                aliases,
+                mib=4,
             )(*args)
-            done.append(spec)
+            return spec, give
+
+        spec = give = other = None
+        for step in range(1, chips):
+            if step >= 2:
+                *chains, give = lax.optimization_barrier((*chains, give))
+            came = [lax.ppermute(chains[l], "tile", ways[l]) for l in (0, 1)]
+            if step >= 2:
+                other = lax.ppermute(give, "tile", pair)
+            if step == 4:
+                other, near, far, far_seen = lax.optimization_barrier(
+                    (other, near, far, far_seen)
+                )
+            spec, give = transformed(step - 1, chains, other, spec)
+            chains = came
+        other = lax.ppermute(give, "tile", pair)
+        spec, give = transformed(chips - 1, chains, None, spec)
+        spec = call(
+            functools.partial(rows_last, chips - 1),
+            1,
+            [held] * 4,
+            [held] * 2,
+            shapes[:2],
+            [],
+            {3: 0, 4: 1},
+            mib=4,
+        )(index, other, lax.ppermute(give, "tile", pair), *spec)
     else:
         whole = lax.all_gather(masked, "tile", axis=1, tiled=True)
         table_y = lax.dynamic_index_in_dim(jnp.asarray(full_y, jnp.float32), core, 0, False)
@@ -584,9 +656,9 @@
 
     shared = [
         pl.BlockSpec((1, side, LANES), lambda g, p: (p[0], 0, g)),
-        pl.BlockSpec((1, side, LANES), lambda g, p: (p[0], 0, g)),
+        held,
         pl.BlockSpec((1, 1, 8, LANES), lambda g, p: (p[0], g, 0, 0)),
-        const(mix_f.shape),
+        held,
     ]
     group_spec = pl.BlockSpec((1, 1, wide, wide), lambda g, p: (p[0], g, 0, 0))
     smem = pl.BlockSpec(memory_space=pltpu.SMEM)
@@ -594,28 +666,27 @@
         forward_kernel,
         own,
         [smem]
-        + [lanes((side, wide))] * 2
+        + [held] * 2
         + shared
-        + [pl.BlockSpec((1, 6 * span, period), lambda g, p: (p[1], 0, 0))]
+        + [held]
         + [group_spec] * 2,
-        const((5 * span, side)),
+        held,
         jax.ShapeDtypeStruct((5 * span, side), jnp.float32),
         [pltpu.VMEM((layers, groups, wide, wide), jnp.bfloat16)] * 2
         + [pltpu.VMEM((period, wide), jnp.bfloat16)] * 4
         + [pltpu.VMEM((own, 5 * span, wide), jnp.float32)],
-    )(index, layer_depth, *spec, gain, modulus, wave, mix_f, near, *mix_yb)
+    )(index, layer_depth, *spec, gain, wave_x, wave, mix_f, near, *mix_yb)
 
     other = lax.ppermute(partial, "tile", pair)
     predicted, *grids = call(
         adjoint_kernel,
         own,
         [smem]
-        + [const((5 * span, side))] * 2
-        + [const((6, rows, side))] * 2
+        + [held] * 4
         + shared
-        + [const((period, 6 * span))]
+        + [held]
         + [group_spec] * 2,
-        [const((6, rows, side))] + [lanes((side, wide))] * 4,
+        [const((6, rows, side))] + [held] * 4,
         [jax.ShapeDtypeStruct((6, rows, side), jnp.float32)]
         + [jax.ShapeDtypeStruct((side, side), jnp.bfloat16)] * 4,
         [
@@ -624,42 +695,45 @@
             pltpu.VMEM((layers, groups, wide, wide), jnp.float32),
         ],
     )(
-        index, layer_depth, partial, other, observed, far_seen, gain, modulus, wave,
+        index, layer_depth, partial, other, observed, far_seen, gain, wave_x, wave,
         mix_b, far, *mix_yf,
     )
 
     if chips <= 8:
 
         def share(offset, grids):
-            keep, give = call(
-                strips_kernel,
+            out = call(
+                functools.partial(strips_kernel, 2 + 2 * offset),
                 1,
-                [chip_block((span, side), l, offset) for l in (0, 0, 1, 1)]
-                + [by_core((1,) + mix_y.shape[1:])] * 2,
-                [const((layers, rows, side))] * 2,
-                [jax.ShapeDtypeStruct((layers, rows, side), jnp.float32)] * 2,
+                [held] * 6,
+                [held] * 3,
+                [jax.ShapeDtypeStruct((rows, side), jnp.float32)] * 2
+                + [jax.ShapeDtypeStruct((2 * rows, side), jnp.float32)],
                 [pltpu.VMEM((own, 2 * span, wide), jnp.float32)],
+                mib=4,
             )(index, *grids, *mix_yb)
-            return keep, lax.ppermute(give, "tile", pair)
-
-        keep, give = share(1, grids)
-        now = [keep[l] + give[l] for l in (0, 1)]
+            return out[:2], lax.ppermute(out[2], "tile", pair)
+
+        def part(ready, l):
+            keep, give = ready
+            return keep[l] + give[l * rows : (l + 1) * rows]
+
+        ready = share(1, grids)
+        now = [part(ready, l) for l in (0, 1)]
         ready = share(2, grids)
         for step in range(1, chips):
-            keep, give = ready
+            current = ready
             if step < chips - 1:
-                now, grids = lax.optimization_barrier((now, grids))
+                now[1], grids = lax.optimization_barrier((now[1], grids))
                 ready = share(step + 2, grids)
-            fore = lax.ppermute(now[0], "tile", ahead)
-            rear = lax.ppermute(now[1], "tile", back)
-            now = [fore + (keep[0] + give[0]), rear + (keep[1] + give[1])]
+            now = [lax.ppermute(now[l], "tile", ways[l]) + part(current, l) for l in (0, 1)]
         gradient = jnp.stack(now)
     else:
         table_y = lax.dynamic_index_in_dim(jnp.asarray(full_y, jnp.float32), core, 0, False)
         strip = jnp.stack([h.astype(jnp.float32) + l for h, l in (grids[:2], grids[2:])])
         strip = lax.dot_general(strip, table_y, (((2,), (0,)), ((), ())), precision=HIGH)
         gradient = lax.psum_scatter(strip, "tile", scatter_dimension=1, tiled=True)
-    return (predicted, gradient * active_cells[None])
+    return (predicted, gradient * active.astype(jnp.float32)[None])
 
 
 def solution(mesh):

time: 234 us -> 207 us (0.88)
  Pallas kernels: 144 us -> 87.9 us
  waiting for transfers between devices: 35.1 us -> 76.1 us
  local copies, waits for them, and re-layouts: 13.3 us -> 6.04 us
  starting transfers between devices: 34.7 us -> 32.1 us
    pallas_call x19 -> x20, Pallas kernels: 144 us -> 87.9 us  [the longest x1 36.7 us: body(): call(adjoint_kernel, own, [smem] + [held] * 4 + shared + [held] + [group_...]
    ppermute x52 -> x44, waiting for transfers between devices: 30.4 us -> 71.3 us  [the longest x14 36.9 us: body(): came = [lax.ppermute(chains[l], 'tile', ways[l]) for l in (0, 1)]]
    unnamed x82 -> x32, local copies, waits for them, and re-layouts: 12 us -> 5.31 us
    ppermute x52 -> x44, starting transfers between devices: 33.7 us -> 31.4 us  [the longest x14 15.2 us: body(): came = [lax.ppermute(chains[l], 'tile', ways[l]) for l in (0, 1)]]
  transfers between devices with their start and end apart: 54 -> 46, of which waited for: 26 -> 32; matrix products, arithmetic and copies ran while one was open for 2% -> 1% of each run, Pallas kernels for 27% -> 10%
where the time goes in v1:
time: 207 us
  Pallas kernels  87.9 us (42%)
  waiting for transfers between devices  76.1 us (37%)
  starting transfers between devices  32.1 us (16%)
  local copies, waits for them, and re-layouts  6.04 us (3%)
  other arithmetic  3.85 us (2%)
    ppermute x14, waiting for transfers between devices, body(): came = [lax.ppermute(chains[l], 'tile', ways[l]) for l in (0, 1)]  36.9 us
    pallas_call x1, Pallas kernels, body(): call(adjoint_kernel, own, [smem] + [held] * 4 + shared + [held] + [group_...  36.7 us
    ppermute x14, waiting for transfers between devices, body(): lax.ppermute(now[l], 'tile', ways[l]) + part(current, l)  32.2 us
    pallas_call x1, Pallas kernels, body(): call(forward_kernel, own, [smem] + [held] * 2 + shared + [held] + [group_...  26.8 us
    ppermute x14, starting transfers between devices, body(): came = [lax.ppermute(chains[l], 'tile', ways[l]) for l in (0, 1)]  15.2 us
    ppermute x14, starting transfers between devices, body(): lax.ppermute(now[l], 'tile', ways[l]) + part(current, l)  14.5 us
    pallas_call x8, Pallas kernels, transformed(): call(kernel, 1, [held] * (len(args) - 1), [held] * 3, shapes, [pltpu.VMEM...  11.3 us
    pallas_call x8, Pallas kernels, share(): call(functools.partial(strips_kernel, 2 + 2 * offset), 1, [held] * 6, [he...  10.8 us
  transfers between devices with their start and end apart: 46, of which 32 were waited for; matrix products, arithmetic and copies ran while one was open for 1% of the time, Pallas kernels for 10%

profile of v1, /device:TPU:0, one launch (start us, length us, event | category | flops | bytes accessed | tf_op | source)
XLA Modules:
  0.0 207.0 jit_solution(11596899463255164074)
XLA Ops:
  2.9 3.1 %collective-permute-start = (f32[64,1024]{1,0:T(8,128)S(1)}, f32[64,1024]{1,0:T(8,128)S(1)}, u32[]{:S(2)}, u32[]{:S(2)}) collective-permute-start(f32[64,1024]{1,0:T(8,128)S(1)} %get-tuple-element.237.a), channel_id=1, source_target_pairs={{0,4},{1,5},{4,8},{5,9},{8,12},{9,13},{12,14},{13,15},{14,10},{15,... | collective-permute-start | bytes 786440 | tf_op jit(solution)/shard_map/ppermute | solution.py:630
  9.1 1.4 shard_map.176
  10.6 1.7 collective-permute-done.a
  12.2 1.5 collective-permute-done.1.b
  14.3 1.6 collective-permute-start.2
  16.4 1.4 shard_map.177
  17.8 4.7 %collective-permute-done.2.a = f32[64,1024]{1,0:T(8,128)S(1)} collective-permute-done((f32[64,1024]{1,0:T(8,128)S(1)}, f32[64,1024]{1,0:T(8,128)S(1)}, u32[]{:S(2)}, u32[]{:S(2)}) %collective-permute-start.2) | collective-permute-done | bytes 262176 | tf_op jit(solution)/shard_map/ppermute | solution.py:630
  23.8 1.6 collective-permute-start.5
  25.8 1.4 shard_map.178
  27.2 5.3 %collective-permute-done.5.a = f32[64,1024]{1,0:T(8,128)S(1)} collective-permute-done((f32[64,1024]{1,0:T(8,128)S(1)}, f32[64,1024]{1,0:T(8,128)S(1)}, u32[]{:S(2)}, u32[]{:S(2)}) %collective-permute-start.5) | collective-permute-done | bytes 262176 | tf_op jit(solution)/shard_map/ppermute | solution.py:630
  33.8 1.5 collective-permute-start.8
  35.8 1.6 shard_map.179
  37.5 1.4 shard_map.180
  38.9 3.6 %collective-permute-done.8.a = f32[64,1024]{1,0:T(8,128)S(1)} collective-permute-done((f32[64,1024]{1,0:T(8,128)S(1)}, f32[64,1024]{1,0:T(8,128)S(1)}, u32[]{:S(2)}, u32[]{:S(2)}) %collective-permute-start.8) | collective-permute-done | bytes 262176 | tf_op jit(solution)/shard_map/ppermute | solution.py:630
  44.2 1.6 collective-permute-start.13
  45.8 1.4 shard_map.181
  47.2 5.3 %collective-permute-done.12.a = f32[64,1024]{1,0:T(8,128)S(1)} collective-permute-done((f32[64,1024]{1,0:T(8,128)S(1)}, f32[64,1024]{1,0:T(8,128)S(1)}, u32[]{:S(2)}, u32[]{:S(2)}) %collective-permute-start.12) | collective-permute-done | bytes 262176 | tf_op jit(solution)/shard_map/ppermute | solution.py:630
  53.1 1.6 collective-permute-start.16
  54.7 1.4 shard_map.182
  56.1 5.3 %collective-permute-done.15.a = f32[64,1024]{1,0:T(8,128)S(1)} collective-permute-done((f32[64,1024]{1,0:T(8,128)S(1)}, f32[64,1024]{1,0:T(8,128)S(1)}, u32[]{:S(2)}, u32[]{:S(2)}) %collective-permute-start.15) | collective-permute-done | bytes 262176 | tf_op jit(solution)/shard_map/ppermute | solution.py:630
  62.0 1.6 collective-permute-start.21
  63.6 1.4 shard_map.183
  65.0 5.3 %collective-permute-done.20.a = f32[64,1024]{1,0:T(8,128)S(1)} collective-permute-done((f32[64,1024]{1,0:T(8,128)S(1)}, f32[64,1024]{1,0:T(8,128)S(1)}, u32[]{:S(2)}, u32[]{:S(2)}) %collective-permute-start.20) | collective-permute-done | bytes 262176 | tf_op jit(solution)/shard_map/ppermute | solution.py:630
  70.4 1.4 shard_map.184
  72.4 1.4 collective-permute-done.22.far
  78.0 26.8 %shard_map.186.field = f32[640,1024]{1,0:T(8,128)S(1)} custom-call(s32[20]{0:T(128)S(1)} %dynamic-slice_bitcast_fusion.place, f32[2]{0:T(128)S(1)} %copy-done.15, f32[1024,1024]{1,0:T(8,128)S(1)} %get-tuple-element.156.spec_a, f32[1024,1024]{1,0:T(8,128)S(1)} %get-tuple-element.157.spec_b, f32[2,1024,512]{2,1,0:T(8,128)S(1)} %copy-done.6, ...), custom_call_target="tpu_custom_call" | custom-call | tf_op jit(solution)/shard_map/pallas_call | solution.py:665
  105.1 4.8 %collective-permute-done.23.other = f32[640,1024]{1,0:T(8,128)S(1)} collective-permute-done((f32[640,1024]{1,0:T(8,128)S(1)}, f32[640,1024]{1,0:T(8,128)S(1)}, u32[]{:S(2)}, u32[]{:S(2)}) %collective-permute-start.23) | collective-permute-done | bytes 2621472 | tf_op jit(solution)/shard_map/ppermute | solution.py:680
  109.9 36.7 %shard_map.187 = (f32[6,64,1024]{2,1,0:T(8,128)}, bf16[1024,1024]{1,0:T(8,128)(2,1)S(1)}, bf16[1024,1024]{1,0:T(8,128)(2,1)S(1)}, bf16[1024,1024]{1,0:T(8,128)(2,1)S(1)}, bf16[1024,1024]{1,0:T(8,128)(2,1)S(1)}) custom-call(s32[20]{0:T(128)S(1)} %dynamic-slice_bitcast_fusion.place, f32[2]{0:T(128)S(1)} %copy-done.15, f32[640,1024]{1,0:T(8,128)S(1)} %shard_map.186.field, ...), custom_call_target="tpu_custom_call" | custom-call | tf_op jit(solution)/shard_map/pallas_call | solution.py:681
  146.6 1.3 shard_map.188
  148.1 1.5 shard_map.189
  150.2 1.6 collective-permute-start.30
  153.7 4.9 %collective-permute-done.30 = f32[64,1024]{1,0:T(8,128)S(1)} collective-permute-done((f32[64,1024]{1,0:T(8,128)S(1)}, f32[64,1024]{1,0:T(8,128)S(1)}, u32[]{:S(2)}, u32[]{:S(2)}) %collective-permute-start.30) | collective-permute-done | bytes 262176 | tf_op jit(solution)/shard_map/ppermute | solution.py:729
  160.0 1.6 collective-permute-start.33
  163.5 3.8 %collective-permute-done.33 = f32[64,1024]{1,0:T(8,128)S(1)} collective-permute-done((f32[64,1024]{1,0:T(8,128)S(1)}, f32[64,1024]{1,0:T(8,128)S(1)}, u32[]{:S(2)}, u32[]{:S(2)}) %collective-permute-start.33) | collective-permute-done | bytes 262176 | tf_op jit(solution)/shard_map/ppermute | solution.py:729
  168.6 1.6 collective-permute-start.36
  172.1 2.9 %collective-permute-done.36 = f32[64,1024]{1,0:T(8,128)S(1)} collective-permute-done((f32[64,1024]{1,0:T(8,128)S(1)}, f32[64,1024]{1,0:T(8,128)S(1)}, u32[]{:S(2)}, u32[]{:S(2)}) %collective-permute-start.36) | collective-permute-done | bytes 262176 | tf_op jit(solution)/shard_map/ppermute | solution.py:729
  175.0 1.6 collective-permute-done.29
  177.4 1.4 collective-permute-start.32
  178.8 1.3 shard_map.193
  180.2 2.9 %collective-permute-done.39 = f32[64,1024]{1,0:T(8,128)S(1)} collective-permute-done((f32[64,1024]{1,0:T(8,128)S(1)}, f32[64,1024]{1,0:T(8,128)S(1)}, u32[]{:S(2)}, u32[]{:S(2)}) %collective-permute-start.39) | collective-permute-done | bytes 262176 | tf_op jit(solution)/shard_map/ppermute | solution.py:729
  184.5 1.5 collective-permute-start.35
  187.4 2.9 %collective-permute-done.42 = f32[64,1024]{1,0:T(8,128)S(1)} collective-permute-done((f32[64,1024]{1,0:T(8,128)S(1)}, f32[64,1024]{1,0:T(8,128)S(1)}, u32[]{:S(2)}, u32[]{:S(2)}) %collective-permute-start.42) | collective-permute-done | bytes 262176 | tf_op jit(solution)/shard_map/ppermute | solution.py:729
  191.4 1.6 collective-permute-start.38
  193.0 1.3 shard_map.195
  194.4 2.9 %collective-permute-done.44 = f32[64,1024]{1,0:T(8,128)S(1)} collective-permute-done((f32[64,1024]{1,0:T(8,128)S(1)}, f32[64,1024]{1,0:T(8,128)S(1)}, u32[]{:S(2)}, u32[]{:S(2)}) %collective-permute-start.44) | collective-permute-done | bytes 262176 | tf_op jit(solution)/shard_map/ppermute | solution.py:729
  198.0 1.7 collective-permute-start.41
  200.0 4.3 %collective-permute-done.41 = f32[64,1024]{1,0:T(8,128)S(1)} collective-permute-done((f32[64,1024]{1,0:T(8,128)S(1)}, f32[64,1024]{1,0:T(8,128)S(1)}, u32[]{:S(2)}, u32[]{:S(2)}) %collective-permute-start.41) | collective-permute-done | bytes 262176 | tf_op jit(solution)/shard_map/ppermute | solution.py:729
  204.4 1.7 collective-permute-done.45
  (109 shorter events, 33.7 us)
Async XLA Ops:
  2.9 9.3 %collective-permute-start = (f32[64,1024]{1,0:T(8,128)S(1)}, f32[64,1024]{1,0:T(8,128)S(1)}, u32[]{:S(2)}, u32[]{:S(2)}) collective-permute-start(f32[64,1024]{1,0:T(8,128)S(1)} %get-tuple-element.237.a), channel_id=1, source_target_pairs={{0,4},{1,5},{4,8},{5,9},{8,12},{9,13},{12,14},{13,15},{14,10},{15,... | collective-permute-start | bytes 786440 | tf_op jit(solution)/shard_map/ppermute | solution.py:630
  6.0 7.8 %collective-permute-start.1 = (f32[64,1024]{1,0:T(8,128)S(1)}, f32[64,1024]{1,0:T(8,128)S(1)}, u32[]{:S(2)}, u32[]{:S(2)}) collective-permute-start(f32[64,1024]{1,0:T(8,128)S(1)} %get-tuple-element.236.b), channel_id=1, source_target_pairs={{0,2},{1,3},{4,0},{5,1},{8,4},{9,5},{12,8},{13,9},{14,12},{15,13},... | collective-permute-start | bytes 786440 | tf_op jit(solution)/shard_map/ppermute | solution.py:630
  13.8 2.6 %collective-permute-start.4 = (f32[128,1024]{1,0:T(8,128)S(1)}, f32[128,1024]{1,0:T(8,128)S(1)}, u32[]{:S(2)}, u32[]{:S(2)}) collective-permute-start(f32[128,1024]{1,0:T(8,128)S(1)} %get-tuple-element.114), channel_id=1, source_target_pairs={{0,1},{1,0},{2,3},{3,2},{4,5},{5,4},{6,7},{7,6},{8,9},{9,8},{10,11... | collective-permute-start | bytes 1572872 | tf_op jit(solution)/shard_map/ppermute | solution.py:632
  13.8 23.7 %collective-permute-start.11 = (f32[6,64,1024]{2,1,0:T(8,128)}, f32[6,64,1024]{2,1,0:T(8,128)S(1)}, u32[]{:S(2)}, u32[]{:S(2)}) collective-permute-start(f32[6,64,1024]{2,1,0:T(8,128)} %seen.1), channel_id=1, source_target_pairs={{0,1},{1,0},{2,3},{3,2},{4,5},{5,4},{6,7},{7,6},{8,9},{9,8},{10,11... | collective-permute-start | bytes 4718600 | tf_op jit(solution)/shard_map/ppermute | solution.py:559
  14.3 8.2 %collective-permute-start.2 = (f32[64,1024]{1,0:T(8,128)S(1)}, f32[64,1024]{1,0:T(8,128)S(1)}, u32[]{:S(2)}, u32[]{:S(2)}) collective-permute-start(f32[64,1024]{1,0:T(8,128)S(1)} %collective-permute-done.a), channel_id=1, source_target_pairs={{0,4},{1,5},{4,8},{5,9},{8,12},{9,13},{12,14},{13,15},{14,10},{15,... | collective-permute-start | bytes 786440 | tf_op jit(solution)/shard_map/ppermute | solution.py:630
  15.9 7.9 %collective-permute-start.3 = (f32[64,1024]{1,0:T(8,128)S(1)}, f32[64,1024]{1,0:T(8,128)S(1)}, u32[]{:S(2)}, u32[]{:S(2)}) collective-permute-start(f32[64,1024]{1,0:T(8,128)S(1)} %collective-permute-done.1.b), channel_id=1, source_target_pairs={{0,2},{1,3},{4,0},{5,1},{8,4},{9,5},{12,8},{13,9},{14,12},{15,13},... | collective-permute-start | bytes 786440 | tf_op jit(solution)/shard_map/ppermute | solution.py:630
  23.8 2.0 collective-permute-start.7
  23.8 8.7 %collective-permute-start.5 = (f32[64,1024]{1,0:T(8,128)S(1)}, f32[64,1024]{1,0:T(8,128)S(1)}, u32[]{:S(2)}, u32[]{:S(2)}) collective-permute-start(f32[64,1024]{1,0:T(8,128)S(1)} %collective-permute-done.2.a), channel_id=1, source_target_pairs={{0,4},{1,5},{4,8},{5,9},{8,12},{9,13},{12,14},{13,15},{14,10},{15,... | collective-permute-start | bytes 786440 | tf_op jit(solution)/shard_map/ppermute | solution.py:630
  25.4 8.4 %collective-permute-start.6 = (f32[64,1024]{1,0:T(8,128)S(1)}, f32[64,1024]{1,0:T(8,128)S(1)}, u32[]{:S(2)}, u32[]{:S(2)}) collective-permute-start(f32[64,1024]{1,0:T(8,128)S(1)} %collective-permute-done.3.b), channel_id=1, source_target_pairs={{0,2},{1,3},{4,0},{5,1},{8,4},{9,5},{12,8},{13,9},{14,12},{15,13},... | collective-permute-start | bytes 786440 | tf_op jit(solution)/shard_map/ppermute | solution.py:630
  33.8 3.7 %collective-permute-start.10 = (f32[128,1024]{1,0:T(8,128)S(1)}, f32[128,1024]{1,0:T(8,128)S(1)}, u32[]{:S(2)}, u32[]{:S(2)}) collective-permute-start(f32[128,1024]{1,0:T(8,128)S(1)} %get-tuple-element.126), channel_id=1, source_target_pairs={{0,1},{1,0},{2,3},{3,2},{4,5},{5,4},{6,7},{7,6},{8,9},{9,8},{10,11... | collective-permute-start | bytes 1572872 | tf_op jit(solution)/shard_map/ppermute | solution.py:632
  33.8 8.7 %collective-permute-start.8 = (f32[64,1024]{1,0:T(8,128)S(1)}, f32[64,1024]{1,0:T(8,128)S(1)}, u32[]{:S(2)}, u32[]{:S(2)}) collective-permute-start(f32[64,1024]{1,0:T(8,128)S(1)} %collective-permute-done.5.a), channel_id=1, source_target_pairs={{0,4},{1,5},{4,8},{5,9},{8,12},{9,13},{12,14},{13,15},{14,10},{15,... | collective-permute-start | bytes 786440 | tf_op jit(solution)/shard_map/ppermute | solution.py:630
  35.3 8.4 %collective-permute-start.9 = (f32[64,1024]{1,0:T(8,128)S(1)}, f32[64,1024]{1,0:T(8,128)S(1)}, u32[]{:S(2)}, u32[]{:S(2)}) collective-permute-start(f32[64,1024]{1,0:T(8,128)S(1)} %collective-permute-done.6.b), channel_id=1, source_target_pairs={{0,2},{1,3},{4,0},{5,1},{8,4},{9,5},{12,8},{13,9},{14,12},{15,13},... | collective-permute-start | bytes 786440 | tf_op jit(solution)/shard_map/ppermute | solution.py:630
  43.7 2.0 collective-permute-start.14
  43.7 8.7 %collective-permute-start.12 = (f32[64,1024]{1,0:T(8,128)S(1)}, f32[64,1024]{1,0:T(8,128)S(1)}, u32[]{:S(2)}, u32[]{:S(2)}) collective-permute-start(f32[64,1024]{1,0:T(8,128)S(1)} %collective-permute-done.8.a), channel_id=1, source_target_pairs={{0,4},{1,5},{4,8},{5,9},{8,12},{9,13},{12,14},{13,15},{14,10},{15,... | collective-permute-start | bytes 786440 | tf_op jit(solution)/shard_map/ppermute | solution.py:630
  44.2 8.4 %collective-permute-start.13 = (f32[64,1024]{1,0:T(8,128)S(1)}, f32[64,1024]{1,0:T(8,128)S(1)}, u32[]{:S(2)}, u32[]{:S(2)}) collective-permute-start(f32[64,1024]{1,0:T(8,128)S(1)} %collective-permute-done.9.b), channel_id=1, source_target_pairs={{0,2},{1,3},{4,0},{5,1},{8,4},{9,5},{12,8},{13,9},{14,12},{15,13},... | collective-permute-start | bytes 786440 | tf_op jit(solution)/shard_map/ppermute | solution.py:630
  52.6 2.0 collective-permute-start.17
  52.6 8.7 %collective-permute-start.15 = (f32[64,1024]{1,0:T(8,128)S(1)}, f32[64,1024]{1,0:T(8,128)S(1)}, u32[]{:S(2)}, u32[]{:S(2)}) collective-permute-start(f32[64,1024]{1,0:T(8,128)S(1)} %collective-permute-done.12.a), channel_id=1, source_target_pairs={{0,4},{1,5},{4,8},{5,9},{8,12},{9,13},{12,14},{13,15},{14,10},{15,... | collective-permute-start | bytes 786440 | tf_op jit(solution)/shard_map/ppermute | solution.py:630
  53.1 8.4 %collective-permute-start.16 = (f32[64,1024]{1,0:T(8,128)S(1)}, f32[64,1024]{1,0:T(8,128)S(1)}, u32[]{:S(2)}, u32[]{:S(2)}) collective-permute-start(f32[64,1024]{1,0:T(8,128)S(1)} %collective-permute-done.13.b), channel_id=1, source_target_pairs={{0,2},{1,3},{4,0},{5,1},{8,4},{9,5},{12,8},{13,9},{14,12},{15,13},... | collective-permute-start | bytes 786440 | tf_op jit(solution)/shard_map/ppermute | solution.py:630
  61.5 2.0 collective-permute-start.18
  61.5 8.7 %collective-permute-start.20 = (f32[64,1024]{1,0:T(8,128)S(1)}, f32[64,1024]{1,0:T(8,128)S(1)}, u32[]{:S(2)}, u32[]{:S(2)}) collective-permute-start(f32[64,1024]{1,0:T(8,128)S(1)} %collective-permute-done.15.a), channel_id=1, source_target_pairs={{0,4},{1,5},{4,8},{5,9},{8,12},{9,13},{12,14},{13,15},{14,10},{15,... | collective-permute-start | bytes 786440 | tf_op jit(solution)/shard_map/ppermute | solution.py:630
  62.0 8.4 %collective-permute-start.21 = (f32[64,1024]{1,0:T(8,128)S(1)}, f32[64,1024]{1,0:T(8,128)S(1)}, u32[]{:S(2)}, u32[]{:S(2)}) collective-permute-start(f32[64,1024]{1,0:T(8,128)S(1)} %collective-permute-done.16.b), channel_id=1, source_target_pairs={{0,2},{1,3},{4,0},{5,1},{8,4},{9,5},{12,8},{13,9},{14,12},{15,13},... | collective-permute-start | bytes 786440 | tf_op jit(solution)/shard_map/ppermute | solution.py:630
  71.8 2.0 collective-permute-start.22
  71.9 2.6 %collective-permute-start.19 = (f32[128,1024]{1,0:T(8,128)S(1)}, f32[128,1024]{1,0:T(8,128)S(1)}, u32[]{:S(2)}, u32[]{:S(2)}) collective-permute-start(f32[128,1024]{1,0:T(8,128)S(1)} %get-tuple-element.150), channel_id=1, source_target_pairs={{0,1},{1,0},{2,3},{3,2},{4,5},{5,4},{6,7},{7,6},{8,9},{9,8},{10,11... | collective-permute-start | bytes 1572872 | tf_op jit(solution)/shard_map/ppermute | solution.py:639
  78.0 31.8 %copy-start.7 = (bf16[8,512,256]{2,1,0:T(8,128)(2,1)S(1)}, bf16[8,512,256]{2,1,0:T(8,128)(2,1)}, u32[]{:S(2)}) copy-start(bf16[8,512,256]{2,1,0:T(8,128)(2,1)} %constant.41.clone.mix) | copy-start | bytes 6291460
  78.0 31.8 %copy-start.10 = (f32[6,64,1024]{2,1,0:T(8,128)S(1)}, f32[6,64,1024]{2,1,0:T(8,128)}, u32[]{:S(2)}) copy-start(f32[6,64,1024]{2,1,0:T(8,128)} %seen.1) | copy-start | bytes 4718596
  104.9 5.0 %collective-permute-start.23 = (f32[640,1024]{1,0:T(8,128)S(1)}, f32[640,1024]{1,0:T(8,128)S(1)}, u32[]{:S(2)}, u32[]{:S(2)}) collective-permute-start(f32[640,1024]{1,0:T(8,128)S(1)} %shard_map.186.field), channel_id=1, source_target_pairs={{0,1},{1,0},{2,3},{3,2},{4,5},{5,4},{6,7},{7,6},{8,9},{9,8},{10,11... | collective-permute-start | bytes 7864328 | tf_op jit(solution)/shard_map/ppermute | solution.py:680
  147.9 2.2 %collective-permute-start.24 = (f32[128,1024]{1,0:T(8,128)S(1)}, f32[128,1024]{1,0:T(8,128)S(1)}, u32[]{:S(2)}, u32[]{:S(2)}) collective-permute-start(f32[128,1024]{1,0:T(8,128)S(1)} %get-tuple-element.167), channel_id=1, source_target_pairs={{0,1},{1,0},{2,3},{3,2},{4,5},{5,4},{6,7},{7,6},{8,9},{9,8},{10,11... | collective-permute-start | bytes 1572872 | tf_op jit(solution)/shard_map/ppermute | solution.py:715
  149.7 4.0 %collective-permute-start.26 = (f32[128,1024]{1,0:T(8,128)S(1)}, f32[128,1024]{1,0:T(8,128)S(1)}, u32[]{:S(2)}, u32[]{:S(2)}) collective-permute-start(f32[128,1024]{1,0:T(8,128)S(1)} %get-tuple-element.169), channel_id=1, source_target_pairs={{0,1},{1,0},{2,3},{3,2},{4,5},{5,4},{6,7},{7,6},{8,9},{9,8},{10,11... | collective-permute-start | bytes 1572872 | tf_op jit(solution)/shard_map/ppermute | solution.py:715
  150.2 8.4 %collective-permute-start.30 = (f32[64,1024]{1,0:T(8,128)S(1)}, f32[64,1024]{1,0:T(8,128)S(1)}, u32[]{:S(2)}, u32[]{:S(2)}) collective-permute-start(f32[64,1024]{1,0:T(8,128)S(1)} %get-tuple-element.177), channel_id=1, source_target_pairs={{0,2},{1,3},{4,0},{5,1},{8,4},{9,5},{12,8},{13,9},{14,12},{15,13},... | collective-permute-start | bytes 786440 | tf_op jit(solution)/shard_map/ppermute | solution.py:729
  151.8 8.1 %collective-permute-start.25 = (f32[64,1024]{1,0:T(8,128)S(1)}, f32[64,1024]{1,0:T(8,128)S(1)}, u32[]{:S(2)}, u32[]{:S(2)}) collective-permute-start(f32[64,1024]{1,0:T(8,128)S(1)} %get-tuple-element.234), channel_id=1, source_target_pairs={{0,4},{1,5},{4,8},{5,9},{8,12},{9,13},{12,14},{13,15},{14,10},{15,... | collective-permute-start | bytes 786440 | tf_op jit(solution)/shard_map/ppermute | solution.py:729
  153.6 13.6 %collective-permute-start.28 = (f32[128,1024]{1,0:T(8,128)S(1)}, f32[128,1024]{1,0:T(8,128)S(1)}, u32[]{:S(2)}, u32[]{:S(2)}) collective-permute-start(f32[128,1024]{1,0:T(8,128)S(1)} %get-tuple-element.176), channel_id=1, source_target_pairs={{0,1},{1,0},{2,3},{3,2},{4,5},{5,4},{6,7},{7,6},{8,9},{9,8},{10,11... | collective-permute-start | bytes 1572872 | tf_op jit(solution)/shard_map/ppermute | solution.py:715
  160.0 7.2 %collective-permute-start.33 = (f32[64,1024]{1,0:T(8,128)S(1)}, f32[64,1024]{1,0:T(8,128)S(1)}, u32[]{:S(2)}, u32[]{:S(2)}) collective-permute-start(f32[64,1024]{1,0:T(8,128)S(1)} %get-tuple-element.185), channel_id=1, source_target_pairs={{0,2},{1,3},{4,0},{5,1},{8,4},{9,5},{12,8},{13,9},{14,12},{15,13},... | collective-permute-start | bytes 786440 | tf_op jit(solution)/shard_map/ppermute | solution.py:729
  161.6 6.9 %collective-permute-start.27 = (f32[64,1024]{1,0:T(8,128)S(1)}, f32[64,1024]{1,0:T(8,128)S(1)}, u32[]{:S(2)}, u32[]{:S(2)}) collective-permute-start(f32[64,1024]{1,0:T(8,128)S(1)} %get-tuple-element.232), channel_id=1, source_target_pairs={{0,4},{1,5},{4,8},{5,9},{8,12},{9,13},{12,14},{13,15},{14,10},{15,... | collective-permute-start | bytes 786440 | tf_op jit(solution)/shard_map/ppermute | solution.py:729
  163.4 11.7 %collective-permute-start.31 = (f32[128,1024]{1,0:T(8,128)S(1)}, f32[128,1024]{1,0:T(8,128)S(1)}, u32[]{:S(2)}, u32[]{:S(2)}) collective-permute-start(f32[128,1024]{1,0:T(8,128)S(1)} %get-tuple-element.184), channel_id=1, source_target_pairs={{0,1},{1,0},{2,3},{3,2},{4,5},{5,4},{6,7},{7,6},{8,9},{9,8},{10,11... | collective-permute-start | bytes 1572872 | tf_op jit(solution)/shard_map/ppermute | solution.py:715
  168.6 6.4 %collective-permute-start.36 = (f32[64,1024]{1,0:T(8,128)S(1)}, f32[64,1024]{1,0:T(8,128)S(1)}, u32[]{:S(2)}, u32[]{:S(2)}) collective-permute-start(f32[64,1024]{1,0:T(8,128)S(1)} %get-tuple-element.193), channel_id=1, source_target_pairs={{0,2},{1,3},{4,0},{5,1},{8,4},{9,5},{12,8},{13,9},{14,12},{15,13},... | collective-permute-start | bytes 786440 | tf_op jit(solution)/shard_map/ppermute | solution.py:729
  170.3 6.4 %collective-permute-start.29 = (f32[64,1024]{1,0:T(8,128)S(1)}, f32[64,1024]{1,0:T(8,128)S(1)}, u32[]{:S(2)}, u32[]{:S(2)}) collective-permute-start(f32[64,1024]{1,0:T(8,128)S(1)} %get-tuple-element.230), channel_id=1, source_target_pairs={{0,4},{1,5},{4,8},{5,9},{8,12},{9,13},{12,14},{13,15},{14,10},{15,... | collective-permute-start | bytes 786440 | tf_op jit(solution)/shard_map/ppermute | solution.py:729
  172.0 11.1 %collective-permute-start.34 = (f32[128,1024]{1,0:T(8,128)S(1)}, f32[128,1024]{1,0:T(8,128)S(1)}, u32[]{:S(2)}, u32[]{:S(2)}) collective-permute-start(f32[128,1024]{1,0:T(8,128)S(1)} %get-tuple-element.192), channel_id=1, source_target_pairs={{0,1},{1,0},{2,3},{3,2},{4,5},{5,4},{6,7},{7,6},{8,9},{9,8},{10,11... | collective-permute-start | bytes 1572872 | tf_op jit(solution)/shard_map/ppermute | solution.py:715
  176.7 6.4 %collective-permute-start.39 = (f32[64,1024]{1,0:T(8,128)S(1)}, f32[64,1024]{1,0:T(8,128)S(1)}, u32[]{:S(2)}, u32[]{:S(2)}) collective-permute-start(f32[64,1024]{1,0:T(8,128)S(1)} %get-tuple-element.201), channel_id=1, source_target_pairs={{0,2},{1,3},{4,0},{5,1},{8,4},{9,5},{12,8},{13,9},{14,12},{15,13},... | collective-permute-start | bytes 786440 | tf_op jit(solution)/shard_map/ppermute | solution.py:729
  177.4 6.4 %collective-permute-start.32 = (f32[64,1024]{1,0:T(8,128)S(1)}, f32[64,1024]{1,0:T(8,128)S(1)}, u32[]{:S(2)}, u32[]{:S(2)}) collective-permute-start(f32[64,1024]{1,0:T(8,128)S(1)} %get-tuple-element.228), channel_id=1, source_target_pairs={{0,4},{1,5},{4,8},{5,9},{8,12},{9,13},{12,14},{13,15},{14,10},{15,... | collective-permute-start | bytes 786440 | tf_op jit(solution)/shard_map/ppermute | solution.py:729
  180.1 10.2 %collective-permute-start.37 = (f32[128,1024]{1,0:T(8,128)S(1)}, f32[128,1024]{1,0:T(8,128)S(1)}, u32[]{:S(2)}, u32[]{:S(2)}) collective-permute-start(f32[128,1024]{1,0:T(8,128)S(1)} %get-tuple-element.200), channel_id=1, source_target_pairs={{0,1},{1,0},{2,3},{3,2},{4,5},{5,4},{6,7},{7,6},{8,9},{9,8},{10,11... | collective-permute-start | bytes 1572872 | tf_op jit(solution)/shard_map/ppermute | solution.py:715
  183.9 6.4 %collective-permute-start.42 = (f32[64,1024]{1,0:T(8,128)S(1)}, f32[64,1024]{1,0:T(8,128)S(1)}, u32[]{:S(2)}, u32[]{:S(2)}) collective-permute-start(f32[64,1024]{1,0:T(8,128)S(1)} %get-tuple-element.209), channel_id=1, source_target_pairs={{0,2},{1,3},{4,0},{5,1},{8,4},{9,5},{12,8},{13,9},{14,12},{15,13},... | collective-permute-start | bytes 786440 | tf_op jit(solution)/shard_map/ppermute | solution.py:729
  184.5 6.4 %collective-permute-start.35 = (f32[64,1024]{1,0:T(8,128)S(1)}, f32[64,1024]{1,0:T(8,128)S(1)}, u32[]{:S(2)}, u32[]{:S(2)}) collective-permute-start(f32[64,1024]{1,0:T(8,128)S(1)} %get-tuple-element.226), channel_id=1, source_target_pairs={{0,4},{1,5},{4,8},{5,9},{8,12},{9,13},{12,14},{13,15},{14,10},{15,... | collective-permute-start | bytes 786440 | tf_op jit(solution)/shard_map/ppermute | solution.py:729
  187.3 10.1 %collective-permute-start.40 = (f32[128,1024]{1,0:T(8,128)S(1)}, f32[128,1024]{1,0:T(8,128)S(1)}, u32[]{:S(2)}, u32[]{:S(2)}) collective-permute-start(f32[128,1024]{1,0:T(8,128)S(1)} %get-tuple-element.208), channel_id=1, source_target_pairs={{0,1},{1,0},{2,3},{3,2},{4,5},{5,4},{6,7},{7,6},{8,9},{9,8},{10,11... | collective-permute-start | bytes 1572872 | tf_op jit(solution)/shard_map/ppermute | solution.py:715
  190.9 6.4 %collective-permute-start.44 = (f32[64,1024]{1,0:T(8,128)S(1)}, f32[64,1024]{1,0:T(8,128)S(1)}, u32[]{:S(2)}, u32[]{:S(2)}) collective-permute-start(f32[64,1024]{1,0:T(8,128)S(1)} %get-tuple-element.217), channel_id=1, source_target_pairs={{0,2},{1,3},{4,0},{5,1},{8,4},{9,5},{12,8},{13,9},{14,12},{15,13},... | collective-permute-start | bytes 786440 | tf_op jit(solution)/shard_map/ppermute | solution.py:729
  191.4 6.4 %collective-permute-start.38 = (f32[64,1024]{1,0:T(8,128)S(1)}, f32[64,1024]{1,0:T(8,128)S(1)}, u32[]{:S(2)}, u32[]{:S(2)}) collective-permute-start(f32[64,1024]{1,0:T(8,128)S(1)} %get-tuple-element.224), channel_id=1, source_target_pairs={{0,4},{1,5},{4,8},{5,9},{8,12},{9,13},{12,14},{13,15},{14,10},{15,... | collective-permute-start | bytes 786440 | tf_op jit(solution)/shard_map/ppermute | solution.py:729
  194.3 5.7 %collective-permute-start.43 = (f32[128,1024]{1,0:T(8,128)S(1)}, f32[128,1024]{1,0:T(8,128)S(1)}, u32[]{:S(2)}, u32[]{:S(2)}) collective-permute-start(f32[128,1024]{1,0:T(8,128)S(1)} %get-tuple-element.216), channel_id=1, source_target_pairs={{0,1},{1,0},{2,3},{3,2},{4,5},{5,4},{6,7},{7,6},{8,9},{9,8},{10,11... | collective-permute-start | bytes 1572872 | tf_op jit(solution)/shard_map/ppermute | solution.py:715
  198.0 6.4 %collective-permute-start.41 = (f32[64,1024]{1,0:T(8,128)S(1)}, f32[64,1024]{1,0:T(8,128)S(1)}, u32[]{:S(2)}, u32[]{:S(2)}) collective-permute-start(f32[64,1024]{1,0:T(8,128)S(1)} %get-tuple-element.222), channel_id=1, source_target_pairs={{0,4},{1,5},{4,8},{5,9},{8,12},{9,13},{12,14},{13,15},{14,10},{15,... | collective-permute-start | bytes 786440 | tf_op jit(solution)/shard_map/ppermute | solution.py:729
  199.7 6.4 %collective-permute-start.45 = (f32[64,1024]{1,0:T(8,128)S(1)}, f32[64,1024]{1,0:T(8,128)S(1)}, u32[]{:S(2)}, u32[]{:S(2)}) collective-permute-start(f32[64,1024]{1,0:T(8,128)S(1)} %get-tuple-element.223), channel_id=1, source_target_pairs={{0,2},{1,3},{4,0},{5,1},{8,4},{9,5},{12,8},{13,9},{14,12},{15,13},... | collective-permute-start | bytes 786440 | tf_op jit(solution)/shard_map/ppermute | solution.py:729
  (14 other events, 83.4 us)

commit v2 on v1

--- a/solution.py
+++ b/solution.py
@@ -185,7 +185,8 @@
 
 
 def decay(modulus, gain, depth, l, g):
-    return jnp.exp(-modulus * depth[l]) * gain[0, g * LANES : (g + 1) * LANES, :]
+    lane = pl.ds(pl.multiple_of(pl.program_id(0) * LANES, LANES), LANES)
+    return jnp.exp(-modulus * depth[l]) * gain[g * LANES : (g + 1) * LANES, lane]
 
 
 def on_core(place, run):
@@ -320,7 +321,7 @@
                 val_l[l, g, pl.ds(LANES + at, STRIP), :] = low
             return carry
 
-        lax.fori_loop(0, LANES // STRIP, strip, 0)
+        lax.fori_loop(0, LANES // STRIP, strip, 0, unroll=True)
 
     ky = wave[0, 0, 0:1, :]
     for g in range(groups):
@@ -365,13 +366,15 @@
         on_core(place, run)
 
 
-def near_kernel(place, base, rotate, wave, near, far):
+def near_kernel(place, base, rotate, wave, gains, near, far, gain):
     span = near.shape[0] // 6
     start = place[1] * span
     first = pl.multiple_of(lax.rem(start, LANES), STRIP)
     rows = pl.ds(first, span)
     block = lax.div(start, LANES)
-    for g in range(far.shape[0]):
+    groups = rotate.shape[0]
+    gain[...] = gains[place[0]]
+    for g in range(groups):
         lane = slice(g * LANES, (g + 1) * LANES)
         both = slice(2 * g * LANES, 2 * (g + 1) * LANES)
         cos_b, sin_b = base[0, rows, lane], base[1, rows, lane]
@@ -384,12 +387,12 @@
         bend = -twofold(k * k) * value
         for n, half in enumerate(halves(jnp.concatenate([value, slope, bend]))):
             near[n * 3 * span : (n + 1) * 3 * span, both] = half
-            far[g, n * 2 * LANES : (n + 1) * 2 * LANES, :] = half.T
+            far[pl.ds((n * groups + g) * 2 * LANES, 2 * LANES), :] = half.T
 
 
 def adjoint_kernel(
     place, depth, field, other, seen, far_seen, gain, wave_x, wave, mix, far, fold_h, fold_l,
-    predicted, high_a, low_a, high_b, low_b, left, val_y, val,
+    predicted, high_a, low_a, high_b, low_b, left, val_y, val, sums_all, slopes_all,
 ):
     grids = ((high_a, low_a), (high_b, low_b))
     layers = len(grids)
@@ -456,11 +459,12 @@
     low = halves(jnp.concatenate([both * both * part[0], -turn(part[1], ky), -part[2]]))
     high = halves(jnp.concatenate([-turn(part[3], ky), part[4]]))
 
+    sums_all[...] = stacked(far[...], *low, groups * wide)
+    slopes_all[...] = stacked(far[:, : 2 * span], *high, groups * wide)
     for g in range(groups):
-        sums = stacked(far[g], *low, wide)
-        slopes = stacked(far[g, :, : 2 * span], *high, wide)
+        here = slice(g * wide, (g + 1) * wide)
         modulus = length(wave_x, ky, g)
-        sums = sums + double(modulus) * slopes
+        sums = sums_all[here, :] + double(modulus) * slopes_all[here, :]
         for l in range(layers):
             scaled = sums * double(decay(modulus, gain, depth, l, g))
             val[l, g] = stacked(mix[g], *halves(scaled), wide)
@@ -478,7 +482,7 @@
                 grids[l][0][here, column], grids[l][1][here, column] = halves(value)
             return carry
 
-        lax.fori_loop(0, LANES // STRIP, strip, 0)
+        lax.fori_loop(0, LANES // STRIP, strip, 0, unroll=True)
 
 
 def body(density, observed, active, layer_depth):
@@ -584,18 +588,19 @@
         )
 
     masked = density * active.astype(jnp.float32)[None]
-    near, far = call(
+    near, far, gain = call(
         near_kernel,
         1,
+        [held] * 4,
         [held] * 3,
-        [held] * 2,
         [
             jax.ShapeDtypeStruct((6 * span, period), jnp.bfloat16),
-            jax.ShapeDtypeStruct((groups, 2 * wide, 3 * span), jnp.bfloat16),
+            jax.ShapeDtypeStruct((2 * period, 3 * span), jnp.bfloat16),
+            jax.ShapeDtypeStruct((side, side // 2), jnp.float32),
         ],
         [],
         mib=4,
-    )(index, base, rotate, line)
+    )(index, base, rotate, line, gain)
 
     if chips <= 8:
         chains = [masked[0], masked[1]]
@@ -631,8 +636,8 @@
             if step >= 2:
                 other = lax.ppermute(give, "tile", pair)
             if step == 4:
-                other, near, far, far_seen = lax.optimization_barrier(
-                    (other, near, far, far_seen)
+                other, near, far, gain, far_seen = lax.optimization_barrier(
+                    (other, near, far, gain, far_seen)
                 )
             spec, give = transformed(step - 1, chains, other, spec)
             chains = came
@@ -655,7 +660,7 @@
         spec = [spec[0], spec[1]]
 
     shared = [
-        pl.BlockSpec((1, side, LANES), lambda g, p: (p[0], 0, g)),
+        held,
         held,
         pl.BlockSpec((1, 1, 8, LANES), lambda g, p: (p[0], g, 0, 0)),
         held,
@@ -693,7 +698,10 @@
             pltpu.VMEM((5 * span, side), jnp.float32),
             pltpu.VMEM((own, 10 * span, wide), jnp.bfloat16),
             pltpu.VMEM((layers, groups, wide, wide), jnp.float32),
+            pltpu.VMEM((period, wide), jnp.float32),
+            pltpu.VMEM((period, wide), jnp.float32),
         ],
+        mib=26,
     )(
         index, layer_depth, partial, other, observed, far_seen, gain, wave_x, wave,
         mix_b, far, *mix_yf,

time: 207 us -> 198 us (0.957)
  Pallas kernels: 87.9 us -> 79.8 us
    pallas_call x1, Pallas kernels: 36.7 us -> 31.2 us  [body(): call(adjoint_kernel, own, [smem] + [held] * 4 + shared + [held] + [group_...]
    pallas_call x1, Pallas kernels: 26.8 us -> 24.1 us  [body(): call(forward_kernel, own, [smem] + [held] * 2 + shared + [held] + [group_...]
  transfers between devices with their start and end apart: 46 -> 46, of which waited for: 32 -> 32; matrix products, arithmetic and copies ran while one was open for 1% -> 1% of each run, Pallas kernels for 10% -> 11%
where the time goes in v2:
time: 198 us
  Pallas kernels  79.8 us (40%)
  waiting for transfers between devices  76 us (38%)
  starting transfers between devices  32.1 us (16%)
  local copies, waits for them, and re-layouts  4.88 us (2%)
  other arithmetic  3.87 us (2%)
    ppermute x14, waiting for transfers between devices, body(): came = [lax.ppermute(chains[l], 'tile', ways[l]) for l in (0, 1)]  36.7 us
    ppermute x14, waiting for transfers between devices, body(): lax.ppermute(now[l], 'tile', ways[l]) + part(current, l)  32.2 us
    pallas_call x1, Pallas kernels, body(): call(adjoint_kernel, own, [smem] + [held] * 4 + shared + [held] + [group_...  31.2 us
    pallas_call x1, Pallas kernels, body(): call(forward_kernel, own, [smem] + [held] * 2 + shared + [held] + [group_...  24.1 us
    ppermute x14, starting transfers between devices, body(): came = [lax.ppermute(chains[l], 'tile', ways[l]) for l in (0, 1)]  15.2 us
    ppermute x14, starting transfers between devices, body(): lax.ppermute(now[l], 'tile', ways[l]) + part(current, l)  14.5 us
    pallas_call x8, Pallas kernels, transformed(): call(kernel, 1, [held] * (len(args) - 1), [held] * 3, shapes, [pltpu.VMEM...  11.3 us
    pallas_call x8, Pallas kernels, share(): call(functools.partial(strips_kernel, 2 + 2 * offset), 1, [held] * 6, [he...  10.8 us
  transfers between devices with their start and end apart: 46, of which 32 were waited for; matrix products, arithmetic and copies ran while one was open for 1% of the time, Pallas kernels for 11%

profile of v2, /device:TPU:0, one launch (start us, length us, event | category | flops | bytes accessed | tf_op | source)
XLA Modules:
  0.0 197.7 jit_solution(15062063923442173753)
XLA Ops:
  2.9 3.1 %collective-permute-start = (f32[64,1024]{1,0:T(8,128)S(1)}, f32[64,1024]{1,0:T(8,128)S(1)}, u32[]{:S(2)}, u32[]{:S(2)}) collective-permute-start(f32[64,1024]{1,0:T(8,128)S(1)} %get-tuple-element.241.a), channel_id=1, source_target_pairs={{0,4},{1,5},{4,8},{5,9},{8,12},{9,13},{12,14},{13,15},{14,10},{15,... | collective-permute-start | bytes 786440 | tf_op jit(solution)/shard_map/ppermute | solution.py:635
  9.1 1.4 shard_map.176
  10.6 1.7 collective-permute-done.a
  12.2 1.5 collective-permute-done.1.b
  14.3 1.6 collective-permute-start.2
  16.4 1.4 shard_map.177
  17.8 4.7 %collective-permute-done.2.a = f32[64,1024]{1,0:T(8,128)S(1)} collective-permute-done((f32[64,1024]{1,0:T(8,128)S(1)}, f32[64,1024]{1,0:T(8,128)S(1)}, u32[]{:S(2)}, u32[]{:S(2)}) %collective-permute-start.2) | collective-permute-done | bytes 262176 | tf_op jit(solution)/shard_map/ppermute | solution.py:635
  23.8 1.6 collective-permute-start.5
  25.8 1.4 shard_map.178
  27.3 5.2 %collective-permute-done.5.a = f32[64,1024]{1,0:T(8,128)S(1)} collective-permute-done((f32[64,1024]{1,0:T(8,128)S(1)}, f32[64,1024]{1,0:T(8,128)S(1)}, u32[]{:S(2)}, u32[]{:S(2)}) %collective-permute-start.5) | collective-permute-done | bytes 262176 | tf_op jit(solution)/shard_map/ppermute | solution.py:635
  33.8 1.5 collective-permute-start.8
  35.8 1.7 shard_map.179
  37.6 1.4 shard_map.180
  39.0 3.5 %collective-permute-done.8.a = f32[64,1024]{1,0:T(8,128)S(1)} collective-permute-done((f32[64,1024]{1,0:T(8,128)S(1)}, f32[64,1024]{1,0:T(8,128)S(1)}, u32[]{:S(2)}, u32[]{:S(2)}) %collective-permute-start.8) | collective-permute-done | bytes 262176 | tf_op jit(solution)/shard_map/ppermute | solution.py:635
  44.2 1.6 collective-permute-start.13
  45.8 1.4 shard_map.181
  47.2 5.3 %collective-permute-done.12.a = f32[64,1024]{1,0:T(8,128)S(1)} collective-permute-done((f32[64,1024]{1,0:T(8,128)S(1)}, f32[64,1024]{1,0:T(8,128)S(1)}, u32[]{:S(2)}, u32[]{:S(2)}) %collective-permute-start.12) | collective-permute-done | bytes 262176 | tf_op jit(solution)/shard_map/ppermute | solution.py:635
  53.1 1.6 collective-permute-start.16
  54.7 1.4 shard_map.182
  56.1 5.3 %collective-permute-done.15.a = f32[64,1024]{1,0:T(8,128)S(1)} collective-permute-done((f32[64,1024]{1,0:T(8,128)S(1)}, f32[64,1024]{1,0:T(8,128)S(1)}, u32[]{:S(2)}, u32[]{:S(2)}) %collective-permute-start.15) | collective-permute-done | bytes 262176 | tf_op jit(solution)/shard_map/ppermute | solution.py:635
  62.0 1.6 collective-permute-start.21
  63.6 1.4 shard_map.183
  65.0 5.3 %collective-permute-done.20.a = f32[64,1024]{1,0:T(8,128)S(1)} collective-permute-done((f32[64,1024]{1,0:T(8,128)S(1)}, f32[64,1024]{1,0:T(8,128)S(1)}, u32[]{:S(2)}, u32[]{:S(2)}) %collective-permute-start.20) | collective-permute-done | bytes 262176 | tf_op jit(solution)/shard_map/ppermute | solution.py:635
  70.4 1.4 shard_map.184
  72.4 1.4 collective-permute-done.22.far
  76.9 24.1 %shard_map.186.field = f32[640,1024]{1,0:T(8,128)S(1)} custom-call(s32[20]{0:T(128)S(1)} %dynamic-slice_bitcast_fusion.place, f32[2]{0:T(128)S(1)} %copy-done.15, f32[1024,1024]{1,0:T(8,128)S(1)} %get-tuple-element.159.spec_a, f32[1024,1024]{1,0:T(8,128)S(1)} %get-tuple-element.160.spec_b, f32[1024,512]{1,0:T(8,128)S(1)} %get-tuple-element.161.gain, ...), custom_call_target="tpu_custom_call" | custom-call | tf_op jit(solution)/shard_map/pallas_call | solution.py:670
  101.2 4.8 %collective-permute-done.23.other = f32[640,1024]{1,0:T(8,128)S(1)} collective-permute-done((f32[640,1024]{1,0:T(8,128)S(1)}, f32[640,1024]{1,0:T(8,128)S(1)}, u32[]{:S(2)}, u32[]{:S(2)}) %collective-permute-start.23) | collective-permute-done | bytes 2621472 | tf_op jit(solution)/shard_map/ppermute | solution.py:685
  106.0 31.2 %shard_map.187 = (f32[6,64,1024]{2,1,0:T(8,128)}, bf16[1024,1024]{1,0:T(8,128)(2,1)S(1)}, bf16[1024,1024]{1,0:T(8,128)(2,1)S(1)}, bf16[1024,1024]{1,0:T(8,128)(2,1)S(1)}, bf16[1024,1024]{1,0:T(8,128)(2,1)S(1)}) custom-call(s32[20]{0:T(128)S(1)} %dynamic-slice_bitcast_fusion.place, f32[2]{0:T(128)S(1)} %copy-done.15, f32[640,1024]{1,0:T(8,128)S(1)} %shard_map.186.field, ...), custom_call_target="tpu_custom_call" | custom-call | tf_op jit(solution)/shard_map/pallas_call | solution.py:686
  137.2 1.5 shard_map.188
  139.0 1.3 shard_map.189
  140.8 1.6 collective-permute-start.30
  144.3 4.9 %collective-permute-done.30 = f32[64,1024]{1,0:T(8,128)S(1)} collective-permute-done((f32[64,1024]{1,0:T(8,128)S(1)}, f32[64,1024]{1,0:T(8,128)S(1)}, u32[]{:S(2)}, u32[]{:S(2)}) %collective-permute-start.30) | collective-permute-done | bytes 262176 | tf_op jit(solution)/shard_map/ppermute | solution.py:737
  150.6 1.6 collective-permute-start.33
  154.1 3.8 %collective-permute-done.33 = f32[64,1024]{1,0:T(8,128)S(1)} collective-permute-done((f32[64,1024]{1,0:T(8,128)S(1)}, f32[64,1024]{1,0:T(8,128)S(1)}, u32[]{:S(2)}, u32[]{:S(2)}) %collective-permute-start.33) | collective-permute-done | bytes 262176 | tf_op jit(solution)/shard_map/ppermute | solution.py:737
  159.3 1.6 collective-permute-start.36
  161.3 1.3 shard_map.192
  162.8 2.9 %collective-permute-done.36 = f32[64,1024]{1,0:T(8,128)S(1)} collective-permute-done((f32[64,1024]{1,0:T(8,128)S(1)}, f32[64,1024]{1,0:T(8,128)S(1)}, u32[]{:S(2)}, u32[]{:S(2)}) %collective-permute-start.36) | collective-permute-done | bytes 262176 | tf_op jit(solution)/shard_map/ppermute | solution.py:737
  165.7 1.6 collective-permute-done.29
  168.0 1.4 collective-permute-start.32
  170.9 2.9 %collective-permute-done.39 = f32[64,1024]{1,0:T(8,128)S(1)} collective-permute-done((f32[64,1024]{1,0:T(8,128)S(1)}, f32[64,1024]{1,0:T(8,128)S(1)}, u32[]{:S(2)}, u32[]{:S(2)}) %collective-permute-start.39) | collective-permute-done | bytes 262176 | tf_op jit(solution)/shard_map/ppermute | solution.py:737
  175.1 1.5 collective-permute-start.35
  178.0 2.9 %collective-permute-done.42 = f32[64,1024]{1,0:T(8,128)S(1)} collective-permute-done((f32[64,1024]{1,0:T(8,128)S(1)}, f32[64,1024]{1,0:T(8,128)S(1)}, u32[]{:S(2)}, u32[]{:S(2)}) %collective-permute-start.42) | collective-permute-done | bytes 262176 | tf_op jit(solution)/shard_map/ppermute | solution.py:737
  182.1 1.6 collective-permute-start.38
  183.7 1.3 shard_map.195
  185.1 2.9 %collective-permute-done.44 = f32[64,1024]{1,0:T(8,128)S(1)} collective-permute-done((f32[64,1024]{1,0:T(8,128)S(1)}, f32[64,1024]{1,0:T(8,128)S(1)}, u32[]{:S(2)}, u32[]{:S(2)}) %collective-permute-start.44) | collective-permute-done | bytes 262176 | tf_op jit(solution)/shard_map/ppermute | solution.py:737
  188.6 1.7 collective-permute-start.41
  190.7 4.3 %collective-permute-done.41 = f32[64,1024]{1,0:T(8,128)S(1)} collective-permute-done((f32[64,1024]{1,0:T(8,128)S(1)}, f32[64,1024]{1,0:T(8,128)S(1)}, u32[]{:S(2)}, u32[]{:S(2)}) %collective-permute-start.41) | collective-permute-done | bytes 262176 | tf_op jit(solution)/shard_map/ppermute | solution.py:737
  195.1 1.7 collective-permute-done.45
  (109 shorter events, 32.7 us)
Async XLA Ops:
  2.9 9.3 %collective-permute-start = (f32[64,1024]{1,0:T(8,128)S(1)}, f32[64,1024]{1,0:T(8,128)S(1)}, u32[]{:S(2)}, u32[]{:S(2)}) collective-permute-start(f32[64,1024]{1,0:T(8,128)S(1)} %get-tuple-element.241.a), channel_id=1, source_target_pairs={{0,4},{1,5},{4,8},{5,9},{8,12},{9,13},{12,14},{13,15},{14,10},{15,... | collective-permute-start | bytes 786440 | tf_op jit(solution)/shard_map/ppermute | solution.py:635
  6.0 7.8 %collective-permute-start.1 = (f32[64,1024]{1,0:T(8,128)S(1)}, f32[64,1024]{1,0:T(8,128)S(1)}, u32[]{:S(2)}, u32[]{:S(2)}) collective-permute-start(f32[64,1024]{1,0:T(8,128)S(1)} %get-tuple-element.240.b), channel_id=1, source_target_pairs={{0,2},{1,3},{4,0},{5,1},{8,4},{9,5},{12,8},{13,9},{14,12},{15,13},... | collective-permute-start | bytes 786440 | tf_op jit(solution)/shard_map/ppermute | solution.py:635
  13.8 2.6 %collective-permute-start.4 = (f32[128,1024]{1,0:T(8,128)S(1)}, f32[128,1024]{1,0:T(8,128)S(1)}, u32[]{:S(2)}, u32[]{:S(2)}) collective-permute-start(f32[128,1024]{1,0:T(8,128)S(1)} %get-tuple-element.116), channel_id=1, source_target_pairs={{0,1},{1,0},{2,3},{3,2},{4,5},{5,4},{6,7},{7,6},{8,9},{9,8},{10,11... | collective-permute-start | bytes 1572872 | tf_op jit(solution)/shard_map/ppermute | solution.py:637
  13.8 23.8 %collective-permute-start.11 = (f32[6,64,1024]{2,1,0:T(8,128)}, f32[6,64,1024]{2,1,0:T(8,128)S(1)}, u32[]{:S(2)}, u32[]{:S(2)}) collective-permute-start(f32[6,64,1024]{2,1,0:T(8,128)} %seen.1), channel_id=1, source_target_pairs={{0,1},{1,0},{2,3},{3,2},{4,5},{5,4},{6,7},{7,6},{8,9},{9,8},{10,11... | collective-permute-start | bytes 4718600 | tf_op jit(solution)/shard_map/ppermute | solution.py:563
  14.3 8.2 %collective-permute-start.2 = (f32[64,1024]{1,0:T(8,128)S(1)}, f32[64,1024]{1,0:T(8,128)S(1)}, u32[]{:S(2)}, u32[]{:S(2)}) collective-permute-start(f32[64,1024]{1,0:T(8,128)S(1)} %collective-permute-done.a), channel_id=1, source_target_pairs={{0,4},{1,5},{4,8},{5,9},{8,12},{9,13},{12,14},{13,15},{14,10},{15,... | collective-permute-start | bytes 786440 | tf_op jit(solution)/shard_map/ppermute | solution.py:635
  15.9 7.9 %collective-permute-start.3 = (f32[64,1024]{1,0:T(8,128)S(1)}, f32[64,1024]{1,0:T(8,128)S(1)}, u32[]{:S(2)}, u32[]{:S(2)}) collective-permute-start(f32[64,1024]{1,0:T(8,128)S(1)} %collective-permute-done.1.b), channel_id=1, source_target_pairs={{0,2},{1,3},{4,0},{5,1},{8,4},{9,5},{12,8},{13,9},{14,12},{15,13},... | collective-permute-start | bytes 786440 | tf_op jit(solution)/shard_map/ppermute | solution.py:635
  23.8 2.0 %collective-permute-start.7 = (f32[128,1024]{1,0:T(8,128)S(1)}, f32[128,1024]{1,0:T(8,128)S(1)}, u32[]{:S(2)}, u32[]{:S(2)}) collective-permute-start(f32[128,1024]{1,0:T(8,128)S(1)} %get-tuple-element.122), channel_id=1, source_target_pairs={{0,1},{1,0},{2,3},{3,2},{4,5},{5,4},{6,7},{7,6},{8,9},{9,8},{10,11... | collective-permute-start | bytes 1572872 | tf_op jit(solution)/shard_map/ppermute | solution.py:637
  23.8 8.7 %collective-permute-start.5 = (f32[64,1024]{1,0:T(8,128)S(1)}, f32[64,1024]{1,0:T(8,128)S(1)}, u32[]{:S(2)}, u32[]{:S(2)}) collective-permute-start(f32[64,1024]{1,0:T(8,128)S(1)} %collective-permute-done.2.a), channel_id=1, source_target_pairs={{0,4},{1,5},{4,8},{5,9},{8,12},{9,13},{12,14},{13,15},{14,10},{15,... | collective-permute-start | bytes 786440 | tf_op jit(solution)/shard_map/ppermute | solution.py:635
  25.4 8.4 %collective-permute-start.6 = (f32[64,1024]{1,0:T(8,128)S(1)}, f32[64,1024]{1,0:T(8,128)S(1)}, u32[]{:S(2)}, u32[]{:S(2)}) collective-permute-start(f32[64,1024]{1,0:T(8,128)S(1)} %collective-permute-done.3.b), channel_id=1, source_target_pairs={{0,2},{1,3},{4,0},{5,1},{8,4},{9,5},{12,8},{13,9},{14,12},{15,13},... | collective-permute-start | bytes 786440 | tf_op jit(solution)/shard_map/ppermute | solution.py:635
  33.8 3.8 %collective-permute-start.10 = (f32[128,1024]{1,0:T(8,128)S(1)}, f32[128,1024]{1,0:T(8,128)S(1)}, u32[]{:S(2)}, u32[]{:S(2)}) collective-permute-start(f32[128,1024]{1,0:T(8,128)S(1)} %get-tuple-element.128), channel_id=1, source_target_pairs={{0,1},{1,0},{2,3},{3,2},{4,5},{5,4},{6,7},{7,6},{8,9},{9,8},{10,11... | collective-permute-start | bytes 1572872 | tf_op jit(solution)/shard_map/ppermute | solution.py:637
  33.8 8.7 %collective-permute-start.8 = (f32[64,1024]{1,0:T(8,128)S(1)}, f32[64,1024]{1,0:T(8,128)S(1)}, u32[]{:S(2)}, u32[]{:S(2)}) collective-permute-start(f32[64,1024]{1,0:T(8,128)S(1)} %collective-permute-done.5.a), channel_id=1, source_target_pairs={{0,4},{1,5},{4,8},{5,9},{8,12},{9,13},{12,14},{13,15},{14,10},{15,... | collective-permute-start | bytes 786440 | tf_op jit(solution)/shard_map/ppermute | solution.py:635
  35.3 8.4 %collective-permute-start.9 = (f32[64,1024]{1,0:T(8,128)S(1)}, f32[64,1024]{1,0:T(8,128)S(1)}, u32[]{:S(2)}, u32[]{:S(2)}) collective-permute-start(f32[64,1024]{1,0:T(8,128)S(1)} %collective-permute-done.6.b), channel_id=1, source_target_pairs={{0,2},{1,3},{4,0},{5,1},{8,4},{9,5},{12,8},{13,9},{14,12},{15,13},... | collective-permute-start | bytes 786440 | tf_op jit(solution)/shard_map/ppermute | solution.py:635
  43.7 2.0 %collective-permute-start.14 = (f32[128,1024]{1,0:T(8,128)S(1)}, f32[128,1024]{1,0:T(8,128)S(1)}, u32[]{:S(2)}, u32[]{:S(2)}) collective-permute-start(f32[128,1024]{1,0:T(8,128)S(1)} %get-tuple-element.138), channel_id=1, source_target_pairs={{0,1},{1,0},{2,3},{3,2},{4,5},{5,4},{6,7},{7,6},{8,9},{9,8},{10,11... | collective-permute-start | bytes 1572872 | tf_op jit(solution)/shard_map/ppermute | solution.py:637
  43.7 8.7 %collective-permute-start.12 = (f32[64,1024]{1,0:T(8,128)S(1)}, f32[64,1024]{1,0:T(8,128)S(1)}, u32[]{:S(2)}, u32[]{:S(2)}) collective-permute-start(f32[64,1024]{1,0:T(8,128)S(1)} %collective-permute-done.8.a), channel_id=1, source_target_pairs={{0,4},{1,5},{4,8},{5,9},{8,12},{9,13},{12,14},{13,15},{14,10},{15,... | collective-permute-start | bytes 786440 | tf_op jit(solution)/shard_map/ppermute | solution.py:635
  44.2 8.4 %collective-permute-start.13 = (f32[64,1024]{1,0:T(8,128)S(1)}, f32[64,1024]{1,0:T(8,128)S(1)}, u32[]{:S(2)}, u32[]{:S(2)}) collective-permute-start(f32[64,1024]{1,0:T(8,128)S(1)} %collective-permute-done.9.b), channel_id=1, source_target_pairs={{0,2},{1,3},{4,0},{5,1},{8,4},{9,5},{12,8},{13,9},{14,12},{15,13},... | collective-permute-start | bytes 786440 | tf_op jit(solution)/shard_map/ppermute | solution.py:635
  52.6 2.0 %collective-permute-start.17 = (f32[128,1024]{1,0:T(8,128)S(1)}, f32[128,1024]{1,0:T(8,128)S(1)}, u32[]{:S(2)}, u32[]{:S(2)}) collective-permute-start(f32[128,1024]{1,0:T(8,128)S(1)} %get-tuple-element.144), channel_id=1, source_target_pairs={{0,1},{1,0},{2,3},{3,2},{4,5},{5,4},{6,7},{7,6},{8,9},{9,8},{10,11... | collective-permute-start | bytes 1572872 | tf_op jit(solution)/shard_map/ppermute | solution.py:637
  52.6 8.7 %collective-permute-start.15 = (f32[64,1024]{1,0:T(8,128)S(1)}, f32[64,1024]{1,0:T(8,128)S(1)}, u32[]{:S(2)}, u32[]{:S(2)}) collective-permute-start(f32[64,1024]{1,0:T(8,128)S(1)} %collective-permute-done.12.a), channel_id=1, source_target_pairs={{0,4},{1,5},{4,8},{5,9},{8,12},{9,13},{12,14},{13,15},{14,10},{15,... | collective-permute-start | bytes 786440 | tf_op jit(solution)/shard_map/ppermute | solution.py:635
  53.1 8.4 %collective-permute-start.16 = (f32[64,1024]{1,0:T(8,128)S(1)}, f32[64,1024]{1,0:T(8,128)S(1)}, u32[]{:S(2)}, u32[]{:S(2)}) collective-permute-start(f32[64,1024]{1,0:T(8,128)S(1)} %collective-permute-done.13.b), channel_id=1, source_target_pairs={{0,2},{1,3},{4,0},{5,1},{8,4},{9,5},{12,8},{13,9},{14,12},{15,13},... | collective-permute-start | bytes 786440 | tf_op jit(solution)/shard_map/ppermute | solution.py:635
  61.5 2.0 %collective-permute-start.18 = (f32[128,1024]{1,0:T(8,128)S(1)}, f32[128,1024]{1,0:T(8,128)S(1)}, u32[]{:S(2)}, u32[]{:S(2)}) collective-permute-start(f32[128,1024]{1,0:T(8,128)S(1)} %get-tuple-element.150), channel_id=1, source_target_pairs={{0,1},{1,0},{2,3},{3,2},{4,5},{5,4},{6,7},{7,6},{8,9},{9,8},{10,11... | collective-permute-start | bytes 1572872 | tf_op jit(solution)/shard_map/ppermute | solution.py:637
  61.5 8.7 %collective-permute-start.20 = (f32[64,1024]{1,0:T(8,128)S(1)}, f32[64,1024]{1,0:T(8,128)S(1)}, u32[]{:S(2)}, u32[]{:S(2)}) collective-permute-start(f32[64,1024]{1,0:T(8,128)S(1)} %collective-permute-done.15.a), channel_id=1, source_target_pairs={{0,4},{1,5},{4,8},{5,9},{8,12},{9,13},{12,14},{13,15},{14,10},{15,... | collective-permute-start | bytes 786440 | tf_op jit(solution)/shard_map/ppermute | solution.py:635
  62.0 8.4 %collective-permute-start.21 = (f32[64,1024]{1,0:T(8,128)S(1)}, f32[64,1024]{1,0:T(8,128)S(1)}, u32[]{:S(2)}, u32[]{:S(2)}) collective-permute-start(f32[64,1024]{1,0:T(8,128)S(1)} %collective-permute-done.16.b), channel_id=1, source_target_pairs={{0,2},{1,3},{4,0},{5,1},{8,4},{9,5},{12,8},{13,9},{14,12},{15,13},... | collective-permute-start | bytes 786440 | tf_op jit(solution)/shard_map/ppermute | solution.py:635
  71.8 2.0 collective-permute-start.22
  71.9 2.6 %collective-permute-start.19 = (f32[128,1024]{1,0:T(8,128)S(1)}, f32[128,1024]{1,0:T(8,128)S(1)}, u32[]{:S(2)}, u32[]{:S(2)}) collective-permute-start(f32[128,1024]{1,0:T(8,128)S(1)} %get-tuple-element.153), channel_id=1, source_target_pairs={{0,1},{1,0},{2,3},{3,2},{4,5},{5,4},{6,7},{7,6},{8,9},{9,8},{10,11... | collective-permute-start | bytes 1572872 | tf_op jit(solution)/shard_map/ppermute | solution.py:644
  76.9 29.1 %copy-start.7 = (bf16[8,512,256]{2,1,0:T(8,128)(2,1)S(1)}, bf16[8,512,256]{2,1,0:T(8,128)(2,1)}, u32[]{:S(2)}) copy-start(bf16[8,512,256]{2,1,0:T(8,128)(2,1)} %constant.41.clone.mix) | copy-start | bytes 6291460
  76.9 29.1 %copy-start.10 = (f32[6,64,1024]{2,1,0:T(8,128)S(1)}, f32[6,64,1024]{2,1,0:T(8,128)}, u32[]{:S(2)}) copy-start(f32[6,64,1024]{2,1,0:T(8,128)} %seen.1) | copy-start | bytes 4718596
  101.0 5.0 %collective-permute-start.23 = (f32[640,1024]{1,0:T(8,128)S(1)}, f32[640,1024]{1,0:T(8,128)S(1)}, u32[]{:S(2)}, u32[]{:S(2)}) collective-permute-start(f32[640,1024]{1,0:T(8,128)S(1)} %shard_map.186.field), channel_id=1, source_target_pairs={{0,1},{1,0},{2,3},{3,2},{4,5},{5,4},{6,7},{7,6},{8,9},{9,8},{10,11... | collective-permute-start | bytes 7864328 | tf_op jit(solution)/shard_map/ppermute | solution.py:685
  138.8 2.0 %collective-permute-start.24 = (f32[128,1024]{1,0:T(8,128)S(1)}, f32[128,1024]{1,0:T(8,128)S(1)}, u32[]{:S(2)}, u32[]{:S(2)}) collective-permute-start(f32[128,1024]{1,0:T(8,128)S(1)} %get-tuple-element.171), channel_id=1, source_target_pairs={{0,1},{1,0},{2,3},{3,2},{4,5},{5,4},{6,7},{7,6},{8,9},{9,8},{10,11... | collective-permute-start | bytes 1572872 | tf_op jit(solution)/shard_map/ppermute | solution.py:723
  140.3 4.0 %collective-permute-start.26 = (f32[128,1024]{1,0:T(8,128)S(1)}, f32[128,1024]{1,0:T(8,128)S(1)}, u32[]{:S(2)}, u32[]{:S(2)}) collective-permute-start(f32[128,1024]{1,0:T(8,128)S(1)} %get-tuple-element.173), channel_id=1, source_target_pairs={{0,1},{1,0},{2,3},{3,2},{4,5},{5,4},{6,7},{7,6},{8,9},{9,8},{10,11... | collective-permute-start | bytes 1572872 | tf_op jit(solution)/shard_map/ppermute | solution.py:723
  140.8 8.4 %collective-permute-start.30 = (f32[64,1024]{1,0:T(8,128)S(1)}, f32[64,1024]{1,0:T(8,128)S(1)}, u32[]{:S(2)}, u32[]{:S(2)}) collective-permute-start(f32[64,1024]{1,0:T(8,128)S(1)} %get-tuple-element.181), channel_id=1, source_target_pairs={{0,2},{1,3},{4,0},{5,1},{8,4},{9,5},{12,8},{13,9},{14,12},{15,13},... | collective-permute-start | bytes 786440 | tf_op jit(solution)/shard_map/ppermute | solution.py:737
  142.4 8.1 %collective-permute-start.25 = (f32[64,1024]{1,0:T(8,128)S(1)}, f32[64,1024]{1,0:T(8,128)S(1)}, u32[]{:S(2)}, u32[]{:S(2)}) collective-permute-start(f32[64,1024]{1,0:T(8,128)S(1)} %get-tuple-element.238), channel_id=1, source_target_pairs={{0,4},{1,5},{4,8},{5,9},{8,12},{9,13},{12,14},{13,15},{14,10},{15,... | collective-permute-start | bytes 786440 | tf_op jit(solution)/shard_map/ppermute | solution.py:737
  144.2 13.6 %collective-permute-start.28 = (f32[128,1024]{1,0:T(8,128)S(1)}, f32[128,1024]{1,0:T(8,128)S(1)}, u32[]{:S(2)}, u32[]{:S(2)}) collective-permute-start(f32[128,1024]{1,0:T(8,128)S(1)} %get-tuple-element.180), channel_id=1, source_target_pairs={{0,1},{1,0},{2,3},{3,2},{4,5},{5,4},{6,7},{7,6},{8,9},{9,8},{10,11... | collective-permute-start | bytes 1572872 | tf_op jit(solution)/shard_map/ppermute | solution.py:723
  150.6 7.2 %collective-permute-start.33 = (f32[64,1024]{1,0:T(8,128)S(1)}, f32[64,1024]{1,0:T(8,128)S(1)}, u32[]{:S(2)}, u32[]{:S(2)}) collective-permute-start(f32[64,1024]{1,0:T(8,128)S(1)} %get-tuple-element.189), channel_id=1, source_target_pairs={{0,2},{1,3},{4,0},{5,1},{8,4},{9,5},{12,8},{13,9},{14,12},{15,13},... | collective-permute-start | bytes 786440 | tf_op jit(solution)/shard_map/ppermute | solution.py:737
  152.2 6.9 %collective-permute-start.27 = (f32[64,1024]{1,0:T(8,128)S(1)}, f32[64,1024]{1,0:T(8,128)S(1)}, u32[]{:S(2)}, u32[]{:S(2)}) collective-permute-start(f32[64,1024]{1,0:T(8,128)S(1)} %get-tuple-element.236), channel_id=1, source_target_pairs={{0,4},{1,5},{4,8},{5,9},{8,12},{9,13},{12,14},{13,15},{14,10},{15,... | collective-permute-start | bytes 786440 | tf_op jit(solution)/shard_map/ppermute | solution.py:737
  154.0 11.7 %collective-permute-start.31 = (f32[128,1024]{1,0:T(8,128)S(1)}, f32[128,1024]{1,0:T(8,128)S(1)}, u32[]{:S(2)}, u32[]{:S(2)}) collective-permute-start(f32[128,1024]{1,0:T(8,128)S(1)} %get-tuple-element.188), channel_id=1, source_target_pairs={{0,1},{1,0},{2,3},{3,2},{4,5},{5,4},{6,7},{7,6},{8,9},{9,8},{10,11... | collective-permute-start | bytes 1572872 | tf_op jit(solution)/shard_map/ppermute | solution.py:723
  159.3 6.4 %collective-permute-start.36 = (f32[64,1024]{1,0:T(8,128)S(1)}, f32[64,1024]{1,0:T(8,128)S(1)}, u32[]{:S(2)}, u32[]{:S(2)}) collective-permute-start(f32[64,1024]{1,0:T(8,128)S(1)} %get-tuple-element.197), channel_id=1, source_target_pairs={{0,2},{1,3},{4,0},{5,1},{8,4},{9,5},{12,8},{13,9},{14,12},{15,13},... | collective-permute-start | bytes 786440 | tf_op jit(solution)/shard_map/ppermute | solution.py:737
  160.9 6.4 %collective-permute-start.29 = (f32[64,1024]{1,0:T(8,128)S(1)}, f32[64,1024]{1,0:T(8,128)S(1)}, u32[]{:S(2)}, u32[]{:S(2)}) collective-permute-start(f32[64,1024]{1,0:T(8,128)S(1)} %get-tuple-element.234), channel_id=1, source_target_pairs={{0,4},{1,5},{4,8},{5,9},{8,12},{9,13},{12,14},{13,15},{14,10},{15,... | collective-permute-start | bytes 786440 | tf_op jit(solution)/shard_map/ppermute | solution.py:737
  162.7 11.1 %collective-permute-start.34 = (f32[128,1024]{1,0:T(8,128)S(1)}, f32[128,1024]{1,0:T(8,128)S(1)}, u32[]{:S(2)}, u32[]{:S(2)}) collective-permute-start(f32[128,1024]{1,0:T(8,128)S(1)} %get-tuple-element.196), channel_id=1, source_target_pairs={{0,1},{1,0},{2,3},{3,2},{4,5},{5,4},{6,7},{7,6},{8,9},{9,8},{10,11... | collective-permute-start | bytes 1572872 | tf_op jit(solution)/shard_map/ppermute | solution.py:723
  167.4 6.4 %collective-permute-start.39 = (f32[64,1024]{1,0:T(8,128)S(1)}, f32[64,1024]{1,0:T(8,128)S(1)}, u32[]{:S(2)}, u32[]{:S(2)}) collective-permute-start(f32[64,1024]{1,0:T(8,128)S(1)} %get-tuple-element.205), channel_id=1, source_target_pairs={{0,2},{1,3},{4,0},{5,1},{8,4},{9,5},{12,8},{13,9},{14,12},{15,13},... | collective-permute-start | bytes 786440 | tf_op jit(solution)/shard_map/ppermute | solution.py:737
  168.0 6.4 %collective-permute-start.32 = (f32[64,1024]{1,0:T(8,128)S(1)}, f32[64,1024]{1,0:T(8,128)S(1)}, u32[]{:S(2)}, u32[]{:S(2)}) collective-permute-start(f32[64,1024]{1,0:T(8,128)S(1)} %get-tuple-element.232), channel_id=1, source_target_pairs={{0,4},{1,5},{4,8},{5,9},{8,12},{9,13},{12,14},{13,15},{14,10},{15,... | collective-permute-start | bytes 786440 | tf_op jit(solution)/shard_map/ppermute | solution.py:737
  170.8 10.2 %collective-permute-start.37 = (f32[128,1024]{1,0:T(8,128)S(1)}, f32[128,1024]{1,0:T(8,128)S(1)}, u32[]{:S(2)}, u32[]{:S(2)}) collective-permute-start(f32[128,1024]{1,0:T(8,128)S(1)} %get-tuple-element.204), channel_id=1, source_target_pairs={{0,1},{1,0},{2,3},{3,2},{4,5},{5,4},{6,7},{7,6},{8,9},{9,8},{10,11... | collective-permute-start | bytes 1572872 | tf_op jit(solution)/shard_map/ppermute | solution.py:723
  174.5 6.4 %collective-permute-start.42 = (f32[64,1024]{1,0:T(8,128)S(1)}, f32[64,1024]{1,0:T(8,128)S(1)}, u32[]{:S(2)}, u32[]{:S(2)}) collective-permute-start(f32[64,1024]{1,0:T(8,128)S(1)} %get-tuple-element.213), channel_id=1, source_target_pairs={{0,2},{1,3},{4,0},{5,1},{8,4},{9,5},{12,8},{13,9},{14,12},{15,13},... | collective-permute-start | bytes 786440 | tf_op jit(solution)/shard_map/ppermute | solution.py:737
  175.1 6.4 %collective-permute-start.35 = (f32[64,1024]{1,0:T(8,128)S(1)}, f32[64,1024]{1,0:T(8,128)S(1)}, u32[]{:S(2)}, u32[]{:S(2)}) collective-permute-start(f32[64,1024]{1,0:T(8,128)S(1)} %get-tuple-element.230), channel_id=1, source_target_pairs={{0,4},{1,5},{4,8},{5,9},{8,12},{9,13},{12,14},{13,15},{14,10},{15,... | collective-permute-start | bytes 786440 | tf_op jit(solution)/shard_map/ppermute | solution.py:737
  177.9 10.1 %collective-permute-start.40 = (f32[128,1024]{1,0:T(8,128)S(1)}, f32[128,1024]{1,0:T(8,128)S(1)}, u32[]{:S(2)}, u32[]{:S(2)}) collective-permute-start(f32[128,1024]{1,0:T(8,128)S(1)} %get-tuple-element.212), channel_id=1, source_target_pairs={{0,1},{1,0},{2,3},{3,2},{4,5},{5,4},{6,7},{7,6},{8,9},{9,8},{10,11... | collective-permute-start | bytes 1572872 | tf_op jit(solution)/shard_map/ppermute | solution.py:723
  181.6 6.4 %collective-permute-start.44 = (f32[64,1024]{1,0:T(8,128)S(1)}, f32[64,1024]{1,0:T(8,128)S(1)}, u32[]{:S(2)}, u32[]{:S(2)}) collective-permute-start(f32[64,1024]{1,0:T(8,128)S(1)} %get-tuple-element.221), channel_id=1, source_target_pairs={{0,2},{1,3},{4,0},{5,1},{8,4},{9,5},{12,8},{13,9},{14,12},{15,13},... | collective-permute-start | bytes 786440 | tf_op jit(solution)/shard_map/ppermute | solution.py:737
  182.1 6.4 %collective-permute-start.38 = (f32[64,1024]{1,0:T(8,128)S(1)}, f32[64,1024]{1,0:T(8,128)S(1)}, u32[]{:S(2)}, u32[]{:S(2)}) collective-permute-start(f32[64,1024]{1,0:T(8,128)S(1)} %get-tuple-element.228), channel_id=1, source_target_pairs={{0,4},{1,5},{4,8},{5,9},{8,12},{9,13},{12,14},{13,15},{14,10},{15,... | collective-permute-start | bytes 786440 | tf_op jit(solution)/shard_map/ppermute | solution.py:737
  185.0 5.7 %collective-permute-start.43 = (f32[128,1024]{1,0:T(8,128)S(1)}, f32[128,1024]{1,0:T(8,128)S(1)}, u32[]{:S(2)}, u32[]{:S(2)}) collective-permute-start(f32[128,1024]{1,0:T(8,128)S(1)} %get-tuple-element.220), channel_id=1, source_target_pairs={{0,1},{1,0},{2,3},{3,2},{4,5},{5,4},{6,7},{7,6},{8,9},{9,8},{10,11... | collective-permute-start | bytes 1572872 | tf_op jit(solution)/shard_map/ppermute | solution.py:723
  188.6 6.4 %collective-permute-start.41 = (f32[64,1024]{1,0:T(8,128)S(1)}, f32[64,1024]{1,0:T(8,128)S(1)}, u32[]{:S(2)}, u32[]{:S(2)}) collective-permute-start(f32[64,1024]{1,0:T(8,128)S(1)} %get-tuple-element.226), channel_id=1, source_target_pairs={{0,4},{1,5},{4,8},{5,9},{8,12},{9,13},{12,14},{13,15},{14,10},{15,... | collective-permute-start | bytes 786440 | tf_op jit(solution)/shard_map/ppermute | solution.py:737
  190.4 6.4 %collective-permute-start.45 = (f32[64,1024]{1,0:T(8,128)S(1)}, f32[64,1024]{1,0:T(8,128)S(1)}, u32[]{:S(2)}, u32[]{:S(2)}) collective-permute-start(f32[64,1024]{1,0:T(8,128)S(1)} %get-tuple-element.227), channel_id=1, source_target_pairs={{0,2},{1,3},{4,0},{5,1},{8,4},{9,5},{12,8},{13,9},{14,12},{15,13},... | collective-permute-start | bytes 786440 | tf_op jit(solution)/shard_map/ppermute | solution.py:737
  (14 other events, 85.9 us)

commit v3 on v2

--- a/solution.py
+++ b/solution.py
@@ -385,9 +385,15 @@
         value = jnp.concatenate([c, s], axis=1)
         slope = jnp.concatenate([-k * s, k * c], axis=1)
         bend = -twofold(k * k) * value
+        turned = []
         for n, half in enumerate(halves(jnp.concatenate([value, slope, bend]))):
             near[n * 3 * span : (n + 1) * 3 * span, both] = half
-            far[pl.ds((n * groups + g) * 2 * LANES, 2 * LANES), :] = half.T
+            turned.append(half.T)
+        high, low = turned
+        cut = slice(0, 2 * span), slice(2 * span, 3 * span)
+        far[both, :] = jnp.concatenate(
+            [part[:, c] for c in cut for part in (high, high, low)], axis=1
+        )
 
 
 def adjoint_kernel(
@@ -459,8 +465,16 @@
     low = halves(jnp.concatenate([both * both * part[0], -turn(part[1], ky), -part[2]]))
     high = halves(jnp.concatenate([-turn(part[3], ky), part[4]]))
 
-    sums_all[...] = stacked(far[...], *low, groups * wide)
-    slopes_all[...] = stacked(far[:, : 2 * span], *high, groups * wide)
+    cut = slice(0, 2 * span), slice(2 * span, 3 * span)
+    low = [low[n][c] for c in cut for n in (0, 1, 0)]
+    sums_all[...] = jnp.dot(
+        far[...], jnp.concatenate(low), preferred_element_type=jnp.float32
+    )
+    slopes_all[...] = jnp.dot(
+        far[:, : 6 * span],
+        jnp.concatenate([high[0], high[1], high[0]]),
+        preferred_element_type=jnp.float32,
+    )
     for g in range(groups):
         here = slice(g * wide, (g + 1) * wide)
         modulus = length(wave_x, ky, g)
@@ -587,7 +601,7 @@
             ),
         )
 
-    masked = density * active.astype(jnp.float32)[None]
+    masked = jnp.where(active[None] != 0, density, 0.0)
     near, far, gain = call(
         near_kernel,
         1,
@@ -595,7 +609,7 @@
         [held] * 3,
         [
             jax.ShapeDtypeStruct((6 * span, period), jnp.bfloat16),
-            jax.ShapeDtypeStruct((2 * period, 3 * span), jnp.bfloat16),
+            jax.ShapeDtypeStruct((period, 9 * span), jnp.bfloat16),
             jax.ShapeDtypeStruct((side, side // 2), jnp.float32),
         ],
         [],
@@ -728,11 +742,13 @@
 
         ready = share(1, grids)
         now = [part(ready, l) for l in (0, 1)]
-        ready = share(2, grids)
         for step in range(1, chips):
+            if step < chips - 1:
+                now[1], grids = lax.optimization_barrier((now[1], grids))
+            if step == 1:
+                ready = share(2, grids)
             current = ready
             if step < chips - 1:
-                now[1], grids = lax.optimization_barrier((now[1], grids))
                 ready = share(step + 2, grids)
             now = [lax.ppermute(now[l], "tile", ways[l]) + part(current, l) for l in (0, 1)]
         gradient = jnp.stack(now)

time: 198 us -> 197 us (level)
  Pallas kernels: 79.8 us -> 76.6 us
  waiting for transfers between devices: 76 us -> 78.1 us
    pallas_call x1, Pallas kernels: 31.2 us -> 28 us  [body(): call(adjoint_kernel, own, [smem] + [held] * 4 + shared + [held] + [group_...]
    unnamed x32 -> x34, local copies, waits for them, and re-layouts: 4.15 us -> 4.15 us
  transfers between devices with their start and end apart: 46 -> 46, of which waited for: 32 -> 33; matrix products, arithmetic and copies ran while one was open for 1% -> 1% of each run, Pallas kernels for 11% -> 10%
where the time goes in v3:
time: 197 us; the launch traced here: 196 us
  waiting for transfers between devices  78.1 us (40%)
  Pallas kernels  76.6 us (39%)
  starting transfers between devices  31.9 us (16%)
  local copies, waits for them, and re-layouts  4.88 us (2%)
  other arithmetic  3.92 us (2%)
    ppermute x14, waiting for transfers between devices, body(): came = [lax.ppermute(chains[l], 'tile', ways[l]) for l in (0, 1)]  36.7 us
    ppermute x14, waiting for transfers between devices, body(): lax.ppermute(now[l], 'tile', ways[l]) + part(current, l)  32.7 us
    pallas_call x1, Pallas kernels, body(): call(adjoint_kernel, own, [smem] + [held] * 4 + shared + [held] + [group_...  28 us
    pallas_call x1, Pallas kernels, body(): call(forward_kernel, own, [smem] + [held] * 2 + shared + [held] + [group_...  24.1 us
    ppermute x14, starting transfers between devices, body(): came = [lax.ppermute(chains[l], 'tile', ways[l]) for l in (0, 1)]  15.2 us
    ppermute x14, starting transfers between devices, body(): lax.ppermute(now[l], 'tile', ways[l]) + part(current, l)  14.5 us
    pallas_call x8, Pallas kernels, transformed(): call(kernel, 1, [held] * (len(args) - 1), [held] * 3, shapes, [pltpu.VMEM...  11.3 us
    pallas_call x8, Pallas kernels, share(): call(functools.partial(strips_kernel, 2 + 2 * offset), 1, [held] * 6, [he...  10.8 us
  transfers between devices with their start and end apart: 46, of which 33 were waited for; matrix products, arithmetic and copies ran while one was open for 1% of the time, Pallas kernels for 10%

profile of v3, /device:TPU:0, one launch (start us, length us, event | category | flops | bytes accessed | tf_op | source)
XLA Modules:
  0.0 196.5 jit_solution(5039754637229632610)
XLA Ops:
  2.9 3.1 %collective-permute-start = (f32[64,1024]{1,0:T(8,128)S(1)}, f32[64,1024]{1,0:T(8,128)S(1)}, u32[]{:S(2)}, u32[]{:S(2)}) collective-permute-start(f32[64,1024]{1,0:T(8,128)S(1)} %get-tuple-element.241.a), channel_id=1, source_target_pairs={{0,4},{1,5},{4,8},{5,9},{8,12},{9,13},{12,14},{13,15},{14,10},{15,... | collective-permute-start | bytes 786440 | tf_op jit(solution)/shard_map/ppermute | solution.py:649
  9.2 1.4 shard_map.176
  10.6 1.7 collective-permute-done.a
  12.2 1.5 collective-permute-done.1.b
  14.3 1.6 collective-permute-start.2
  16.4 1.4 shard_map.177
  17.8 4.7 %collective-permute-done.2.a = f32[64,1024]{1,0:T(8,128)S(1)} collective-permute-done((f32[64,1024]{1,0:T(8,128)S(1)}, f32[64,1024]{1,0:T(8,128)S(1)}, u32[]{:S(2)}, u32[]{:S(2)}) %collective-permute-start.2) | collective-permute-done | bytes 262176 | tf_op jit(solution)/shard_map/ppermute | solution.py:649
  23.8 1.6 collective-permute-start.5
  25.9 1.4 shard_map.178
  27.3 5.2 %collective-permute-done.5.a = f32[64,1024]{1,0:T(8,128)S(1)} collective-permute-done((f32[64,1024]{1,0:T(8,128)S(1)}, f32[64,1024]{1,0:T(8,128)S(1)}, u32[]{:S(2)}, u32[]{:S(2)}) %collective-permute-start.5) | collective-permute-done | bytes 262176 | tf_op jit(solution)/shard_map/ppermute | solution.py:649
  33.8 1.5 collective-permute-start.8
  35.9 1.8 shard_map.179
  37.7 1.4 shard_map.180
  39.1 3.4 %collective-permute-done.8.a = f32[64,1024]{1,0:T(8,128)S(1)} collective-permute-done((f32[64,1024]{1,0:T(8,128)S(1)}, f32[64,1024]{1,0:T(8,128)S(1)}, u32[]{:S(2)}, u32[]{:S(2)}) %collective-permute-start.8) | collective-permute-done | bytes 262176 | tf_op jit(solution)/shard_map/ppermute | solution.py:649
  44.2 1.6 collective-permute-start.13
  45.8 1.4 shard_map.181
  47.2 5.3 %collective-permute-done.12.a = f32[64,1024]{1,0:T(8,128)S(1)} collective-permute-done((f32[64,1024]{1,0:T(8,128)S(1)}, f32[64,1024]{1,0:T(8,128)S(1)}, u32[]{:S(2)}, u32[]{:S(2)}) %collective-permute-start.12) | collective-permute-done | bytes 262176 | tf_op jit(solution)/shard_map/ppermute | solution.py:649
  53.1 1.6 collective-permute-start.16
  54.7 1.4 shard_map.182
  56.1 5.3 %collective-permute-done.15.a = f32[64,1024]{1,0:T(8,128)S(1)} collective-permute-done((f32[64,1024]{1,0:T(8,128)S(1)}, f32[64,1024]{1,0:T(8,128)S(1)}, u32[]{:S(2)}, u32[]{:S(2)}) %collective-permute-start.15) | collective-permute-done | bytes 262176 | tf_op jit(solution)/shard_map/ppermute | solution.py:649
  62.0 1.6 collective-permute-start.21
  63.6 1.4 shard_map.183
  65.0 5.3 %collective-permute-done.20.a = f32[64,1024]{1,0:T(8,128)S(1)} collective-permute-done((f32[64,1024]{1,0:T(8,128)S(1)}, f32[64,1024]{1,0:T(8,128)S(1)}, u32[]{:S(2)}, u32[]{:S(2)}) %collective-permute-start.20) | collective-permute-done | bytes 262176 | tf_op jit(solution)/shard_map/ppermute | solution.py:649
  70.4 1.4 shard_map.184
  72.4 1.4 collective-permute-done.22.far
  76.9 24.1 %shard_map.186.field = f32[640,1024]{1,0:T(8,128)S(1)} custom-call(s32[20]{0:T(128)S(1)} %dynamic-slice_bitcast_fusion.place, f32[2]{0:T(128)S(1)} %copy-done.15, f32[1024,1024]{1,0:T(8,128)S(1)} %get-tuple-element.159.spec_a, f32[1024,1024]{1,0:T(8,128)S(1)} %get-tuple-element.160.spec_b, f32[1024,512]{1,0:T(8,128)S(1)} %get-tuple-element.161.gain, ...), custom_call_target="tpu_custom_call" | custom-call | tf_op jit(solution)/shard_map/pallas_call | solution.py:684
  101.2 4.8 %collective-permute-done.23.other = f32[640,1024]{1,0:T(8,128)S(1)} collective-permute-done((f32[640,1024]{1,0:T(8,128)S(1)}, f32[640,1024]{1,0:T(8,128)S(1)}, u32[]{:S(2)}, u32[]{:S(2)}) %collective-permute-start.23) | collective-permute-done | bytes 2621472 | tf_op jit(solution)/shard_map/ppermute | solution.py:699
  106.0 28.0 %shard_map.187 = (f32[6,64,1024]{2,1,0:T(8,128)}, bf16[1024,1024]{1,0:T(8,128)(2,1)S(1)}, bf16[1024,1024]{1,0:T(8,128)(2,1)S(1)}, bf16[1024,1024]{1,0:T(8,128)(2,1)S(1)}, bf16[1024,1024]{1,0:T(8,128)(2,1)S(1)}) custom-call(s32[20]{0:T(128)S(1)} %dynamic-slice_bitcast_fusion.place, f32[2]{0:T(128)S(1)} %copy-done.15, f32[640,1024]{1,0:T(8,128)S(1)} %shard_map.186.field, ...), custom_call_target="tpu_custom_call" | custom-call | tf_op jit(solution)/shard_map/pallas_call | solution.py:700
  135.5 1.8 collective-permute-done.24
  137.4 1.5 shard_map.189
  139.1 1.6 collective-permute-start.30
  142.6 5.1 %collective-permute-done.30 = f32[64,1024]{1,0:T(8,128)S(1)} collective-permute-done((f32[64,1024]{1,0:T(8,128)S(1)}, f32[64,1024]{1,0:T(8,128)S(1)}, u32[]{:S(2)}, u32[]{:S(2)}) %collective-permute-start.30) | collective-permute-done | bytes 262176 | tf_op jit(solution)/shard_map/ppermute | solution.py:753
  149.1 1.6 collective-permute-start.33
  152.6 4.0 %collective-permute-done.33 = f32[64,1024]{1,0:T(8,128)S(1)} collective-permute-done((f32[64,1024]{1,0:T(8,128)S(1)}, f32[64,1024]{1,0:T(8,128)S(1)}, u32[]{:S(2)}, u32[]{:S(2)}) %collective-permute-start.33) | collective-permute-done | bytes 262176 | tf_op jit(solution)/shard_map/ppermute | solution.py:753
  158.0 1.6 collective-permute-start.36
  161.5 2.9 %collective-permute-done.36 = f32[64,1024]{1,0:T(8,128)S(1)} collective-permute-done((f32[64,1024]{1,0:T(8,128)S(1)}, f32[64,1024]{1,0:T(8,128)S(1)}, u32[]{:S(2)}, u32[]{:S(2)}) %collective-permute-start.36) | collective-permute-done | bytes 262176 | tf_op jit(solution)/shard_map/ppermute | solution.py:753
  164.5 1.6 collective-permute-done.29
  166.8 1.4 collective-permute-start.32
  169.6 2.9 %collective-permute-done.39 = f32[64,1024]{1,0:T(8,128)S(1)} collective-permute-done((f32[64,1024]{1,0:T(8,128)S(1)}, f32[64,1024]{1,0:T(8,128)S(1)}, u32[]{:S(2)}, u32[]{:S(2)}) %collective-permute-start.39) | collective-permute-done | bytes 262176 | tf_op jit(solution)/shard_map/ppermute | solution.py:753
  173.9 1.5 collective-permute-start.35
  175.4 1.3 shard_map.194
  176.8 2.9 %collective-permute-done.42 = f32[64,1024]{1,0:T(8,128)S(1)} collective-permute-done((f32[64,1024]{1,0:T(8,128)S(1)}, f32[64,1024]{1,0:T(8,128)S(1)}, u32[]{:S(2)}, u32[]{:S(2)}) %collective-permute-start.42) | collective-permute-done | bytes 262176 | tf_op jit(solution)/shard_map/ppermute | solution.py:753
  180.9 1.6 collective-permute-start.38
  182.4 1.3 shard_map.195
  183.8 2.9 %collective-permute-done.44 = f32[64,1024]{1,0:T(8,128)S(1)} collective-permute-done((f32[64,1024]{1,0:T(8,128)S(1)}, f32[64,1024]{1,0:T(8,128)S(1)}, u32[]{:S(2)}, u32[]{:S(2)}) %collective-permute-start.44) | collective-permute-done | bytes 262176 | tf_op jit(solution)/shard_map/ppermute | solution.py:753
  187.4 1.7 collective-permute-start.41
  189.5 4.3 %collective-permute-done.41 = f32[64,1024]{1,0:T(8,128)S(1)} collective-permute-done((f32[64,1024]{1,0:T(8,128)S(1)}, f32[64,1024]{1,0:T(8,128)S(1)}, u32[]{:S(2)}, u32[]{:S(2)}) %collective-permute-start.41) | collective-permute-done | bytes 262176 | tf_op jit(solution)/shard_map/ppermute | solution.py:753
  193.8 1.7 collective-permute-done.45
  (112 shorter events, 33.8 us)
Async XLA Ops:
  2.9 9.3 %collective-permute-start = (f32[64,1024]{1,0:T(8,128)S(1)}, f32[64,1024]{1,0:T(8,128)S(1)}, u32[]{:S(2)}, u32[]{:S(2)}) collective-permute-start(f32[64,1024]{1,0:T(8,128)S(1)} %get-tuple-element.241.a), channel_id=1, source_target_pairs={{0,4},{1,5},{4,8},{5,9},{8,12},{9,13},{12,14},{13,15},{14,10},{15,... | collective-permute-start | bytes 786440 | tf_op jit(solution)/shard_map/ppermute | solution.py:649
  6.0 7.8 %collective-permute-start.1 = (f32[64,1024]{1,0:T(8,128)S(1)}, f32[64,1024]{1,0:T(8,128)S(1)}, u32[]{:S(2)}, u32[]{:S(2)}) collective-permute-start(f32[64,1024]{1,0:T(8,128)S(1)} %get-tuple-element.240.b), channel_id=1, source_target_pairs={{0,2},{1,3},{4,0},{5,1},{8,4},{9,5},{12,8},{13,9},{14,12},{15,13},... | collective-permute-start | bytes 786440 | tf_op jit(solution)/shard_map/ppermute | solution.py:649
  13.8 2.6 %collective-permute-start.4 = (f32[128,1024]{1,0:T(8,128)S(1)}, f32[128,1024]{1,0:T(8,128)S(1)}, u32[]{:S(2)}, u32[]{:S(2)}) collective-permute-start(f32[128,1024]{1,0:T(8,128)S(1)} %get-tuple-element.116), channel_id=1, source_target_pairs={{0,1},{1,0},{2,3},{3,2},{4,5},{5,4},{6,7},{7,6},{8,9},{9,8},{10,11... | collective-permute-start | bytes 1572872 | tf_op jit(solution)/shard_map/ppermute | solution.py:651
  13.8 23.9 %collective-permute-start.11 = (f32[6,64,1024]{2,1,0:T(8,128)}, f32[6,64,1024]{2,1,0:T(8,128)S(1)}, u32[]{:S(2)}, u32[]{:S(2)}) collective-permute-start(f32[6,64,1024]{2,1,0:T(8,128)} %seen.1), channel_id=1, source_target_pairs={{0,1},{1,0},{2,3},{3,2},{4,5},{5,4},{6,7},{7,6},{8,9},{9,8},{10,11... | collective-permute-start | bytes 4718600 | tf_op jit(solution)/shard_map/ppermute | solution.py:577
  14.3 8.2 %collective-permute-start.2 = (f32[64,1024]{1,0:T(8,128)S(1)}, f32[64,1024]{1,0:T(8,128)S(1)}, u32[]{:S(2)}, u32[]{:S(2)}) collective-permute-start(f32[64,1024]{1,0:T(8,128)S(1)} %collective-permute-done.a), channel_id=1, source_target_pairs={{0,4},{1,5},{4,8},{5,9},{8,12},{9,13},{12,14},{13,15},{14,10},{15,... | collective-permute-start | bytes 786440 | tf_op jit(solution)/shard_map/ppermute | solution.py:649
  15.9 7.9 %collective-permute-start.3 = (f32[64,1024]{1,0:T(8,128)S(1)}, f32[64,1024]{1,0:T(8,128)S(1)}, u32[]{:S(2)}, u32[]{:S(2)}) collective-permute-start(f32[64,1024]{1,0:T(8,128)S(1)} %collective-permute-done.1.b), channel_id=1, source_target_pairs={{0,2},{1,3},{4,0},{5,1},{8,4},{9,5},{12,8},{13,9},{14,12},{15,13},... | collective-permute-start | bytes 786440 | tf_op jit(solution)/shard_map/ppermute | solution.py:649
  23.8 2.0 %collective-permute-start.7 = (f32[128,1024]{1,0:T(8,128)S(1)}, f32[128,1024]{1,0:T(8,128)S(1)}, u32[]{:S(2)}, u32[]{:S(2)}) collective-permute-start(f32[128,1024]{1,0:T(8,128)S(1)} %get-tuple-element.122), channel_id=1, source_target_pairs={{0,1},{1,0},{2,3},{3,2},{4,5},{5,4},{6,7},{7,6},{8,9},{9,8},{10,11... | collective-permute-start | bytes 1572872 | tf_op jit(solution)/shard_map/ppermute | solution.py:651
  23.8 8.7 %collective-permute-start.5 = (f32[64,1024]{1,0:T(8,128)S(1)}, f32[64,1024]{1,0:T(8,128)S(1)}, u32[]{:S(2)}, u32[]{:S(2)}) collective-permute-start(f32[64,1024]{1,0:T(8,128)S(1)} %collective-permute-done.2.a), channel_id=1, source_target_pairs={{0,4},{1,5},{4,8},{5,9},{8,12},{9,13},{12,14},{13,15},{14,10},{15,... | collective-permute-start | bytes 786440 | tf_op jit(solution)/shard_map/ppermute | solution.py:649
  25.4 8.4 %collective-permute-start.6 = (f32[64,1024]{1,0:T(8,128)S(1)}, f32[64,1024]{1,0:T(8,128)S(1)}, u32[]{:S(2)}, u32[]{:S(2)}) collective-permute-start(f32[64,1024]{1,0:T(8,128)S(1)} %collective-permute-done.3.b), channel_id=1, source_target_pairs={{0,2},{1,3},{4,0},{5,1},{8,4},{9,5},{12,8},{13,9},{14,12},{15,13},... | collective-permute-start | bytes 786440 | tf_op jit(solution)/shard_map/ppermute | solution.py:649
  33.8 3.9 %collective-permute-start.10 = (f32[128,1024]{1,0:T(8,128)S(1)}, f32[128,1024]{1,0:T(8,128)S(1)}, u32[]{:S(2)}, u32[]{:S(2)}) collective-permute-start(f32[128,1024]{1,0:T(8,128)S(1)} %get-tuple-element.128), channel_id=1, source_target_pairs={{0,1},{1,0},{2,3},{3,2},{4,5},{5,4},{6,7},{7,6},{8,9},{9,8},{10,11... | collective-permute-start | bytes 1572872 | tf_op jit(solution)/shard_map/ppermute | solution.py:651
  33.8 8.7 %collective-permute-start.8 = (f32[64,1024]{1,0:T(8,128)S(1)}, f32[64,1024]{1,0:T(8,128)S(1)}, u32[]{:S(2)}, u32[]{:S(2)}) collective-permute-start(f32[64,1024]{1,0:T(8,128)S(1)} %collective-permute-done.5.a), channel_id=1, source_target_pairs={{0,4},{1,5},{4,8},{5,9},{8,12},{9,13},{12,14},{13,15},{14,10},{15,... | collective-permute-start | bytes 786440 | tf_op jit(solution)/shard_map/ppermute | solution.py:649
  35.3 8.4 %collective-permute-start.9 = (f32[64,1024]{1,0:T(8,128)S(1)}, f32[64,1024]{1,0:T(8,128)S(1)}, u32[]{:S(2)}, u32[]{:S(2)}) collective-permute-start(f32[64,1024]{1,0:T(8,128)S(1)} %collective-permute-done.6.b), channel_id=1, source_target_pairs={{0,2},{1,3},{4,0},{5,1},{8,4},{9,5},{12,8},{13,9},{14,12},{15,13},... | collective-permute-start | bytes 786440 | tf_op jit(solution)/shard_map/ppermute | solution.py:649
  43.8 2.0 %collective-permute-start.14 = (f32[128,1024]{1,0:T(8,128)S(1)}, f32[128,1024]{1,0:T(8,128)S(1)}, u32[]{:S(2)}, u32[]{:S(2)}) collective-permute-start(f32[128,1024]{1,0:T(8,128)S(1)} %get-tuple-element.138), channel_id=1, source_target_pairs={{0,1},{1,0},{2,3},{3,2},{4,5},{5,4},{6,7},{7,6},{8,9},{9,8},{10,11... | collective-permute-start | bytes 1572872 | tf_op jit(solution)/shard_map/ppermute | solution.py:651
  43.8 8.7 %collective-permute-start.12 = (f32[64,1024]{1,0:T(8,128)S(1)}, f32[64,1024]{1,0:T(8,128)S(1)}, u32[]{:S(2)}, u32[]{:S(2)}) collective-permute-start(f32[64,1024]{1,0:T(8,128)S(1)} %collective-permute-done.8.a), channel_id=1, source_target_pairs={{0,4},{1,5},{4,8},{5,9},{8,12},{9,13},{12,14},{13,15},{14,10},{15,... | collective-permute-start | bytes 786440 | tf_op jit(solution)/shard_map/ppermute | solution.py:649
  44.2 8.4 %collective-permute-start.13 = (f32[64,1024]{1,0:T(8,128)S(1)}, f32[64,1024]{1,0:T(8,128)S(1)}, u32[]{:S(2)}, u32[]{:S(2)}) collective-permute-start(f32[64,1024]{1,0:T(8,128)S(1)} %collective-permute-done.9.b), channel_id=1, source_target_pairs={{0,2},{1,3},{4,0},{5,1},{8,4},{9,5},{12,8},{13,9},{14,12},{15,13},... | collective-permute-start | bytes 786440 | tf_op jit(solution)/shard_map/ppermute | solution.py:649
  52.7 2.0 %collective-permute-start.17 = (f32[128,1024]{1,0:T(8,128)S(1)}, f32[128,1024]{1,0:T(8,128)S(1)}, u32[]{:S(2)}, u32[]{:S(2)}) collective-permute-start(f32[128,1024]{1,0:T(8,128)S(1)} %get-tuple-element.144), channel_id=1, source_target_pairs={{0,1},{1,0},{2,3},{3,2},{4,5},{5,4},{6,7},{7,6},{8,9},{9,8},{10,11... | collective-permute-start | bytes 1572872 | tf_op jit(solution)/shard_map/ppermute | solution.py:651
  52.7 8.7 %collective-permute-start.15 = (f32[64,1024]{1,0:T(8,128)S(1)}, f32[64,1024]{1,0:T(8,128)S(1)}, u32[]{:S(2)}, u32[]{:S(2)}) collective-permute-start(f32[64,1024]{1,0:T(8,128)S(1)} %collective-permute-done.12.a), channel_id=1, source_target_pairs={{0,4},{1,5},{4,8},{5,9},{8,12},{9,13},{12,14},{13,15},{14,10},{15,... | collective-permute-start | bytes 786440 | tf_op jit(solution)/shard_map/ppermute | solution.py:649
  53.1 8.4 %collective-permute-start.16 = (f32[64,1024]{1,0:T(8,128)S(1)}, f32[64,1024]{1,0:T(8,128)S(1)}, u32[]{:S(2)}, u32[]{:S(2)}) collective-permute-start(f32[64,1024]{1,0:T(8,128)S(1)} %collective-permute-done.13.b), channel_id=1, source_target_pairs={{0,2},{1,3},{4,0},{5,1},{8,4},{9,5},{12,8},{13,9},{14,12},{15,13},... | collective-permute-start | bytes 786440 | tf_op jit(solution)/shard_map/ppermute | solution.py:649
  61.5 2.0 %collective-permute-start.18 = (f32[128,1024]{1,0:T(8,128)S(1)}, f32[128,1024]{1,0:T(8,128)S(1)}, u32[]{:S(2)}, u32[]{:S(2)}) collective-permute-start(f32[128,1024]{1,0:T(8,128)S(1)} %get-tuple-element.150), channel_id=1, source_target_pairs={{0,1},{1,0},{2,3},{3,2},{4,5},{5,4},{6,7},{7,6},{8,9},{9,8},{10,11... | collective-permute-start | bytes 1572872 | tf_op jit(solution)/shard_map/ppermute | solution.py:651
  61.5 8.7 %collective-permute-start.20 = (f32[64,1024]{1,0:T(8,128)S(1)}, f32[64,1024]{1,0:T(8,128)S(1)}, u32[]{:S(2)}, u32[]{:S(2)}) collective-permute-start(f32[64,1024]{1,0:T(8,128)S(1)} %collective-permute-done.15.a), channel_id=1, source_target_pairs={{0,4},{1,5},{4,8},{5,9},{8,12},{9,13},{12,14},{13,15},{14,10},{15,... | collective-permute-start | bytes 786440 | tf_op jit(solution)/shard_map/ppermute | solution.py:649
  62.0 8.4 %collective-permute-start.21 = (f32[64,1024]{1,0:T(8,128)S(1)}, f32[64,1024]{1,0:T(8,128)S(1)}, u32[]{:S(2)}, u32[]{:S(2)}) collective-permute-start(f32[64,1024]{1,0:T(8,128)S(1)} %collective-permute-done.16.b), channel_id=1, source_target_pairs={{0,2},{1,3},{4,0},{5,1},{8,4},{9,5},{12,8},{13,9},{14,12},{15,13},... | collective-permute-start | bytes 786440 | tf_op jit(solution)/shard_map/ppermute | solution.py:649
  71.8 2.0 %collective-permute-start.22 = (f32[128,1024]{1,0:T(8,128)S(1)}, f32[128,1024]{1,0:T(8,128)S(1)}, u32[]{:S(2)}, u32[]{:S(2)}) collective-permute-start(f32[128,1024]{1,0:T(8,128)S(1)} %get-tuple-element.156), channel_id=1, source_target_pairs={{0,1},{1,0},{2,3},{3,2},{4,5},{5,4},{6,7},{7,6},{8,9},{9,8},{10,11... | collective-permute-start | bytes 1572872 | tf_op jit(solution)/shard_map/ppermute | solution.py:669
  71.9 2.6 %collective-permute-start.19 = (f32[128,1024]{1,0:T(8,128)S(1)}, f32[128,1024]{1,0:T(8,128)S(1)}, u32[]{:S(2)}, u32[]{:S(2)}) collective-permute-start(f32[128,1024]{1,0:T(8,128)S(1)} %get-tuple-element.153), channel_id=1, source_target_pairs={{0,1},{1,0},{2,3},{3,2},{4,5},{5,4},{6,7},{7,6},{8,9},{9,8},{10,11... | collective-permute-start | bytes 1572872 | tf_op jit(solution)/shard_map/ppermute | solution.py:658
  76.9 29.1 %copy-start.7 = (bf16[8,512,256]{2,1,0:T(8,128)(2,1)S(1)}, bf16[8,512,256]{2,1,0:T(8,128)(2,1)}, u32[]{:S(2)}) copy-start(bf16[8,512,256]{2,1,0:T(8,128)(2,1)} %constant.44.clone.mix) | copy-start | bytes 6291460
  76.9 29.1 %copy-start.10 = (f32[6,64,1024]{2,1,0:T(8,128)S(1)}, f32[6,64,1024]{2,1,0:T(8,128)}, u32[]{:S(2)}) copy-start(f32[6,64,1024]{2,1,0:T(8,128)} %seen.1) | copy-start | bytes 4718596
  101.0 5.0 %collective-permute-start.23 = (f32[640,1024]{1,0:T(8,128)S(1)}, f32[640,1024]{1,0:T(8,128)S(1)}, u32[]{:S(2)}, u32[]{:S(2)}) collective-permute-start(f32[640,1024]{1,0:T(8,128)S(1)} %shard_map.186.field), channel_id=1, source_target_pairs={{0,1},{1,0},{2,3},{3,2},{4,5},{5,4},{6,7},{7,6},{8,9},{9,8},{10,11... | collective-permute-start | bytes 7864328 | tf_op jit(solution)/shard_map/ppermute | solution.py:699
  135.3 2.0 %collective-permute-start.24 = (f32[128,1024]{1,0:T(8,128)S(1)}, f32[128,1024]{1,0:T(8,128)S(1)}, u32[]{:S(2)}, u32[]{:S(2)}) collective-permute-start(f32[128,1024]{1,0:T(8,128)S(1)} %get-tuple-element.171), channel_id=1, source_target_pairs={{0,1},{1,0},{2,3},{3,2},{4,5},{5,4},{6,7},{7,6},{8,9},{9,8},{10,11... | collective-permute-start | bytes 1572872 | tf_op jit(solution)/shard_map/ppermute | solution.py:737
  138.9 10.1 %collective-permute-start.26 = (f32[128,1024]{1,0:T(8,128)S(1)}, f32[128,1024]{1,0:T(8,128)S(1)}, u32[]{:S(2)}, u32[]{:S(2)}) collective-permute-start(f32[128,1024]{1,0:T(8,128)S(1)} %get-tuple-element.178), channel_id=1, source_target_pairs={{0,1},{1,0},{2,3},{3,2},{4,5},{5,4},{6,7},{7,6},{8,9},{9,8},{10,11... | collective-permute-start | bytes 1572872 | tf_op jit(solution)/shard_map/ppermute | solution.py:737
  139.1 8.6 %collective-permute-start.30 = (f32[64,1024]{1,0:T(8,128)S(1)}, f32[64,1024]{1,0:T(8,128)S(1)}, u32[]{:S(2)}, u32[]{:S(2)}) collective-permute-start(f32[64,1024]{1,0:T(8,128)S(1)} %get-tuple-element.181), channel_id=1, source_target_pairs={{0,2},{1,3},{4,0},{5,1},{8,4},{9,5},{12,8},{13,9},{14,12},{15,13},... | collective-permute-start | bytes 786440 | tf_op jit(solution)/shard_map/ppermute | solution.py:753
  140.7 8.3 %collective-permute-start.25 = (f32[64,1024]{1,0:T(8,128)S(1)}, f32[64,1024]{1,0:T(8,128)S(1)}, u32[]{:S(2)}, u32[]{:S(2)}) collective-permute-start(f32[64,1024]{1,0:T(8,128)S(1)} %get-tuple-element.238), channel_id=1, source_target_pairs={{0,4},{1,5},{4,8},{5,9},{8,12},{9,13},{12,14},{13,15},{14,10},{15,... | collective-permute-start | bytes 786440 | tf_op jit(solution)/shard_map/ppermute | solution.py:753
  142.5 10.1 %collective-permute-start.28 = (f32[128,1024]{1,0:T(8,128)S(1)}, f32[128,1024]{1,0:T(8,128)S(1)}, u32[]{:S(2)}, u32[]{:S(2)}) collective-permute-start(f32[128,1024]{1,0:T(8,128)S(1)} %get-tuple-element.180), channel_id=1, source_target_pairs={{0,1},{1,0},{2,3},{3,2},{4,5},{5,4},{6,7},{7,6},{8,9},{9,8},{10,11... | collective-permute-start | bytes 1572872 | tf_op jit(solution)/shard_map/ppermute | solution.py:737
  149.1 7.5 %collective-permute-start.33 = (f32[64,1024]{1,0:T(8,128)S(1)}, f32[64,1024]{1,0:T(8,128)S(1)}, u32[]{:S(2)}, u32[]{:S(2)}) collective-permute-start(f32[64,1024]{1,0:T(8,128)S(1)} %get-tuple-element.189), channel_id=1, source_target_pairs={{0,2},{1,3},{4,0},{5,1},{8,4},{9,5},{12,8},{13,9},{14,12},{15,13},... | collective-permute-start | bytes 786440 | tf_op jit(solution)/shard_map/ppermute | solution.py:753
  150.8 7.2 %collective-permute-start.27 = (f32[64,1024]{1,0:T(8,128)S(1)}, f32[64,1024]{1,0:T(8,128)S(1)}, u32[]{:S(2)}, u32[]{:S(2)}) collective-permute-start(f32[64,1024]{1,0:T(8,128)S(1)} %get-tuple-element.236), channel_id=1, source_target_pairs={{0,4},{1,5},{4,8},{5,9},{8,12},{9,13},{12,14},{13,15},{14,10},{15,... | collective-permute-start | bytes 786440 | tf_op jit(solution)/shard_map/ppermute | solution.py:753
  152.5 11.9 %collective-permute-start.31 = (f32[128,1024]{1,0:T(8,128)S(1)}, f32[128,1024]{1,0:T(8,128)S(1)}, u32[]{:S(2)}, u32[]{:S(2)}) collective-permute-start(f32[128,1024]{1,0:T(8,128)S(1)} %get-tuple-element.188), channel_id=1, source_target_pairs={{0,1},{1,0},{2,3},{3,2},{4,5},{5,4},{6,7},{7,6},{8,9},{9,8},{10,11... | collective-permute-start | bytes 1572872 | tf_op jit(solution)/shard_map/ppermute | solution.py:737
  158.0 6.4 %collective-permute-start.36 = (f32[64,1024]{1,0:T(8,128)S(1)}, f32[64,1024]{1,0:T(8,128)S(1)}, u32[]{:S(2)}, u32[]{:S(2)}) collective-permute-start(f32[64,1024]{1,0:T(8,128)S(1)} %get-tuple-element.197), channel_id=1, source_target_pairs={{0,2},{1,3},{4,0},{5,1},{8,4},{9,5},{12,8},{13,9},{14,12},{15,13},... | collective-permute-start | bytes 786440 | tf_op jit(solution)/shard_map/ppermute | solution.py:753
  159.7 6.4 %collective-permute-start.29 = (f32[64,1024]{1,0:T(8,128)S(1)}, f32[64,1024]{1,0:T(8,128)S(1)}, u32[]{:S(2)}, u32[]{:S(2)}) collective-permute-start(f32[64,1024]{1,0:T(8,128)S(1)} %get-tuple-element.234), channel_id=1, source_target_pairs={{0,4},{1,5},{4,8},{5,9},{8,12},{9,13},{12,14},{13,15},{14,10},{15,... | collective-permute-start | bytes 786440 | tf_op jit(solution)/shard_map/ppermute | solution.py:753
  161.4 11.1 %collective-permute-start.34 = (f32[128,1024]{1,0:T(8,128)S(1)}, f32[128,1024]{1,0:T(8,128)S(1)}, u32[]{:S(2)}, u32[]{:S(2)}) collective-permute-start(f32[128,1024]{1,0:T(8,128)S(1)} %get-tuple-element.196), channel_id=1, source_target_pairs={{0,1},{1,0},{2,3},{3,2},{4,5},{5,4},{6,7},{7,6},{8,9},{9,8},{10,11... | collective-permute-start | bytes 1572872 | tf_op jit(solution)/shard_map/ppermute | solution.py:737
  166.1 6.4 %collective-permute-start.39 = (f32[64,1024]{1,0:T(8,128)S(1)}, f32[64,1024]{1,0:T(8,128)S(1)}, u32[]{:S(2)}, u32[]{:S(2)}) collective-permute-start(f32[64,1024]{1,0:T(8,128)S(1)} %get-tuple-element.205), channel_id=1, source_target_pairs={{0,2},{1,3},{4,0},{5,1},{8,4},{9,5},{12,8},{13,9},{14,12},{15,13},... | collective-permute-start | bytes 786440 | tf_op jit(solution)/shard_map/ppermute | solution.py:753
  166.8 6.4 %collective-permute-start.32 = (f32[64,1024]{1,0:T(8,128)S(1)}, f32[64,1024]{1,0:T(8,128)S(1)}, u32[]{:S(2)}, u32[]{:S(2)}) collective-permute-start(f32[64,1024]{1,0:T(8,128)S(1)} %get-tuple-element.232), channel_id=1, source_target_pairs={{0,4},{1,5},{4,8},{5,9},{8,12},{9,13},{12,14},{13,15},{14,10},{15,... | collective-permute-start | bytes 786440 | tf_op jit(solution)/shard_map/ppermute | solution.py:753
  169.6 10.2 %collective-permute-start.37 = (f32[128,1024]{1,0:T(8,128)S(1)}, f32[128,1024]{1,0:T(8,128)S(1)}, u32[]{:S(2)}, u32[]{:S(2)}) collective-permute-start(f32[128,1024]{1,0:T(8,128)S(1)} %get-tuple-element.204), channel_id=1, source_target_pairs={{0,1},{1,0},{2,3},{3,2},{4,5},{5,4},{6,7},{7,6},{8,9},{9,8},{10,11... | collective-permute-start | bytes 1572872 | tf_op jit(solution)/shard_map/ppermute | solution.py:737
  173.3 6.4 %collective-permute-start.42 = (f32[64,1024]{1,0:T(8,128)S(1)}, f32[64,1024]{1,0:T(8,128)S(1)}, u32[]{:S(2)}, u32[]{:S(2)}) collective-permute-start(f32[64,1024]{1,0:T(8,128)S(1)} %get-tuple-element.213), channel_id=1, source_target_pairs={{0,2},{1,3},{4,0},{5,1},{8,4},{9,5},{12,8},{13,9},{14,12},{15,13},... | collective-permute-start | bytes 786440 | tf_op jit(solution)/shard_map/ppermute | solution.py:753
  173.9 6.4 %collective-permute-start.35 = (f32[64,1024]{1,0:T(8,128)S(1)}, f32[64,1024]{1,0:T(8,128)S(1)}, u32[]{:S(2)}, u32[]{:S(2)}) collective-permute-start(f32[64,1024]{1,0:T(8,128)S(1)} %get-tuple-element.230), channel_id=1, source_target_pairs={{0,4},{1,5},{4,8},{5,9},{8,12},{9,13},{12,14},{13,15},{14,10},{15,... | collective-permute-start | bytes 786440 | tf_op jit(solution)/shard_map/ppermute | solution.py:753
  176.7 10.1 %collective-permute-start.40 = (f32[128,1024]{1,0:T(8,128)S(1)}, f32[128,1024]{1,0:T(8,128)S(1)}, u32[]{:S(2)}, u32[]{:S(2)}) collective-permute-start(f32[128,1024]{1,0:T(8,128)S(1)} %get-tuple-element.212), channel_id=1, source_target_pairs={{0,1},{1,0},{2,3},{3,2},{4,5},{5,4},{6,7},{7,6},{8,9},{9,8},{10,11... | collective-permute-start | bytes 1572872 | tf_op jit(solution)/shard_map/ppermute | solution.py:737
  180.4 6.4 %collective-permute-start.44 = (f32[64,1024]{1,0:T(8,128)S(1)}, f32[64,1024]{1,0:T(8,128)S(1)}, u32[]{:S(2)}, u32[]{:S(2)}) collective-permute-start(f32[64,1024]{1,0:T(8,128)S(1)} %get-tuple-element.221), channel_id=1, source_target_pairs={{0,2},{1,3},{4,0},{5,1},{8,4},{9,5},{12,8},{13,9},{14,12},{15,13},... | collective-permute-start | bytes 786440 | tf_op jit(solution)/shard_map/ppermute | solution.py:753
  180.9 6.4 %collective-permute-start.38 = (f32[64,1024]{1,0:T(8,128)S(1)}, f32[64,1024]{1,0:T(8,128)S(1)}, u32[]{:S(2)}, u32[]{:S(2)}) collective-permute-start(f32[64,1024]{1,0:T(8,128)S(1)} %get-tuple-element.228), channel_id=1, source_target_pairs={{0,4},{1,5},{4,8},{5,9},{8,12},{9,13},{12,14},{13,15},{14,10},{15,... | collective-permute-start | bytes 786440 | tf_op jit(solution)/shard_map/ppermute | solution.py:753
  183.8 5.7 %collective-permute-start.43 = (f32[128,1024]{1,0:T(8,128)S(1)}, f32[128,1024]{1,0:T(8,128)S(1)}, u32[]{:S(2)}, u32[]{:S(2)}) collective-permute-start(f32[128,1024]{1,0:T(8,128)S(1)} %get-tuple-element.220), channel_id=1, source_target_pairs={{0,1},{1,0},{2,3},{3,2},{4,5},{5,4},{6,7},{7,6},{8,9},{9,8},{10,11... | collective-permute-start | bytes 1572872 | tf_op jit(solution)/shard_map/ppermute | solution.py:737
  187.4 6.4 %collective-permute-start.41 = (f32[64,1024]{1,0:T(8,128)S(1)}, f32[64,1024]{1,0:T(8,128)S(1)}, u32[]{:S(2)}, u32[]{:S(2)}) collective-permute-start(f32[64,1024]{1,0:T(8,128)S(1)} %get-tuple-element.226), channel_id=1, source_target_pairs={{0,4},{1,5},{4,8},{5,9},{8,12},{9,13},{12,14},{13,15},{14,10},{15,... | collective-permute-start | bytes 786440 | tf_op jit(solution)/shard_map/ppermute | solution.py:753
  189.1 6.4 %collective-permute-start.45 = (f32[64,1024]{1,0:T(8,128)S(1)}, f32[64,1024]{1,0:T(8,128)S(1)}, u32[]{:S(2)}, u32[]{:S(2)}) collective-permute-start(f32[64,1024]{1,0:T(8,128)S(1)} %get-tuple-element.227), channel_id=1, source_target_pairs={{0,2},{1,3},{4,0},{5,1},{8,4},{9,5},{12,8},{13,9},{14,12},{15,13},... | collective-permute-start | bytes 786440 | tf_op jit(solution)/shard_map/ppermute | solution.py:753
  (15 other events, 94.6 us)
